TPU v7x, 32 devices: a whole 2x2x4 slice. The times are simulated.
32 devices in a mesh: row: 4 (over x, core), col: 8 (over z, y).
Axes of the slice: x: 2, y: 2, z: 4, core: 2. Of those that a mesh axis runs over, the one named last changes fastest.
Arguments:
- samples: float32 [384, 8192], P(None, ('row', 'col')), may hold values from -6 to 6
- omega_tiles: float32 [4, 8, 15, 256, 256], P('row', 'col'), may hold values from -6 to 6
- omega_diag: float32 [8192, 256], P(('row', 'col')), as said below
- tile_rows: int32 [4, 8, 15], P('row', 'col'), may hold values from 0 to 7, as said below
- tile_cols: int32 [4, 8, 15], P('row', 'col'), may hold values from 0 to 3
- tile_active: int32 [4, 8, 15], P('row', 'col'), may hold values from 0 to 1, as said below
Outputs:
- new_tiles: float32 [4, 8, 15, 256, 256], P('row', 'col')
- new_diag: float32 [8192, 256], P(('row', 'col'))
Inputs may be any that keep to these rules, and one draw needn't show every extreme that they name: `tile_rows`: on each device the 15 listed tiles (I, J) are distinct and none is diagonal; with o = (J - I) mod (32), o is odd and below 16, or even and above it, so no tile is listed together with its mirror. `tile_active`: on each device the live slots come first and number at least 5; on device (0, 0) all are live. `omega_diag`: every diagonal tile is symmetric and its diagonal entries lie between 0.5 and 4.
All inputs are finite; a program needn't handle non-finite values.
Results may differ from a plain program's by a relative error of at most 0.0003.
Values sent between devices are 32-bit elements; how exact they have to be, the bound alone decides.
No kernel may reach another device: no remote copies, remote signals or barrier semaphores. Data moves between devices by JAX's collectives and lax.ppermute only.
A program may use at most 128 MiB of HBM per device.

v0:
```python
import functools

import jax
import jax.numpy as jnp
from jax import lax
from jax.experimental import pallas as pl
from jax.experimental.pallas import tpu as pltpu
from jax.sharding import PartitionSpec as P

STEP_SIZE = 0.05
PENALTY = 4.0
F32 = jnp.float32
BF16 = jnp.bfloat16
VMEM_BYTES = 32 * 1024 * 1024
COST_BYTES = 20_000_000
NN = (((1,), (0,)), ((), ()))
NT = (((1,), (1,)), ((), ()))


def split(values):
    high = values.astype(BF16)
    return high, (values - high.astype(F32)).astype(BF16)


def dot3(left, right, dims):
    (lh, ll), (rh, rl) = left, right
    mul = functools.partial(lax.dot_general, dimension_numbers=dims, preferred_element_type=F32)
    return mul(lh, rh) + (mul(ll, rh) + mul(lh, rl))


def shrink(values, limit):
    return jnp.maximum(values - limit, 0.0) + jnp.minimum(values + limit, 0.0)


def ring_place(index, count):
    return jnp.where(index % 2 == 0, index // 2, count - 1 - index // 2)


def behind(index, count):
    return lax.rem(ring_place(lax.axis_index("col"), count) - ring_place(index, count) + count, count)


def ahead(index, count):
    return lax.rem(ring_place(index, count) - ring_place(lax.axis_index("col"), count) + count, count)


def row_slot(index, count, sign):
    me = lax.axis_index("row")
    pairs = count // 2
    apart = lax.rem(sign * (me // 2 - index // 2) + pairs, pairs)
    return 2 * apart + lax.rem(me + index, 2)


def fill(refs, high, low):
    for k, ref in enumerate(refs):
        high[k], low[k] = split(ref[...])


def fill_turned(refs, high, low):
    for k, ref in enumerate(refs):
        high[k], low[k] = split(ref[...].T)


def w_kernel(nr, nc, rows, cols, t_ref, *refs):
    x_refs, out_refs, (xh, xl, acc) = refs[:nr], refs[nr : nr + nc], refs[nr + nc :]
    fill(x_refs, xh, xl)
    acc[...] = jnp.zeros_like(acc)
    for slot in range(t_ref.shape[2]):
        j = row_slot(cols[0, 0, slot], nr, 1)
        i = ahead(rows[0, 0, slot], nc)
        acc[i] += dot3((xh[j], xl[j]), split(t_ref[0, 0, slot]), NT)
    for k in range(nc):
        out_refs[k][...] = acc[k]


def y_kernel(nr, nc, rows, cols, t_ref, d_ref, *refs):
    x_refs, out_refs, (xh, xl, acc) = refs[:nc], refs[nc : nc + nr], refs[nc + nr :]
    fill(x_refs, xh, xl)
    acc[...] = jnp.zeros_like(acc)
    acc[0] = dot3((xh[0], xl[0]), split(d_ref[...]), NN)
    for slot in range(t_ref.shape[2]):
        j = row_slot(cols[0, 0, slot], nr, -1)
        i = behind(rows[0, 0, slot], nc)
        acc[j] += dot3((xh[i], xl[i]), split(t_ref[0, 0, slot]), NN)
    for k in range(nr):
        out_refs[k][...] = acc[k]


def a_kernel(nr, nc, scale, rows, cols, t_ref, d_ref, *refs):
    x_refs, z_refs, refs = refs[:nc], refs[nc : nc + nr], refs[nc + nr :]
    out_ref, dout_ref, xh, xl, zh, zl = refs
    fill_turned(x_refs, xh, xl)
    fill(z_refs, zh, zl)
    gradient = dot3((xh[0], xl[0]), (zh[0], zl[0]), NN)
    gradient = (gradient + gradient.T) * scale
    tile = d_ref[...]
    row = lax.broadcasted_iota(jnp.int32, tile.shape, 0)
    on_diagonal = row == lax.broadcasted_iota(jnp.int32, tile.shape, 1)
    gradient = gradient - jnp.where(on_diagonal, 1.0 / jnp.where(on_diagonal, tile, 1.0), 0.0)
    value = tile - STEP_SIZE * gradient
    dout_ref[...] = jnp.where(on_diagonal, value, shrink(value, STEP_SIZE * PENALTY))
    for slot in range(t_ref.shape[2]):
        j = row_slot(cols[0, 0, slot], nr, 1)
        i = behind(rows[0, 0, slot], nc)
        gradient = dot3((xh[i], xl[i]), (zh[j], zl[j]), NN)
        out_ref[slot] = t_ref[0, 0, slot] - (STEP_SIZE * scale) * gradient


def b_kernel(nr, nc, scale, rows, cols, active, t_ref, v_ref, *refs):
    z_refs, x_refs, refs = refs[:nc], refs[nc : nc + nr], refs[nc + nr :]
    out_ref, zh, zl, xh, xl, made, sems = refs
    fill_turned(z_refs, zh, zl)
    fill(x_refs, xh, xl)
    copies = []
    for slot in range(t_ref.shape[2]):
        j = row_slot(cols[0, 0, slot], nr, 1)
        i = behind(rows[0, 0, slot], nc)
        gradient = dot3((zh[i], zl[i]), (xh[j], xl[j]), NN)
        value = shrink(v_ref[slot] - (STEP_SIZE * scale) * gradient, STEP_SIZE * PENALTY)
        made[slot] = jnp.where(active[0, 0, slot] > 0, value, t_ref[0, 0, slot])
        copies.append(pltpu.make_async_copy(made.at[slot], out_ref.at[0, 0, slot], sems.at[slot]))
        copies[-1].start()
    for copy in copies:
        copy.wait()


def per_device(samples, omega_tiles, omega_diag, tile_rows, tile_cols, tile_active):
    nr = lax.axis_size("row")
    nc = lax.axis_size("col")
    count, side = samples.shape
    slots = omega_tiles.shape[2]
    scale = 1.0 / (2.0 * count)
    even_core = lax.axis_index("row") % 2 == 0

    ring = list(range(0, nc, 2)) + list(range(1, nc, 2))[::-1]
    right = [(ring[k], ring[(k + 1) % nc]) for k in range(nc)]
    left = [(b, a) for a, b in right]
    chip = [(k, (k + 2) % nr) for k in range(nr)]
    core = [(k, k ^ 1) for k in range(nr)]
    both = [
        (r * nc + a, r * nc + b) for r in range(nr) for a, b in (right if r % 2 == 0 else left)
    ]
    far = nc // 2
    go = lax.ppermute

    def ring_gather(own):
        found = [own] + [None] * (nc - 1)
        for d in range(1, far):
            found[d] = go(found[d - 1], "col", right)
            found[nc - d] = go(found[(nc - d + 1) % nc], "col", left)
        found[far] = go(jnp.where(even_core, found[far - 1], found[far + 1]), ("row", "col"), both)
        return found

    def ring_sum(parts):
        first = go(parts[far], ("row", "col"), both)
        one = jnp.where(even_core, parts[far - 1] + first, parts[far - 1])
        two = jnp.where(even_core, parts[far + 1], parts[far + 1] + first)
        for d in range(far - 1, 0, -1):
            one = go(one, "col", right)
            two = go(two, "col", left)
            if d > 1:
                one = parts[d - 1] + one
                two = parts[nc - d + 1] + two
        return parts[0], one, two

    def row_gather(own):
        found = [own]
        for _ in range(nr // 2 - 1):
            found.append(go(found[-1], "row", chip))
        return [a for b in found for a in (b, go(b, "row", core))]

    def row_sum(parts):
        sums = [parts[2 * k] + go(parts[2 * k + 1], "row", core) for k in range(nr // 2)]
        total = None
        for k in range(nr // 2 - 1, 0, -1):
            total = go(sums[k] if total is None else sums[k] + total, "row", chip)
        return (sums[0],) if total is None else (sums[0], total)

    scalars = pl.BlockSpec(memory_space=pltpu.SMEM)
    whole = pl.BlockSpec(memory_space=pltpu.VMEM)

    def call(body, n_scalars, n_in, out_specs, out_shape, scratch):
        return pl.pallas_call(
            body,
            in_specs=[scalars] * n_scalars + [whole] * n_in,
            out_specs=out_specs,
            out_shape=out_shape,
            scratch_shapes=scratch,
            compiler_params=pltpu.CompilerParams(vmem_limit_bytes=VMEM_BYTES),
            cost_estimate=pl.CostEstimate(
                flops=6 * slots * count * side * side, bytes_accessed=COST_BYTES, transcendentals=0
            ),
        )

    def panel(n):
        return [pltpu.VMEM((n, count, side), BF16)] * 2

    def panel_t(n):
        return [pltpu.VMEM((n, side, count), BF16)] * 2

    block = jax.ShapeDtypeStruct((count, side), F32)
    tiles = jax.ShapeDtypeStruct((slots, side, side), F32)

    x_col = ring_gather(samples)
    x_row = row_gather(samples)
    w = call(
        functools.partial(w_kernel, nr, nc),
        2,
        1 + nr,
        [whole] * nc,
        [block] * nc,
        panel(nr) + [pltpu.VMEM((nc, count, side), F32)],
    )(tile_rows, tile_cols, omega_tiles, *x_row)
    w_own = ring_sum(w)
    y = call(
        functools.partial(y_kernel, nr, nc),
        2,
        2 + nc,
        [whole] * nr,
        [block] * nr,
        panel(nc) + [pltpu.VMEM((nr, count, side), F32)],
    )(tile_rows, tile_cols, omega_tiles, omega_diag, *x_col)
    z = sum(row_sum(y)[::-1] + w_own)
    z_col = ring_gather(z)
    z_row = row_gather(z)
    partial, new_diag = call(
        functools.partial(a_kernel, nr, nc, scale),
        2,
        2 + nc + nr,
        [whole] * 2,
        [tiles, jax.ShapeDtypeStruct((side, side), F32)],
        panel_t(nc) + panel(nr),
    )(tile_rows, tile_cols, omega_tiles, omega_diag, *x_col, *z_row)
    new_tiles = call(
        functools.partial(b_kernel, nr, nc, scale),
        3,
        2 + nc + nr,
        pl.BlockSpec(memory_space=pl.ANY),
        jax.ShapeDtypeStruct(omega_tiles.shape, F32),
        panel_t(nc) + panel(nr) + [pltpu.VMEM((slots, side, side), F32), pltpu.SemaphoreType.DMA((slots,))],
    )(tile_rows, tile_cols, tile_active, omega_tiles, partial, *z_col, *x_row)
    return new_tiles, new_diag


def solution(mesh):
    in_specs = (
        P(None, ("row", "col")),
        P("row", "col", None, None, None),
        P(("row", "col"), None),
        P("row", "col", None),
        P("row", "col", None),
        P("row", "col", None),
    )
    out_specs = (P("row", "col", None, None, None), P(("row", "col"), None))
    return jax.shard_map(
        per_device, mesh=mesh, in_specs=in_specs, out_specs=out_specs, check_vma=False
    )
```

profile of v0, /device:TPU:0, one launch (start us, length us, event | category | flops | bytes accessed | tf_op | source)
XLA Modules:
  0.0 127.3 jit_solution(8936458258980464017)
XLA Ops:
  0.6 3.0 %collective-permute-start.3 = (f32[384,256]{1,0:T(8,128)}, f32[384,256]{1,0:T(8,128)S(1)}, u32[]{:S(2)}, u32[]{:S(2)}) collective-permute-start(f32[384,256]{1,0:T(8,128)} %refs_8_.1), channel_id=1, source_target_pairs={{2,0},{4,2},{6,4},{7,6},{5,7},{3,5},{1,3},{0,1},{10,8},{12,10},{14... | collective-permute-start | bytes 1179656 | tf_op jit(solution)/shard_map/ppermute | solution.py:150
  3.8 1.9 %collective-permute-start.11 = (f32[384,256]{1,0:T(8,128)}, f32[384,256]{1,0:T(8,128)S(1)}, u32[]{:S(2)}, u32[]{:S(2)}) collective-permute-start(f32[384,256]{1,0:T(8,128)} %refs_8_.1), channel_id=1, source_target_pairs={{0,16},{8,24},{16,0},{24,8},{1,17},{9,25},{17,1},{25,9},{2,18},{10... | collective-permute-start | bytes 1179656 | tf_op jit(solution)/shard_map/ppermute | solution.py:169
  5.6 7.4 %collective-permute-done.3.refs_7_ = f32[384,256]{1,0:T(8,128)S(1)} collective-permute-done((f32[384,256]{1,0:T(8,128)}, f32[384,256]{1,0:T(8,128)S(1)}, u32[]{:S(2)}, u32[]{:S(2)}) %collective-permute-start.3) | collective-permute-done | bytes 393248 | tf_op jit(solution)/shard_map/ppermute | solution.py:150
  13.0 1.7 %collective-permute-start.4 = (f32[384,256]{1,0:T(8,128)S(1)}, f32[384,256]{1,0:T(8,128)S(1)}, u32[]{:S(2)}, u32[]{:S(2)}) collective-permute-start(f32[384,256]{1,0:T(8,128)S(1)} %collective-permute-done.3.refs_7_), channel_id=1, source_target_pairs={{2,0},{4,2},{6,4},{7,6},{5,7},{3,5},{1,3},{0,1},{10,8},{12,10},{14... | collective-permute-start | bytes 1179656 | tf_op jit(solution)/shard_map/ppermute | solution.py:150
  15.6 7.8 %collective-permute-done.4.refs_6_ = f32[384,256]{1,0:T(8,128)S(1)} collective-permute-done((f32[384,256]{1,0:T(8,128)S(1)}, f32[384,256]{1,0:T(8,128)S(1)}, u32[]{:S(2)}, u32[]{:S(2)}) %collective-permute-start.4) | collective-permute-done | bytes 393248 | tf_op jit(solution)/shard_map/ppermute | solution.py:150
  23.3 1.4 %collective-permute-start.5 = (f32[384,256]{1,0:T(8,128)S(1)}, f32[384,256]{1,0:T(8,128)S(1)}, u32[]{:S(2)}, u32[]{:S(2)}) collective-permute-start(f32[384,256]{1,0:T(8,128)S(1)} %collective-permute-done.4.refs_6_), channel_id=1, source_target_pairs={{2,0},{4,2},{6,4},{7,6},{5,7},{3,5},{1,3},{0,1},{10,8},{12,10},{14... | collective-permute-start | bytes 1179656 | tf_op jit(solution)/shard_map/ppermute | solution.py:150
  25.4 2.2 %copy-done = f32[1,1,15,256,256]{4,3,2,1,0:T(8,128)S(1)} copy-done((f32[1,1,15,256,256]{4,3,2,1,0:T(8,128)S(1)}, f32[1,1,15,256,256]{4,3,2,1,0:T(8,128)}, u32[]{:S(2)}) %copy-start) | copy-done | bytes 3932184
  30.0 4.4 %shard_map.78 = (f32[384,256]{1,0:T(8,128)S(1)}, f32[384,256]{1,0:T(8,128)S(1)}, f32[384,256]{1,0:T(8,128)S(1)}, f32[384,256]{1,0:T(8,128)S(1)}, f32[384,256]{1,...) custom-call(s32[1,1,15]{2,1,0:T(1,128)S(1)} %copy-done.19, ...), custom_call_target="tpu_custom_call" | custom-call | flops 2264924160 | bytes 20000000 | tf_op jit(solution)/shard_map/pallas_call | solution.py:206
  38.1 1.4 %collective-permute-start.13 = (f32[384,256]{1,0:T(8,128)}, f32[384,256]{1,0:T(8,128)}, u32[]{:S(2)}, u32[]{:S(2)}) collective-permute-start(f32[384,256]{1,0:T(8,128)} %get-tuple-element.24), channel_id=1, source_target_pairs={{0,2},{2,4},{4,6},{6,7},{7,5},{5,3},{3,1},{1,0},{10,8},{12,10},{14... | collective-permute-start | bytes 1179656 | tf_op jit(solution)/shard_map/ppermute | solution.py:155
  39.6 1.6 %collective-permute-start.6 = (f32[384,256]{1,0:T(8,128)S(1)}, f32[384,256]{1,0:T(8,128)S(1)}, u32[]{:S(2)}, u32[]{:S(2)}) collective-permute-start(f32[384,256]{1,0:T(8,128)S(1)} %broadcast_select_fusion.1), channel_id=1, source_target_pairs={{0,2},{2,4},{4,6},{6,7},{7,5},{5,3},{3,1},{1,0},{10,8},{12,10},{14... | collective-permute-start | bytes 1179656 | tf_op jit(solution)/shard_map/ppermute | solution.py:151
  41.2 5.0 %collective-permute-done.13 = f32[384,256]{1,0:T(8,128)} collective-permute-done((f32[384,256]{1,0:T(8,128)}, f32[384,256]{1,0:T(8,128)}, u32[]{:S(2)}, u32[]{:S(2)}) %collective-permute-start.13) | collective-permute-done | bytes 393248 | tf_op jit(solution)/shard_map/ppermute | solution.py:155
  46.2 1.3 %add_select_fusion.1 = (f32[384,256]{1,0:T(8,128)S(1)}, f32[384,256]{1,0:T(8,128)S(1)}) fusion(f32[384,256]{1,0:T(8,128)} %copy-done.8, f32[384,256]{1,0:T(8,128)} %collective-permute-done.13, pred[]{:T(512)S(6)} %eq.5, f32[384,256]{1,0:T(8,128)} %copy-done.9), kind=kLoop, calls=%fused_computation.1 | loop fusion | flops 393216 | bytes 1966081 | tf_op jit(solution)/shard_map/jit(_where)/select_n | solution.py:156
  47.5 1.5 %collective-permute-start.14 = (f32[384,256]{1,0:T(8,128)S(1)}, f32[384,256]{1,0:T(8,128)S(1)}, u32[]{:S(2)}, u32[]{:S(2)}) collective-permute-start(f32[384,256]{1,0:T(8,128)S(1)} %get-tuple-element.30), channel_id=1, source_target_pairs={{0,2},{2,4},{4,6},{6,7},{7,5},{5,3},{3,1},{1,0},{8,10},{10,12},{12... | collective-permute-start | bytes 1179656 | tf_op jit(solution)/shard_map/ppermute | solution.py:159
  49.6 3.9 %collective-permute-done.6.refs_4_ = f32[384,256]{1,0:T(8,128)S(1)} collective-permute-done((f32[384,256]{1,0:T(8,128)S(1)}, f32[384,256]{1,0:T(8,128)S(1)}, u32[]{:S(2)}, u32[]{:S(2)}) %collective-permute-start.6) | collective-permute-done | bytes 393248 | tf_op jit(solution)/shard_map/ppermute | solution.py:151
  53.4 2.1 %copy-done.1 = f32[1,1,15,256,256]{4,3,2,1,0:T(8,128)S(1)} copy-done((f32[1,1,15,256,256]{4,3,2,1,0:T(8,128)S(1)}, f32[1,1,15,256,256]{4,3,2,1,0:T(8,128)}, u32[]{:S(2)}) %copy-start.1) | copy-done | bytes 3932184
  56.5 4.4 %shard_map.77 = (f32[384,256]{1,0:T(8,128)S(1)}, f32[384,256]{1,0:T(8,128)S(1)}, f32[384,256]{1,0:T(8,128)S(1)}, f32[384,256]{1,0:T(8,128)S(1)}) custom-call(s32[1,1,15]{2,1,0:T(1,128)S(1)} %copy-done.20, s32[1,1,15]{2,1,0:T(1,128)S(1)} %copy-done.22, f32[1,1,15,256,256]{4,3,2,1,0:T(8,128)S(1)} %copy-done.1, f32[256,256]{1,0:T(8,128)S(1)} %copy-done.18, ...), custom_call_target="tpu_custom_call" | custom-call | flops 2264924160 | bytes 20000000 | tf_op jit(solution)/shard_map/pallas_call | solution.py:215
  61.1 1.8 %collective-permute-start.15 = (f32[384,256]{1,0:T(8,128)S(1)}, f32[384,256]{1,0:T(8,128)S(1)}, u32[]{:S(2)}, u32[]{:S(2)}) collective-permute-start(f32[384,256]{1,0:T(8,128)S(1)} %add.46), channel_id=1, source_target_pairs={{0,2},{2,4},{4,6},{6,7},{7,5},{5,3},{3,1},{1,0},{8,10},{10,12},{12... | collective-permute-start | bytes 1179656 | tf_op jit(solution)/shard_map/ppermute | solution.py:159
  63.3 1.7 %collective-permute-start.8 = (f32[384,256]{1,0:T(8,128)S(1)}, f32[384,256]{1,0:T(8,128)S(1)}, u32[]{:S(2)}, u32[]{:S(2)}) collective-permute-start(f32[384,256]{1,0:T(8,128)S(1)} %add.41), channel_id=1, source_target_pairs={{0,16},{8,24},{16,0},{24,8},{1,17},{9,25},{17,1},{25,9},{2,18},{10... | collective-permute-start | bytes 1179656 | tf_op jit(solution)/shard_map/ppermute | solution.py:176
  65.0 7.6 %collective-permute-done.15 = f32[384,256]{1,0:T(8,128)S(1)} collective-permute-done((f32[384,256]{1,0:T(8,128)S(1)}, f32[384,256]{1,0:T(8,128)S(1)}, u32[]{:S(2)}, u32[]{:S(2)}) %collective-permute-start.15) | collective-permute-done | bytes 393248 | tf_op jit(solution)/shard_map/ppermute | solution.py:159
  72.7 1.8 %collective-permute-start.16 = (f32[384,256]{1,0:T(8,128)S(1)}, f32[384,256]{1,0:T(8,128)S(1)}, u32[]{:S(2)}, u32[]{:S(2)}) collective-permute-start(f32[384,256]{1,0:T(8,128)S(1)} %add.47), channel_id=1, source_target_pairs={{0,2},{2,4},{4,6},{6,7},{7,5},{5,3},{3,1},{1,0},{8,10},{10,12},{12... | collective-permute-start | bytes 1179656 | tf_op jit(solution)/shard_map/ppermute | solution.py:159
  74.9 8.5 %collective-permute-done.16 = f32[384,256]{1,0:T(8,128)S(1)} collective-permute-done((f32[384,256]{1,0:T(8,128)S(1)}, f32[384,256]{1,0:T(8,128)S(1)}, u32[]{:S(2)}, u32[]{:S(2)}) %collective-permute-start.16) | collective-permute-done | bytes 393248 | tf_op jit(solution)/shard_map/ppermute | solution.py:159
  83.4 1.6 %collective-permute-done.19 = f32[384,256]{1,0:T(8,128)S(1)} collective-permute-done((f32[384,256]{1,0:T(8,128)S(1)}, f32[384,256]{1,0:T(8,128)S(1)}, u32[]{:S(2)}, u32[]{:S(2)}) %collective-permute-start.19) | collective-permute-done | bytes 393248 | tf_op jit(solution)/shard_map/ppermute | solution.py:160
  85.6 1.7 %collective-permute-start.23 = (f32[384,256]{1,0:T(8,128)S(1)}, f32[384,256]{1,0:T(8,128)S(1)}, u32[]{:S(2)}, u32[]{:S(2)}) collective-permute-start(f32[384,256]{1,0:T(8,128)S(1)} %add_add_fusion.refs_8_.refs_0_), channel_id=1, source_target_pairs={{0,2},{2,4},{4,6},{6,7},{7,5},{5,3},{3,1},{1,0},{8,10},{10,12},{12... | collective-permute-start | bytes 1179656 | tf_op jit(solution)/shard_map/ppermute | solution.py:149
  87.3 7.5 %collective-permute-done.26.refs_7_ = f32[384,256]{1,0:T(8,128)S(1)} collective-permute-done((f32[384,256]{1,0:T(8,128)S(1)}, f32[384,256]{1,0:T(8,128)S(1)}, u32[]{:S(2)}, u32[]{:S(2)}) %collective-permute-start.26) | collective-permute-done | bytes 393248 | tf_op jit(solution)/shard_map/ppermute | solution.py:150
  95.2 1.7 %collective-permute-start.24 = (f32[384,256]{1,0:T(8,128)S(1)}, f32[384,256]{1,0:T(8,128)S(1)}, u32[]{:S(2)}, u32[]{:S(2)}) collective-permute-start(f32[384,256]{1,0:T(8,128)S(1)} %collective-permute-done.23.refs_1_), channel_id=1, source_target_pairs={{0,2},{2,4},{4,6},{6,7},{7,5},{5,3},{3,1},{1,0},{8,10},{10,12},{12... | collective-permute-start | bytes 1179656 | tf_op jit(solution)/shard_map/ppermute | solution.py:149
  96.8 1.4 %collective-permute-start.21 = (f32[384,256]{1,0:T(8,128)S(1)}, f32[384,256]{1,0:T(8,128)S(1)}, u32[]{:S(2)}, u32[]{:S(2)}) collective-permute-start(f32[384,256]{1,0:T(8,128)S(1)} %add_add_fusion.refs_8_.refs_0_), channel_id=1, source_target_pairs={{0,16},{8,24},{16,0},{24,8},{1,17},{9,25},{17,1},{25,9},{2,18},{10... | collective-permute-start | bytes 1179656 | tf_op jit(solution)/shard_map/ppermute | solution.py:169
  98.3 5.8 %collective-permute-done.27.refs_6_ = f32[384,256]{1,0:T(8,128)S(1)} collective-permute-done((f32[384,256]{1,0:T(8,128)S(1)}, f32[384,256]{1,0:T(8,128)S(1)}, u32[]{:S(2)}, u32[]{:S(2)}) %collective-permute-start.27) | collective-permute-done | bytes 393248 | tf_op jit(solution)/shard_map/ppermute | solution.py:150
  104.4 1.7 %collective-permute-start.25 = (f32[384,256]{1,0:T(8,128)S(1)}, f32[384,256]{1,0:T(8,128)S(1)}, u32[]{:S(2)}, u32[]{:S(2)}) collective-permute-start(f32[384,256]{1,0:T(8,128)S(1)} %collective-permute-done.24.refs_2_), channel_id=1, source_target_pairs={{0,2},{2,4},{4,6},{6,7},{7,5},{5,3},{3,1},{1,0},{8,10},{10,12},{12... | collective-permute-start | bytes 1179656 | tf_op jit(solution)/shard_map/ppermute | solution.py:149
  106.6 6.2 %collective-permute-done.28.refs_5_ = f32[384,256]{1,0:T(8,128)S(1)} collective-permute-done((f32[384,256]{1,0:T(8,128)S(1)}, f32[384,256]{1,0:T(8,128)S(1)}, u32[]{:S(2)}, u32[]{:S(2)}) %collective-permute-start.28) | collective-permute-done | bytes 393248 | tf_op jit(solution)/shard_map/ppermute | solution.py:150
  112.9 1.6 %collective-permute-start.29 = (f32[384,256]{1,0:T(8,128)S(1)}, f32[384,256]{1,0:T(8,128)S(1)}, u32[]{:S(2)}, u32[]{:S(2)}) collective-permute-start(f32[384,256]{1,0:T(8,128)S(1)} %broadcast_select_fusion), channel_id=1, source_target_pairs={{0,2},{2,4},{4,6},{6,7},{7,5},{5,3},{3,1},{1,0},{10,8},{12,10},{14... | collective-permute-start | bytes 1179656 | tf_op jit(solution)/shard_map/ppermute | solution.py:151
  114.6 5.4 %shard_map.79 = (f32[15,256,256]{2,1,0:T(8,128)S(1)}, f32[256,256]{1,0:T(8,128)}) custom-call(s32[1,1,15]{2,1,0:T(1,128)S(1)} %copy-done.20, s32[1,1,15]{2,1,0:T(1,128)S(1)} %copy-done.22, f32[1,1,15,256,256]{4,3,2,1,0:T(8,128)S(1)} %copy-done.1, f32[256,256]{1,0:T(8,128)S(1)} %copy-done.18, f32[384,256]{1,0:T(8,128)S(1)} %copy-done.3, ...), custom_call_target="tpu_custom_call" | custom-call | flops 2264924160 | bytes 20000000 | tf_op jit(solution)/shard_map/pallas_call | solution.py:226
  121.0 6.2 %shard_map.80 = f32[1,1,15,256,256]{4,3,2,1,0:T(8,128)} custom-call(s32[1,1,15]{2,1,0:T(1,128)S(1)} %copy-done.20, s32[1,1,15]{2,1,0:T(1,128)S(1)} %copy-done.22, s32[1,1,15]{2,1,0:T(1,128)S(1)} %copy-done.23, f32[1,1,15,256,256]{4,3,2,1,0:T(8,128)S(1)} %copy-done.1, f32[15,256,256]{2,1,0:T(8,128)S(1)} %get-tuple-element.28.v_ref, ...), custom_call_target="tpu_custom_call" | custom-call | flops 2264924160 | bytes 20000000 | tf_op jit(solution)/shard_map/pallas_call | solution.py:234
  (89 shorter events, 13.1 us)
Async XLA Ops:
  0.6 12.4 %collective-permute-start.3 = (f32[384,256]{1,0:T(8,128)}, f32[384,256]{1,0:T(8,128)S(1)}, u32[]{:S(2)}, u32[]{:S(2)}) collective-permute-start(f32[384,256]{1,0:T(8,128)} %refs_8_.1), channel_id=1, source_target_pairs={{2,0},{4,2},{6,4},{7,6},{5,7},{3,5},{1,3},{0,1},{10,8},{12,10},{14... | collective-permute-start | bytes 1179656 | tf_op jit(solution)/shard_map/ppermute | solution.py:150
  3.6 11.1 %collective-permute-start = (f32[384,256]{1,0:T(8,128)}, f32[384,256]{1,0:T(8,128)S(1)}, u32[]{:S(2)}, u32[]{:S(2)}) collective-permute-start(f32[384,256]{1,0:T(8,128)} %refs_8_.1), channel_id=1, source_target_pairs={{0,2},{2,4},{4,6},{6,7},{7,5},{5,3},{3,1},{1,0},{8,10},{10,12},{12... | collective-permute-start | bytes 1179656 | tf_op jit(solution)/shard_map/ppermute | solution.py:149
  3.8 11.3 %collective-permute-start.11 = (f32[384,256]{1,0:T(8,128)}, f32[384,256]{1,0:T(8,128)S(1)}, u32[]{:S(2)}, u32[]{:S(2)}) collective-permute-start(f32[384,256]{1,0:T(8,128)} %refs_8_.1), channel_id=1, source_target_pairs={{0,16},{8,24},{16,0},{24,8},{1,17},{9,25},{17,1},{25,9},{2,18},{10... | collective-permute-start | bytes 1179656 | tf_op jit(solution)/shard_map/ppermute | solution.py:169
  13.0 10.3 %collective-permute-start.4 = (f32[384,256]{1,0:T(8,128)S(1)}, f32[384,256]{1,0:T(8,128)S(1)}, u32[]{:S(2)}, u32[]{:S(2)}) collective-permute-start(f32[384,256]{1,0:T(8,128)S(1)} %collective-permute-done.3.refs_7_), channel_id=1, source_target_pairs={{2,0},{4,2},{6,4},{7,6},{5,7},{3,5},{1,3},{0,1},{10,8},{12,10},{14... | collective-permute-start | bytes 1179656 | tf_op jit(solution)/shard_map/ppermute | solution.py:150
  14.7 10.0 %collective-permute-start.1 = (f32[384,256]{1,0:T(8,128)S(1)}, f32[384,256]{1,0:T(8,128)S(1)}, u32[]{:S(2)}, u32[]{:S(2)}) collective-permute-start(f32[384,256]{1,0:T(8,128)S(1)} %collective-permute-done.refs_1_), channel_id=1, source_target_pairs={{0,2},{2,4},{4,6},{6,7},{7,5},{5,3},{3,1},{1,0},{8,10},{10,12},{12... | collective-permute-start | bytes 1179656 | tf_op jit(solution)/shard_map/ppermute | solution.py:149
  15.1 10.3 %collective-permute-start.10 = (f32[384,256]{1,0:T(8,128)}, f32[384,256]{1,0:T(8,128)S(1)}, u32[]{:S(2)}, u32[]{:S(2)}) collective-permute-start(f32[384,256]{1,0:T(8,128)} %refs_8_.1), channel_id=1, source_target_pairs={{0,8},{8,0},{16,24},{24,16},{1,9},{9,1},{17,25},{25,17},{2,10},{10... | collective-permute-start | bytes 1179656 | tf_op jit(solution)/shard_map/ppermute | solution.py:170
  15.1 10.3 %collective-permute-start.12 = (f32[384,256]{1,0:T(8,128)S(1)}, f32[384,256]{1,0:T(8,128)S(1)}, u32[]{:S(2)}, u32[]{:S(2)}) collective-permute-start(f32[384,256]{1,0:T(8,128)S(1)} %collective-permute-done.11.refs_2_.refs_10_), channel_id=1, source_target_pairs={{0,8},{8,0},{16,24},{24,16},{1,9},{9,1},{17,25},{25,17},{2,10},{10... | collective-permute-start | bytes 1179656 | tf_op jit(solution)/shard_map/ppermute | solution.py:170
  23.3 16.2 %collective-permute-start.5 = (f32[384,256]{1,0:T(8,128)S(1)}, f32[384,256]{1,0:T(8,128)S(1)}, u32[]{:S(2)}, u32[]{:S(2)}) collective-permute-start(f32[384,256]{1,0:T(8,128)S(1)} %collective-permute-done.4.refs_6_), channel_id=1, source_target_pairs={{2,0},{4,2},{6,4},{7,6},{5,7},{3,5},{1,3},{0,1},{10,8},{12,10},{14... | collective-permute-start | bytes 1179656 | tf_op jit(solution)/shard_map/ppermute | solution.py:150
  24.7 14.8 %collective-permute-start.2 = (f32[384,256]{1,0:T(8,128)S(1)}, f32[384,256]{1,0:T(8,128)S(1)}, u32[]{:S(2)}, u32[]{:S(2)}) collective-permute-start(f32[384,256]{1,0:T(8,128)S(1)} %collective-permute-done.1.refs_2_), channel_id=1, source_target_pairs={{0,2},{2,4},{4,6},{6,7},{7,5},{5,3},{3,1},{1,0},{8,10},{10,12},{12... | collective-permute-start | bytes 1179656 | tf_op jit(solution)/shard_map/ppermute | solution.py:149
  29.9 23.5 %copy-start.22 = (s32[1,1,15]{2,1,0:T(1,128)S(1)}, s32[1,1,15]{2,1,0:T(1,128)}, u32[]{:S(2)}) copy-start(s32[1,1,15]{2,1,0:T(1,128)} %cols.7) | copy-start | bytes 184
  38.1 8.1 %collective-permute-start.13 = (f32[384,256]{1,0:T(8,128)}, f32[384,256]{1,0:T(8,128)}, u32[]{:S(2)}, u32[]{:S(2)}) collective-permute-start(f32[384,256]{1,0:T(8,128)} %get-tuple-element.24), channel_id=1, source_target_pairs={{0,2},{2,4},{4,6},{6,7},{7,5},{5,3},{3,1},{1,0},{10,8},{12,10},{14... | collective-permute-start | bytes 1179656 | tf_op jit(solution)/shard_map/ppermute | solution.py:155
  39.6 13.8 %collective-permute-start.6 = (f32[384,256]{1,0:T(8,128)S(1)}, f32[384,256]{1,0:T(8,128)S(1)}, u32[]{:S(2)}, u32[]{:S(2)}) collective-permute-start(f32[384,256]{1,0:T(8,128)S(1)} %broadcast_select_fusion.1), channel_id=1, source_target_pairs={{0,2},{2,4},{4,6},{6,7},{7,5},{5,3},{3,1},{1,0},{10,8},{12,10},{14... | collective-permute-start | bytes 1179656 | tf_op jit(solution)/shard_map/ppermute | solution.py:151
  47.5 13.5 %collective-permute-start.14 = (f32[384,256]{1,0:T(8,128)S(1)}, f32[384,256]{1,0:T(8,128)S(1)}, u32[]{:S(2)}, u32[]{:S(2)}) collective-permute-start(f32[384,256]{1,0:T(8,128)S(1)} %get-tuple-element.30), channel_id=1, source_target_pairs={{0,2},{2,4},{4,6},{6,7},{7,5},{5,3},{3,1},{1,0},{8,10},{10,12},{12... | collective-permute-start | bytes 1179656 | tf_op jit(solution)/shard_map/ppermute | solution.py:159
  49.0 13.9 %collective-permute-start.17 = (f32[384,256]{1,0:T(8,128)S(1)}, f32[384,256]{1,0:T(8,128)S(1)}, u32[]{:S(2)}, u32[]{:S(2)}) collective-permute-start(f32[384,256]{1,0:T(8,128)S(1)} %get-tuple-element.31), channel_id=1, source_target_pairs={{2,0},{4,2},{6,4},{7,6},{5,7},{3,5},{1,3},{0,1},{10,8},{12,10},{14... | collective-permute-start | bytes 1179656 | tf_op jit(solution)/shard_map/ppermute | solution.py:160
  60.9 24.2 %copy-start.11 = (f32[384,256]{1,0:T(8,128)S(1)}, f32[384,256]{1,0:T(8,128)}, u32[]{:S(2)}) copy-start(f32[384,256]{1,0:T(8,128)} %copy-done.10) | copy-start | bytes 1179652
  60.9 2.4 %collective-permute-start.7 = (f32[384,256]{1,0:T(8,128)S(1)}, f32[384,256]{1,0:T(8,128)S(1)}, u32[]{:S(2)}, u32[]{:S(2)}) collective-permute-start(f32[384,256]{1,0:T(8,128)S(1)} %get-tuple-element.17), channel_id=1, source_target_pairs={{0,8},{8,0},{16,24},{24,16},{1,9},{9,1},{17,25},{25,17},{2,10},{10... | collective-permute-start | bytes 1179656 | tf_op jit(solution)/shard_map/ppermute | solution.py:173
  61.1 11.5 %collective-permute-start.15 = (f32[384,256]{1,0:T(8,128)S(1)}, f32[384,256]{1,0:T(8,128)S(1)}, u32[]{:S(2)}, u32[]{:S(2)}) collective-permute-start(f32[384,256]{1,0:T(8,128)S(1)} %add.46), channel_id=1, source_target_pairs={{0,2},{2,4},{4,6},{6,7},{7,5},{5,3},{3,1},{1,0},{8,10},{10,12},{12... | collective-permute-start | bytes 1179656 | tf_op jit(solution)/shard_map/ppermute | solution.py:159
  63.0 11.5 %collective-permute-start.18 = (f32[384,256]{1,0:T(8,128)S(1)}, f32[384,256]{1,0:T(8,128)S(1)}, u32[]{:S(2)}, u32[]{:S(2)}) collective-permute-start(f32[384,256]{1,0:T(8,128)S(1)} %add.50), channel_id=1, source_target_pairs={{2,0},{4,2},{6,4},{7,6},{5,7},{3,5},{1,3},{0,1},{10,8},{12,10},{14... | collective-permute-start | bytes 1179656 | tf_op jit(solution)/shard_map/ppermute | solution.py:160
  63.2 11.6 %collective-permute-start.9 = (f32[384,256]{1,0:T(8,128)S(1)}, f32[384,256]{1,0:T(8,128)S(1)}, u32[]{:S(2)}, u32[]{:S(2)}) collective-permute-start(f32[384,256]{1,0:T(8,128)S(1)} %get-tuple-element.19), channel_id=1, source_target_pairs={{0,8},{8,0},{16,24},{24,16},{1,9},{9,1},{17,25},{25,17},{2,10},{10... | collective-permute-start | bytes 1179656 | tf_op jit(solution)/shard_map/ppermute | solution.py:173
  63.3 11.6 %collective-permute-start.8 = (f32[384,256]{1,0:T(8,128)S(1)}, f32[384,256]{1,0:T(8,128)S(1)}, u32[]{:S(2)}, u32[]{:S(2)}) collective-permute-start(f32[384,256]{1,0:T(8,128)S(1)} %add.41), channel_id=1, source_target_pairs={{0,16},{8,24},{16,0},{24,8},{1,17},{9,25},{17,1},{25,9},{2,18},{10... | collective-permute-start | bytes 1179656 | tf_op jit(solution)/shard_map/ppermute | solution.py:176
  72.7 10.8 %collective-permute-start.16 = (f32[384,256]{1,0:T(8,128)S(1)}, f32[384,256]{1,0:T(8,128)S(1)}, u32[]{:S(2)}, u32[]{:S(2)}) collective-permute-start(f32[384,256]{1,0:T(8,128)S(1)} %add.47), channel_id=1, source_target_pairs={{0,2},{2,4},{4,6},{6,7},{7,5},{5,3},{3,1},{1,0},{8,10},{10,12},{12... | collective-permute-start | bytes 1179656 | tf_op jit(solution)/shard_map/ppermute | solution.py:159
  74.6 10.5 %collective-permute-start.19 = (f32[384,256]{1,0:T(8,128)S(1)}, f32[384,256]{1,0:T(8,128)S(1)}, u32[]{:S(2)}, u32[]{:S(2)}) collective-permute-start(f32[384,256]{1,0:T(8,128)S(1)} %add.51), channel_id=1, source_target_pairs={{2,0},{4,2},{6,4},{7,6},{5,7},{3,5},{1,3},{0,1},{10,8},{12,10},{14... | collective-permute-start | bytes 1179656 | tf_op jit(solution)/shard_map/ppermute | solution.py:160
  85.2 9.6 %collective-permute-start.26 = (f32[384,256]{1,0:T(8,128)S(1)}, f32[384,256]{1,0:T(8,128)S(1)}, u32[]{:S(2)}, u32[]{:S(2)}) collective-permute-start(f32[384,256]{1,0:T(8,128)S(1)} %add_add_fusion.refs_8_.refs_0_), channel_id=1, source_target_pairs={{2,0},{4,2},{6,4},{7,6},{5,7},{3,5},{1,3},{0,1},{10,8},{12,10},{14... | collective-permute-start | bytes 1179656 | tf_op jit(solution)/shard_map/ppermute | solution.py:150
  85.6 9.6 %collective-permute-start.23 = (f32[384,256]{1,0:T(8,128)S(1)}, f32[384,256]{1,0:T(8,128)S(1)}, u32[]{:S(2)}, u32[]{:S(2)}) collective-permute-start(f32[384,256]{1,0:T(8,128)S(1)} %add_add_fusion.refs_8_.refs_0_), channel_id=1, source_target_pairs={{0,2},{2,4},{4,6},{6,7},{7,5},{5,3},{3,1},{1,0},{8,10},{10,12},{12... | collective-permute-start | bytes 1179656 | tf_op jit(solution)/shard_map/ppermute | solution.py:149
  94.8 9.3 %collective-permute-start.27 = (f32[384,256]{1,0:T(8,128)S(1)}, f32[384,256]{1,0:T(8,128)S(1)}, u32[]{:S(2)}, u32[]{:S(2)}) collective-permute-start(f32[384,256]{1,0:T(8,128)S(1)} %collective-permute-done.26.refs_7_), channel_id=1, source_target_pairs={{2,0},{4,2},{6,4},{7,6},{5,7},{3,5},{1,3},{0,1},{10,8},{12,10},{14... | collective-permute-start | bytes 1179656 | tf_op jit(solution)/shard_map/ppermute | solution.py:150
  95.2 9.3 %collective-permute-start.24 = (f32[384,256]{1,0:T(8,128)S(1)}, f32[384,256]{1,0:T(8,128)S(1)}, u32[]{:S(2)}, u32[]{:S(2)}) collective-permute-start(f32[384,256]{1,0:T(8,128)S(1)} %collective-permute-done.23.refs_1_), channel_id=1, source_target_pairs={{0,2},{2,4},{4,6},{6,7},{7,5},{5,3},{3,1},{1,0},{8,10},{10,12},{12... | collective-permute-start | bytes 1179656 | tf_op jit(solution)/shard_map/ppermute | solution.py:149
  96.8 9.3 %collective-permute-start.21 = (f32[384,256]{1,0:T(8,128)S(1)}, f32[384,256]{1,0:T(8,128)S(1)}, u32[]{:S(2)}, u32[]{:S(2)}) collective-permute-start(f32[384,256]{1,0:T(8,128)S(1)} %add_add_fusion.refs_8_.refs_0_), channel_id=1, source_target_pairs={{0,16},{8,24},{16,0},{24,8},{1,17},{9,25},{17,1},{25,9},{2,18},{10... | collective-permute-start | bytes 1179656 | tf_op jit(solution)/shard_map/ppermute | solution.py:169
  104.1 8.8 %collective-permute-start.28 = (f32[384,256]{1,0:T(8,128)S(1)}, f32[384,256]{1,0:T(8,128)S(1)}, u32[]{:S(2)}, u32[]{:S(2)}) collective-permute-start(f32[384,256]{1,0:T(8,128)S(1)} %collective-permute-done.27.refs_6_), channel_id=1, source_target_pairs={{2,0},{4,2},{6,4},{7,6},{5,7},{3,5},{1,3},{0,1},{10,8},{12,10},{14... | collective-permute-start | bytes 1179656 | tf_op jit(solution)/shard_map/ppermute | solution.py:150
  104.4 8.4 %collective-permute-start.25 = (f32[384,256]{1,0:T(8,128)S(1)}, f32[384,256]{1,0:T(8,128)S(1)}, u32[]{:S(2)}, u32[]{:S(2)}) collective-permute-start(f32[384,256]{1,0:T(8,128)S(1)} %collective-permute-done.24.refs_2_), channel_id=1, source_target_pairs={{0,2},{2,4},{4,6},{6,7},{7,5},{5,3},{3,1},{1,0},{8,10},{10,12},{12... | collective-permute-start | bytes 1179656 | tf_op jit(solution)/shard_map/ppermute | solution.py:149
  106.1 8.5 %collective-permute-start.20 = (f32[384,256]{1,0:T(8,128)S(1)}, f32[384,256]{1,0:T(8,128)S(1)}, u32[]{:S(2)}, u32[]{:S(2)}) collective-permute-start(f32[384,256]{1,0:T(8,128)S(1)} %add_add_fusion.refs_8_.refs_0_), channel_id=1, source_target_pairs={{0,8},{8,0},{16,24},{24,16},{1,9},{9,1},{17,25},{25,17},{2,10},{10... | collective-permute-start | bytes 1179656 | tf_op jit(solution)/shard_map/ppermute | solution.py:170
  106.1 8.5 %collective-permute-start.22 = (f32[384,256]{1,0:T(8,128)S(1)}, f32[384,256]{1,0:T(8,128)S(1)}, u32[]{:S(2)}, u32[]{:S(2)}) collective-permute-start(f32[384,256]{1,0:T(8,128)S(1)} %collective-permute-done.21.refs_10_), channel_id=1, source_target_pairs={{0,8},{8,0},{16,24},{24,16},{1,9},{9,1},{17,25},{25,17},{2,10},{10... | collective-permute-start | bytes 1179656 | tf_op jit(solution)/shard_map/ppermute | solution.py:170
  112.9 8.0 %collective-permute-start.29 = (f32[384,256]{1,0:T(8,128)S(1)}, f32[384,256]{1,0:T(8,128)S(1)}, u32[]{:S(2)}, u32[]{:S(2)}) collective-permute-start(f32[384,256]{1,0:T(8,128)S(1)} %broadcast_select_fusion), channel_id=1, source_target_pairs={{0,2},{2,4},{4,6},{6,7},{7,5},{5,3},{3,1},{1,0},{10,8},{12,10},{14... | collective-permute-start | bytes 1179656 | tf_op jit(solution)/shard_map/ppermute | solution.py:151
  (22 other events, 134.0 us)
where the time goes:
time: 128 us; the launch traced here: 127 us
  waiting for transfers between devices  62.2 us (49%)
  starting transfers between devices  30.5 us (24%)
  Pallas kernels  20.3 us (16%)
  local copies, waits for them, and re-layouts  11.4 us (9%)
  other arithmetic  1.85 us (1%)
    ppermute x6, waiting for transfers between devices, ring_gather(): found[nc - d] = go(found[(nc - d + 1) % nc], 'col', left)  34.6 us
    ppermute x3, waiting for transfers between devices, ring_sum(): one = go(one, 'col', right)  16.1 us
    unnamed x48, local copies, waits for them, and re-layouts  11.4 us
    ppermute x6, starting transfers between devices, ring_gather(): found[nc - d] = go(found[(nc - d + 1) % nc], 'col', left)  7.13 us
    ppermute x6, starting transfers between devices, ring_gather(): found[d] = go(found[d - 1], 'col', right)  6.19 us
    pallas_call x1, Pallas kernels, per_device(): call(functools.partial(b_kernel, nr, nc, scale), 3, 2 + nc + nr, pl.Block...  6.19 us
    pallas_call x1, Pallas kernels, per_device(): call(functools.partial(a_kernel, nr, nc, scale), 2, 2 + nc + nr, [whole]...  5.39 us
    ppermute x3, starting transfers between devices, ring_sum(): one = go(one, 'col', right)  5.17 us
  transfers between devices with their start and end apart: 30, of which 11 were waited for; matrix products, arithmetic and copies ran while one was open for 1% of the time, Pallas kernels for 11%

commit v1 on v0

v1 whole, which is shorter than its diff:
```python
import functools

import jax
import jax.numpy as jnp
from jax import lax
from jax.experimental import pallas as pl
from jax.experimental.pallas import tpu as pltpu
from jax.sharding import PartitionSpec as P

STEP_SIZE = 0.05
PENALTY = 4.0
F32 = jnp.float32
BF16 = jnp.bfloat16
COST_BYTES = 20_000_000
GROUP = 5
NN = (((1,), (0,)), ((), ()))
NT = (((1,), (1,)), ((), ()))


def split(values):
    high = values.astype(BF16)
    return high, (values - high.astype(F32)).astype(BF16)


def dot3(left, right, dims):
    (lh, ll), (rh, rl) = left, right
    mul = functools.partial(lax.dot_general, dimension_numbers=dims, preferred_element_type=F32)
    return mul(lh, rh) + (mul(ll, rh) + mul(lh, rl))


def shrink(values, limit):
    return jnp.maximum(values - limit, 0.0) + jnp.minimum(values + limit, 0.0)


def wrapped(index, count):
    return jnp.where(index < 0, index + count, index)


def ring_place(index, count):
    return jnp.where(index & 1 == 0, index >> 1, count - 1 - (index >> 1))


def behind(index, count):
    return wrapped(ring_place(lax.axis_index("col"), count) - ring_place(index, count), count)


def ahead(index, count):
    return wrapped(ring_place(index, count) - ring_place(lax.axis_index("col"), count), count)


def row_slot(index, count, sign):
    me = lax.axis_index("row")
    return 2 * wrapped(sign * ((me >> 1) - (index >> 1)), count // 2) + ((me + index) & 1)


def fill(refs, high, low):
    for k, ref in enumerate(refs):
        high[k], low[k] = split(ref[...])


def fill_turned(refs, high, low):
    for k, ref in enumerate(refs):
        high[k], low[k] = split(ref[...].T)


def fetch(sources, targets, sems):
    copies = [
        pltpu.make_async_copy(a.at[0, 0] if len(a.shape) == 3 else a, b, sems.at[k])
        for k, (a, b) in enumerate(zip(sources, targets))
    ]
    for copy in copies:
        copy.start()
    return copies


def w_kernel(nr, nc, rows_in, cols_in, t_in, *refs):
    x_refs, out_refs, refs = refs[:nr], refs[nr : nr + nc], refs[nr + nc :]
    t_ref, rows, cols, sems, t_sems, out_sems, xh, xl, acc = refs
    small = fetch((rows_in, cols_in), (rows, cols), sems)
    groups = []
    for k in range(t_ref.shape[0] // GROUP):
        at = pl.ds(k * GROUP, GROUP)
        groups.append(pltpu.make_async_copy(t_in.at[0, 0, at], t_ref.at[at], t_sems.at[k]))
        groups[-1].start()
    fill(x_refs, xh, xl)
    acc[...] = jnp.zeros_like(acc)
    for copy in small:
        copy.wait()
    for slot in range(t_ref.shape[0]):
        if slot % GROUP == 0:
            groups[slot // GROUP].wait()
        j = row_slot(cols[slot], nr, 1)
        i = ahead(rows[slot], nc)
        acc[i] += dot3((xh[j], xl[j]), split(t_ref[slot]), NT)
    copies = [pltpu.make_async_copy(acc.at[k], out_refs[k], out_sems.at[k]) for k in range(nc)]
    for copy in copies:
        copy.start()
    for copy in copies:
        copy.wait()


def y_kernel(nr, nc, rows_in, cols_in, d_in, t_ref, *refs):
    x_refs, out_refs, refs = refs[:nc], refs[nc : nc + nr], refs[nc + nr :]
    rows, cols, d_ref, sems, xh, xl, acc = refs
    small = fetch((rows_in, cols_in, d_in), (rows, cols, d_ref), sems)
    fill(x_refs, xh, xl)
    acc[...] = jnp.zeros_like(acc)
    for copy in small:
        copy.wait()
    acc[0] = dot3((xh[0], xl[0]), split(d_ref[...]), NN)
    for slot in range(t_ref.shape[0]):
        j = row_slot(cols[slot], nr, -1)
        i = behind(rows[slot], nc)
        acc[j] += dot3((xh[i], xl[i]), split(t_ref[slot]), NN)
    for k in range(nr):
        out_refs[k][...] = acc[k]


def prepare_kernel(nr, nc, *refs):
    x_refs, r_refs, (th, tl, rh, rl) = refs[:nc], refs[nc : nc + nr], refs[nc + nr :]
    fill_turned(x_refs, th, tl)
    fill(r_refs, rh, rl)


def first_kernel(nr, nc, scale, rows_in, cols_in, live_in, d_in, t_ref, th, tl, *refs):
    z_refs, refs = refs[:nr], refs[nr:]
    out_ref, dout_ref, rows, cols, live, d_ref, sems, zh, zl = refs
    small = fetch((rows_in, cols_in, live_in, d_in), (rows, cols, live, d_ref), sems)
    fill(z_refs, zh, zl)
    for copy in small:
        copy.wait()
    gradient = dot3((th[0], tl[0]), (zh[0], zl[0]), NN)
    gradient = (gradient + gradient.T) * scale
    tile = d_ref[...]
    row = lax.broadcasted_iota(jnp.int32, tile.shape, 0)
    on_diagonal = row == lax.broadcasted_iota(jnp.int32, tile.shape, 1)
    gradient = gradient - jnp.where(on_diagonal, 1.0 / jnp.where(on_diagonal, tile, 1.0), 0.0)
    value = tile - STEP_SIZE * gradient
    dout_ref[...] = jnp.where(on_diagonal, value, shrink(value, STEP_SIZE * PENALTY))
    for slot in range(t_ref.shape[0]):
        j = row_slot(cols[slot], nr, 1)
        i = behind(rows[slot], nc)
        gradient = dot3((th[i], tl[i]), (zh[j], zl[j]), NN)
        out_ref[slot] = t_ref[slot] - jnp.where(live[slot] > 0, STEP_SIZE * scale, 0.0) * gradient


def second_kernel(nr, nc, scale, places, rows_in, cols_in, live_in, v_ref, rh, rl, *refs):
    z_refs, refs = refs[: len(places)], refs[len(places) :]
    out_ref, made, rows, cols, live, sems, zh, zl, out_sems = refs
    small = fetch((rows_in, cols_in, live_in), (rows, cols, live), sems)
    fill_turned(z_refs, zh, zl)
    for copy in small:
        copy.wait()
    copies, mine = [], []
    for slot in range(v_ref.shape[0]):
        place = behind(rows[slot], nc)
        i = sum(jnp.where(place == p, k, 0) for k, p in enumerate(places))
        mine.append(functools.reduce(jnp.logical_or, [place == p for p in places]))
        copies.append(pltpu.make_async_copy(made.at[slot], out_ref.at[0, 0, slot], out_sems.at[slot]))
        j = row_slot(cols[slot], nr, 1)
        gradient = dot3((zh[i], zl[i]), (rh[j], rl[j]), NN)
        value = v_ref[slot]
        new = shrink(value - (STEP_SIZE * scale) * gradient, STEP_SIZE * PENALTY)
        made[slot] = jnp.where(jnp.logical_and(live[slot] > 0, mine[slot]), new, value)
    for slot in range(v_ref.shape[0]):
        pl.when(mine[slot])(copies[slot].start)
    for slot in range(v_ref.shape[0]):
        pl.when(mine[slot])(copies[slot].wait)


def late_kernel(nr, nc, scale, places, rows_in, cols_in, live_in, v_ref, rh, rl, *refs):
    z_refs, refs = refs[: len(places)], refs[len(places) :]
    _, out_ref, rows, cols, live, sems, zh, zl, made, out_sems = refs
    small = fetch((rows_in, cols_in, live_in), (rows, cols, live), sems)
    fill_turned(z_refs, zh, zl)
    for copy in small:
        copy.wait()
    mine, copies = [], []
    for slot in range(v_ref.shape[0]):
        place = behind(rows[slot], nc)
        i = sum(jnp.where(place == p, k, 0) for k, p in enumerate(places))
        mine.append(functools.reduce(jnp.logical_or, [place == p for p in places]))
        copies.append(pltpu.make_async_copy(made.at[slot], out_ref.at[0, 0, slot], out_sems.at[slot]))

        @pl.when(mine[slot])
        def _():
            j = row_slot(cols[slot], nr, 1)
            gradient = dot3((zh[i], zl[i]), (rh[j], rl[j]), NN)
            value = v_ref[slot]
            new = shrink(value - (STEP_SIZE * scale) * gradient, STEP_SIZE * PENALTY)
            made[slot] = jnp.where(live[slot] > 0, new, value)
            copies[slot].start()

    for slot in range(v_ref.shape[0]):
        pl.when(mine[slot])(copies[slot].wait)


def per_device(samples, omega_tiles, omega_diag, tile_rows, tile_cols, tile_active):
    nr = lax.axis_size("row")
    nc = lax.axis_size("col")
    count, side = samples.shape
    slots = omega_tiles.shape[2]
    scale = 1.0 / (2.0 * count)
    even_core = lax.axis_index("row") % 2 == 0

    ring = list(range(0, nc, 2)) + list(range(1, nc, 2))[::-1]
    right = [(ring[k], ring[(k + 1) % nc]) for k in range(nc)]
    left = [(b, a) for a, b in right]
    chip = [(k, (k + 2) % nr) for k in range(nr)]
    core = [(k, k ^ 1) for k in range(nr)]
    both = [
        (r * nc + a, r * nc + b) for r in range(nr) for a, b in (right if r % 2 == 0 else left)
    ]
    far = nc // 2
    go = lax.ppermute

    def ring_gather(own, beside):
        found = [own] + [None] * (nc - 1)
        for d in range(1, far + 1):
            one, two = found[d - 1], found[(nc - d + 1) % nc]
            if d in beside:
                one, two, _ = lax.optimization_barrier((one, two, beside[d](found)))
            if d < far:
                found[d] = go(one, "col", right)
                found[nc - d] = go(two, "col", left)
            else:
                found[far] = go(jnp.where(even_core, one, two), ("row", "col"), both)
        return found

    def ring_sum(parts):
        first = go(parts[far], ("row", "col"), both)
        one = jnp.where(even_core, parts[far - 1] + first, parts[far - 1])
        two = jnp.where(even_core, parts[far + 1], parts[far + 1] + first)
        for d in range(far - 1, 0, -1):
            one = go(one, "col", right)
            two = go(two, "col", left)
            if d > 1:
                one = parts[d - 1] + one
                two = parts[nc - d + 1] + two
        return parts[0], one, two

    def row_gather(own):
        found = [own]
        for _ in range(nr // 2 - 1):
            found.append(go(found[-1], "row", chip))
        return [a for b in found for a in (b, go(b, "row", core))]

    def row_sum(parts):
        sums = [parts[2 * k] + go(parts[2 * k + 1], "row", core) for k in range(nr // 2)]
        total = None
        for k in range(nr // 2 - 1, 0, -1):
            total = go(sums[k] if total is None else sums[k] + total, "row", chip)
        return (sums[0],) if total is None else (sums[0], total)

    whole = pl.BlockSpec(memory_space=pltpu.VMEM)
    in_place = pl.BlockSpec(memory_space=pltpu.HBM)

    def call(body, n_hbm, n_vmem, out_specs, out_shape, scratch, megabytes, aliases=None):
        return pl.pallas_call(
            body,
            in_specs=[in_place] * n_hbm + [whole] * n_vmem + [in_place] * len(aliases or {}),
            out_specs=out_specs,
            out_shape=out_shape,
            scratch_shapes=scratch,
            input_output_aliases=aliases or {},
            compiler_params=pltpu.CompilerParams(vmem_limit_bytes=megabytes * 1024 * 1024),
            cost_estimate=pl.CostEstimate(
                flops=6 * slots * count * side * side, bytes_accessed=COST_BYTES, transcendentals=0
            ),
        )

    def ids(n):
        return [pltpu.SMEM((slots,), jnp.int32)] * n

    def sems(n):
        return pltpu.SemaphoreType.DMA((n,))

    def panel(n):
        return [pltpu.VMEM((n, count, side), BF16)] * 2

    def panel_t(n):
        return [pltpu.VMEM((n, side, count), BF16)] * 2

    block = jax.ShapeDtypeStruct((count, side), F32)
    tile = jax.ShapeDtypeStruct((side, side), F32)
    tiles = jax.ShapeDtypeStruct((slots, side, side), F32)
    turned = jax.ShapeDtypeStruct((nc, side, count), BF16)
    straight = jax.ShapeDtypeStruct((nr, count, side), BF16)

    in_hbm = functools.partial(pltpu.with_memory_space_constraint, memory_space=pltpu.HBM)
    tile_rows, tile_cols, tile_active, omega_tiles, omega_diag = map(
        in_hbm, (tile_rows, tile_cols, tile_active, omega_tiles, omega_diag)
    )
    x_row = row_gather(samples)
    *w, held = call(
        functools.partial(w_kernel, nr, nc),
        3,
        nr,
        [in_place] * nc + [whole],
        [pltpu.HBM((count, side), F32)] * nc + [tiles],
        ids(2) + [sems(2), sems(slots // GROUP), sems(nc)] + panel(nr) + [pltpu.VMEM((nc, count, side), F32)],
        10 + nc,
    )(tile_rows, tile_cols, omega_tiles, *x_row)
    x_col = ring_gather(samples, {far - 1: lambda found: w[0]})
    w_own = ring_sum(w)
    y = call(
        functools.partial(y_kernel, nr, nc),
        3,
        1 + nc,
        [whole] * nr,
        [block] * nr,
        ids(2) + [pltpu.VMEM((side, side), F32), sems(3)] + panel(nc) + [pltpu.VMEM((nr, count, side), F32)],
        10 + nc,
    )(tile_rows, tile_cols, omega_diag, held, *x_col)
    z = sum(row_sum(y)[::-1] + w_own)
    th, tl, rh, rl = call(
        functools.partial(prepare_kernel, nr, nc),
        0,
        nc + nr,
        [whole] * 4,
        [turned] * 2 + [straight] * 2,
        [],
        8,
    )(*x_col, *x_row)
    z, th, tl, rh, rl = lax.optimization_barrier((z, th, tl, rh, rl))
    z_row = row_gather(z)
    made = []

    def first(found):
        made.extend(
            call(
                functools.partial(first_kernel, nr, nc, scale),
                4,
                3 + nr,
                [whole] * 2,
                [tiles, tile],
                ids(3) + [pltpu.VMEM((side, side), F32), sems(4)] + panel(nr),
                10 + nc,
            )(tile_rows, tile_cols, tile_active, omega_diag, held, th, tl, *z_row)
        )
        return made[0]

    def second(found):
        places = sum(steps[:-2], [])
        made.extend(
            call(
                functools.partial(second_kernel, nr, nc, scale, places),
                3,
                3 + len(places),
                [in_place, whole],
                [jax.ShapeDtypeStruct(omega_tiles.shape, F32), tiles],
                ids(3) + [sems(3)] + panel_t(len(places)) + [sems(slots)],
                10 + nc,
            )(tile_rows, tile_cols, tile_active, made[0], rh, rl, *[found[p] for p in places])
        )
        return made[-1]

    steps = [[0], *[[d, nc - d] for d in range(1, far)], [far]]
    z_col = ring_gather(z, {far - 1: first, far: second})
    _, new_diag, new_tiles, partial = made
    for places in steps[-2:]:
        new_tiles = call(
            functools.partial(late_kernel, nr, nc, scale, places),
            3,
            3 + len(places),
            in_place,
            jax.ShapeDtypeStruct(omega_tiles.shape, F32),
            ids(3)
            + [sems(3)]
            + panel_t(len(places))
            + [pltpu.VMEM((slots, side, side), F32), sems(slots)],
            10 + nc,
            {6 + len(places): 0},
        )(tile_rows, tile_cols, tile_active, partial, rh, rl, *[z_col[p] for p in places], new_tiles)
    return new_tiles, new_diag


def solution(mesh):
    in_specs = (
        P(None, ("row", "col")),
        P("row", "col", None, None, None),
        P(("row", "col"), None),
        P("row", "col", None),
        P("row", "col", None),
        P("row", "col", None),
    )
    out_specs = (P("row", "col", None, None, None), P(("row", "col"), None))
    return jax.shard_map(
        per_device, mesh=mesh, in_specs=in_specs, out_specs=out_specs, check_vma=False
    )
```

time: 128 us -> 116 us (0.906)
  waiting for transfers between devices: 62.2 us -> 48.1 us
  Pallas kernels: 20.3 us -> 30.6 us
  local copies, waits for them, and re-layouts: 11.4 us -> 2.93 us
  other arithmetic: 1.85 us -> 3.81 us
    ppermute x14, waiting for transfers between devices: 39.5 us -> 16.3 us  [the longest x6 10.6 us: ring_gather(): found[d] = go(one, 'col', right)]
    ppermute x3, waiting for transfers between devices: 16.1 us -> 1.4 us  [ring_sum(): one = go(one, 'col', right)]
    ppermute x2, waiting for transfers between devices: 0.01 us -> 12.8 us  [row_gather(): found.append(go(found[-1], 'row', chip))]
    pallas_call x4 -> x7, Pallas kernels: 20.3 us -> 30.6 us  [the longest x1 6.33 us: per_device(): call(functools.partial(w_kernel, nr, nc), 3, nr, [in_place] * nc + [whole...]
    unnamed x48 -> x14, local copies, waits for them, and re-layouts: 11.4 us -> 2.93 us
    ppermute x3, waiting for transfers between devices: 1.62 us -> 9.79 us  [ring_sum(): two = go(two, 'col', left)]
    ppermute x3, starting transfers between devices: 1.17 us -> 4.98 us  [ring_sum(): two = go(two, 'col', left)]
    ppermute x3, starting transfers between devices: 5.17 us -> 1.36 us  [ring_sum(): one = go(one, 'col', right)]
  transfers between devices with their start and end apart: 30 -> 30, of which waited for: 11 -> 17; matrix products, arithmetic and copies ran while one was open for 1% -> 3% of each run, Pallas kernels for 11% -> 24%
where the time goes in v1:
time: 116 us
  waiting for transfers between devices  48.1 us (41%)
  Pallas kernels  30.6 us (26%)
  starting transfers between devices  29.5 us (25%)
  other arithmetic  3.81 us (3%)
  local copies, waits for them, and re-layouts  2.93 us (3%)
    ppermute x2, waiting for transfers between devices, row_gather(): found.append(go(found[-1], 'row', chip))  12.8 us
    ppermute x6, waiting for transfers between devices, ring_gather(): found[d] = go(one, 'col', right)  10.6 us
    ppermute x3, waiting for transfers between devices, ring_sum(): two = go(two, 'col', left)  9.79 us
    ppermute x6, starting transfers between devices, ring_gather(): found[d] = go(one, 'col', right)  9.03 us
    ppermute x1, waiting for transfers between devices, ring_sum(): first = go(parts[far], ('row', 'col'), both)  7.51 us
    pallas_call x1, Pallas kernels, per_device(): call(functools.partial(w_kernel, nr, nc), 3, nr, [in_place] * nc + [whole...  6.33 us
    pallas_call x1, Pallas kernels, second(): call(functools.partial(second_kernel, nr, nc, scale, places), 3, 3 + len(...  6.15 us
    pallas_call x2, Pallas kernels, per_device(): call(functools.partial(late_kernel, nr, nc, scale, places), 3, 3 + len(pl...  5.95 us
  transfers between devices with their start and end apart: 30, of which 17 were waited for; matrix products, arithmetic and copies ran while one was open for 3% of the time, Pallas kernels for 24%

profile of v1, /device:TPU:0, one launch (start us, length us, event | category | flops | bytes accessed | tf_op | source)
XLA Modules:
  0.0 115.8 jit_solution(4802214048129899355)
XLA Ops:
  0.6 3.0 %collective-permute-start.1 = (f32[384,256]{1,0:T(8,128)}, f32[384,256]{1,0:T(8,128)S(1)}, u32[]{:S(2)}, u32[]{:S(2)}) collective-permute-start(f32[384,256]{1,0:T(8,128)} %refs_8_.1), channel_id=1, source_target_pairs={{0,16},{8,24},{16,0},{24,8},{1,17},{9,25},{17,1},{25,9},{2,18},{10... | collective-permute-start | bytes 1179656 | tf_op jit(solution)/shard_map/ppermute | solution.py:245
  3.6 1.6 %collective-permute-start.3 = (f32[384,256]{1,0:T(8,128)}, f32[384,256]{1,0:T(8,128)S(1)}, u32[]{:S(2)}, u32[]{:S(2)}) collective-permute-start(f32[384,256]{1,0:T(8,128)} %refs_8_.1), channel_id=1, source_target_pairs={{0,2},{2,4},{4,6},{6,7},{7,5},{5,3},{3,1},{1,0},{8,10},{10,12},{12... | collective-permute-start | bytes 1179656 | tf_op jit(solution)/shard_map/ppermute | solution.py:224
  5.7 7.3 %collective-permute-done.1.refs_2_.refs_10_ = f32[384,256]{1,0:T(8,128)S(1)} collective-permute-done((f32[384,256]{1,0:T(8,128)}, f32[384,256]{1,0:T(8,128)S(1)}, u32[]{:S(2)}, u32[]{:S(2)}) %collective-permute-start.1) | collective-permute-done | bytes 393248 | tf_op jit(solution)/shard_map/ppermute | solution.py:245
  13.0 1.5 %collective-permute-done.3.refs_1_ = f32[384,256]{1,0:T(8,128)S(1)} collective-permute-done((f32[384,256]{1,0:T(8,128)}, f32[384,256]{1,0:T(8,128)S(1)}, u32[]{:S(2)}, u32[]{:S(2)}) %collective-permute-start.3) | collective-permute-done | bytes 393248 | tf_op jit(solution)/shard_map/ppermute | solution.py:224
  14.4 1.6 %collective-permute-start.4 = (f32[384,256]{1,0:T(8,128)S(1)}, f32[384,256]{1,0:T(8,128)S(1)}, u32[]{:S(2)}, u32[]{:S(2)}) collective-permute-start(f32[384,256]{1,0:T(8,128)S(1)} %collective-permute-done.3.refs_1_), channel_id=1, source_target_pairs={{0,2},{2,4},{4,6},{6,7},{7,5},{5,3},{3,1},{1,0},{8,10},{10,12},{12... | collective-permute-start | bytes 1179656 | tf_op jit(solution)/shard_map/ppermute | solution.py:224
  17.5 6.3 %shard_map.77 = (f32[384,256]{1,0:T(8,128)}, f32[384,256]{1,0:T(8,128)}, f32[384,256]{1,0:T(8,128)}, f32[384,256]{1,0:T(8,128)}, f32[384,256]{1,0:T(8,128)}, /*i...) custom-call(s32[1,1,15]{2,1,0:T(1,128)} %rows_in.11, ...), custom_call_target="tpu_custom_call" | custom-call | flops 2264924160 | bytes 20000000 | tf_op jit(solution)/shard_map/pallas_call | solution.py:295
  23.8 1.9 %copy-done = f32[15,256,256]{2,1,0:T(8,128)} copy-done((f32[15,256,256]{2,1,0:T(8,128)}, f32[15,256,256]{2,1,0:T(8,128)S(1)}, u32[]{:S(2)}) %copy-start) | copy-done | bytes 3932184
  25.7 1.6 %collective-permute-start.13 = (f32[384,256]{1,0:T(8,128)}, f32[384,256]{1,0:T(8,128)}, u32[]{:S(2)}, u32[]{:S(2)}) collective-permute-start(f32[384,256]{1,0:T(8,128)} %get-tuple-element.45), channel_id=1, source_target_pairs={{0,2},{2,4},{4,6},{6,7},{7,5},{5,3},{3,1},{1,0},{10,8},{12,10},{14... | collective-permute-start | bytes 1179656 | tf_op jit(solution)/shard_map/ppermute | solution.py:231
  27.3 1.6 %collective-permute-start.7 = (f32[384,256]{1,0:T(8,128)S(1)}, f32[384,256]{1,0:T(8,128)S(1)}, u32[]{:S(2)}, u32[]{:S(2)}) collective-permute-start(f32[384,256]{1,0:T(8,128)S(1)} %collective-permute-done.4.refs_2_), channel_id=1, source_target_pairs={{0,2},{2,4},{4,6},{6,7},{7,5},{5,3},{3,1},{1,0},{8,10},{10,12},{12... | collective-permute-start | bytes 1179656 | tf_op jit(solution)/shard_map/ppermute | solution.py:224
  29.3 7.5 %collective-permute-done.13 = f32[384,256]{1,0:T(8,128)} collective-permute-done((f32[384,256]{1,0:T(8,128)}, f32[384,256]{1,0:T(8,128)}, u32[]{:S(2)}, u32[]{:S(2)}) %collective-permute-start.13) | collective-permute-done | bytes 393248 | tf_op jit(solution)/shard_map/ppermute | solution.py:231
  36.8 1.3 %add_select_fusion.1 = (f32[384,256]{1,0:T(8,128)S(1)}, f32[384,256]{1,0:T(8,128)S(1)}) fusion(f32[384,256]{1,0:T(8,128)} %get-tuple-element.44, f32[384,256]{1,0:T(8,128)} %collective-permute-done.13, pred[]{:T(512)S(6)} %eq.5, f32[384,256]{1,0:T(8,128)} %get-tuple-element.48), kind=kLoop, calls=%fused_computation.1 | loop fusion | flops 393216 | bytes 1966081 | tf_op jit(solution)/shard_map/jit(_where)/select_n | solution.py:232
  38.1 1.6 %collective-permute-start.17 = (f32[384,256]{1,0:T(8,128)S(1)}, f32[384,256]{1,0:T(8,128)S(1)}, u32[]{:S(2)}, u32[]{:S(2)}) collective-permute-start(f32[384,256]{1,0:T(8,128)S(1)} %get-tuple-element.67), channel_id=1, source_target_pairs={{2,0},{4,2},{6,4},{7,6},{5,7},{3,5},{1,3},{0,1},{10,8},{12,10},{14... | collective-permute-start | bytes 1179656 | tf_op jit(solution)/shard_map/ppermute | solution.py:236
  40.2 3.9 %collective-permute-done.7.refs_3_ = f32[384,256]{1,0:T(8,128)S(1)} collective-permute-done((f32[384,256]{1,0:T(8,128)S(1)}, f32[384,256]{1,0:T(8,128)S(1)}, u32[]{:S(2)}, u32[]{:S(2)}) %collective-permute-start.7) | collective-permute-done | bytes 393248 | tf_op jit(solution)/shard_map/ppermute | solution.py:224
  45.4 4.8 %collective-permute-done.17 = f32[384,256]{1,0:T(8,128)S(1)} collective-permute-done((f32[384,256]{1,0:T(8,128)S(1)}, f32[384,256]{1,0:T(8,128)S(1)}, u32[]{:S(2)}, u32[]{:S(2)}) %collective-permute-start.17) | collective-permute-done | bytes 393248 | tf_op jit(solution)/shard_map/ppermute | solution.py:236
  51.3 1.6 %collective-permute-start.18 = (f32[384,256]{1,0:T(8,128)S(1)}, f32[384,256]{1,0:T(8,128)S(1)}, u32[]{:S(2)}, u32[]{:S(2)}) collective-permute-start(f32[384,256]{1,0:T(8,128)S(1)} %add.50), channel_id=1, source_target_pairs={{2,0},{4,2},{6,4},{7,6},{5,7},{3,5},{1,3},{0,1},{10,8},{12,10},{14... | collective-permute-start | bytes 1179656 | tf_op jit(solution)/shard_map/ppermute | solution.py:236
  54.6 5.0 %shard_map.78 = (f32[384,256]{1,0:T(8,128)S(1)}, f32[384,256]{1,0:T(8,128)S(1)}, f32[384,256]{1,0:T(8,128)S(1)}, f32[384,256]{1,0:T(8,128)S(1)}) custom-call(s32[1,1,15]{2,1,0:T(1,128)} %rows_in.11, s32[1,1,15]{2,1,0:T(1,128)} %cols_in.11, f32[256,256]{1,0:T(8,128)} %d_in.3, f32[15,256,256]{2,1,0:T(8,128)S(1)} %copy-done.1, f32[384,256]{1,0:T(8,128)S(1)} %copy-done.3, ...), custom_call_target="tpu_custom_call" | custom-call | flops 2264924160 | bytes 20000000 | tf_op jit(solution)/shard_map/pallas_call | solution.py:306
  60.9 1.7 %collective-permute-start.19 = (f32[384,256]{1,0:T(8,128)S(1)}, f32[384,256]{1,0:T(8,128)S(1)}, u32[]{:S(2)}, u32[]{:S(2)}) collective-permute-start(f32[384,256]{1,0:T(8,128)S(1)} %add.51), channel_id=1, source_target_pairs={{2,0},{4,2},{6,4},{7,6},{5,7},{3,5},{1,3},{0,1},{10,8},{12,10},{14... | collective-permute-start | bytes 1179656 | tf_op jit(solution)/shard_map/ppermute | solution.py:236
  63.1 1.8 %collective-permute-start.11 = (f32[384,256]{1,0:T(8,128)S(1)}, f32[384,256]{1,0:T(8,128)S(1)}, u32[]{:S(2)}, u32[]{:S(2)}) collective-permute-start(f32[384,256]{1,0:T(8,128)S(1)} %add.41), channel_id=1, source_target_pairs={{0,16},{8,24},{16,0},{24,8},{1,17},{9,25},{17,1},{25,9},{2,18},{10... | collective-permute-start | bytes 1179656 | tf_op jit(solution)/shard_map/ppermute | solution.py:252
  64.9 2.2 %shard_map.79 = (bf16[8,256,384]{2,1,0:T(8,128)(2,1)S(1)}, bf16[8,256,384]{2,1,0:T(8,128)(2,1)S(1)}, bf16[4,384,256]{2,1,0:T(8,128)(2,1)S(1)}, bf16[4,384,256]{2,1,0:T(8,128)(2,1)S(1)}) custom-call(f32[384,256]{1,0:T(8,128)S(1)} %copy-done.3, f32[384,256]{1,0:T(8,128)S(1)} %collective-permute-done.3.refs_1_, f32[384,256]{1,0:T(8,128)S(1)} %collective-permute-done.4.refs_2_, ...), custom_call_target="tpu_custom_call" | custom-call | flops 2264924160 | bytes 20000000 | tf_op jit(solution)/shard_map/pallas_call | solution.py:316
  67.1 4.3 %collective-permute-done.19 = f32[384,256]{1,0:T(8,128)S(1)} collective-permute-done((f32[384,256]{1,0:T(8,128)S(1)}, f32[384,256]{1,0:T(8,128)S(1)}, u32[]{:S(2)}, u32[]{:S(2)}) %collective-permute-start.19) | collective-permute-done | bytes 393248 | tf_op jit(solution)/shard_map/ppermute | solution.py:236
  71.4 1.4 %collective-permute-done.16 = f32[384,256]{1,0:T(8,128)S(1)} collective-permute-done((f32[384,256]{1,0:T(8,128)S(1)}, f32[384,256]{1,0:T(8,128)S(1)}, u32[]{:S(2)}, u32[]{:S(2)}) %collective-permute-start.16) | collective-permute-done | bytes 393248 | tf_op jit(solution)/shard_map/ppermute | solution.py:235
  73.3 1.6 %collective-permute-start.21 = (f32[384,256]{1,0:T(8,128)S(1)}, f32[384,256]{1,0:T(8,128)S(1)}, u32[]{:S(2)}, u32[]{:S(2)}) collective-permute-start(f32[384,256]{1,0:T(8,128)S(1)} %add_add_fusion.refs_0_), channel_id=1, source_target_pairs={{0,16},{8,24},{16,0},{24,8},{1,17},{9,25},{17,1},{25,9},{2,18},{10... | collective-permute-start | bytes 1179656 | tf_op jit(solution)/shard_map/ppermute | solution.py:245
  74.8 1.4 %collective-permute-start.23 = (f32[384,256]{1,0:T(8,128)S(1)}, f32[384,256]{1,0:T(8,128)S(1)}, u32[]{:S(2)}, u32[]{:S(2)}) collective-permute-start(f32[384,256]{1,0:T(8,128)S(1)} %add_add_fusion.refs_0_), channel_id=1, source_target_pairs={{0,2},{2,4},{4,6},{6,7},{7,5},{5,3},{3,1},{1,0},{8,10},{10,12},{12... | collective-permute-start | bytes 1179656 | tf_op jit(solution)/shard_map/ppermute | solution.py:224
  76.9 5.5 %collective-permute-done.21.refs_2_ = f32[384,256]{1,0:T(8,128)S(1)} collective-permute-done((f32[384,256]{1,0:T(8,128)S(1)}, f32[384,256]{1,0:T(8,128)S(1)}, u32[]{:S(2)}, u32[]{:S(2)}) %collective-permute-start.21) | collective-permute-done | bytes 393248 | tf_op jit(solution)/shard_map/ppermute | solution.py:245
  85.5 5.0 %shard_map.80 = (f32[15,256,256]{2,1,0:T(8,128)S(1)}, f32[256,256]{1,0:T(8,128)}) custom-call(s32[1,1,15]{2,1,0:T(1,128)} %rows_in.11, s32[1,1,15]{2,1,0:T(1,128)} %cols_in.11, s32[1,1,15]{2,1,0:T(1,128)} %live_in.7, f32[256,256]{1,0:T(8,128)} %d_in.3, f32[15,256,256]{2,1,0:T(8,128)S(1)} %copy-done.1, bf16[8,256,384]{2,1,0:T(8,128)(2,1)S(1)} %get-tuple-element.53.th, ...), custom_call_target="tpu_custom_call" | custom-call | flops 2264924160 | bytes 20000000 | tf_op jit(solution)/shard_map/pallas_call | solution.py:331
  90.5 3.4 %collective-permute-done.25.refs_3_ = f32[384,256]{1,0:T(8,128)S(1)} collective-permute-done((f32[384,256]{1,0:T(8,128)S(1)}, f32[384,256]{1,0:T(8,128)S(1)}, u32[]{:S(2)}, u32[]{:S(2)}) %collective-permute-start.25) | collective-permute-done | bytes 393248 | tf_op jit(solution)/shard_map/ppermute | solution.py:224
  94.4 1.6 %collective-permute-start.27 = (f32[384,256]{1,0:T(8,128)S(1)}, f32[384,256]{1,0:T(8,128)S(1)}, u32[]{:S(2)}, u32[]{:S(2)}) collective-permute-start(f32[384,256]{1,0:T(8,128)S(1)} %collective-permute-done.25.refs_3_), channel_id=1, source_target_pairs={{0,2},{2,4},{4,6},{6,7},{7,5},{5,3},{3,1},{1,0},{8,10},{10,12},{12... | collective-permute-start | bytes 1179656 | tf_op jit(solution)/shard_map/ppermute | solution.py:224
  96.5 6.2 %shard_map.81 = (f32[1,1,15,256,256]{4,3,2,1,0:T(8,128)}, f32[15,256,256]{2,1,0:T(8,128)S(1)}) custom-call(s32[1,1,15]{2,1,0:T(1,128)} %rows_in.11, s32[1,1,15]{2,1,0:T(1,128)} %cols_in.11, s32[1,1,15]{2,1,0:T(1,128)} %live_in.7, f32[15,256,256]{2,1,0:T(8,128)S(1)} %get-tuple-element.56.v_ref, bf16[4,384,256]{2,1,0:T(8,128)(2,1)S(1)} %get-tuple-element.57.rh, ...), custom_call_target="tpu_custom_call" | custom-call | flops 2264924160 | bytes 20000000 | tf_op jit(solution)/shard_map/pallas_call | solution.py:346
  103.4 1.9 %collective-permute-done.28.refs_1_ = f32[384,256]{1,0:T(8,128)S(1)} collective-permute-done((f32[384,256]{1,0:T(8,128)S(1)}, f32[384,256]{1,0:T(8,128)S(1)}, u32[]{:S(2)}, u32[]{:S(2)}) %collective-permute-start.28) | collective-permute-done | bytes 393248 | tf_op jit(solution)/shard_map/ppermute | solution.py:225
  106.6 3.4 %shard_map.82.refs_1_ = f32[1,1,15,256,256]{4,3,2,1,0:T(8,128)} custom-call(s32[1,1,15]{2,1,0:T(1,128)} %rows_in.11, s32[1,1,15]{2,1,0:T(1,128)} %cols_in.11, s32[1,1,15]{2,1,0:T(1,128)} %live_in.7, f32[15,256,256]{2,1,0:T(8,128)S(1)} %get-tuple-element.59.v_ref, bf16[4,384,256]{2,1,0:T(8,128)(2,1)S(1)} %get-tuple-element.57.rh, ...), custom_call_target="tpu_custom_call", output_to_operand_aliasing={{}: (8, {})} | custom-call | flops 2264924160 | bytes 20000000 | tf_op jit(solution)/shard_map/pallas_call | solution.py:362
  110.0 3.1 %collective-permute-done.29.refs_0_ = f32[384,256]{1,0:T(8,128)S(1)} collective-permute-done((f32[384,256]{1,0:T(8,128)S(1)}, f32[384,256]{1,0:T(8,128)S(1)}, u32[]{:S(2)}, u32[]{:S(2)}) %collective-permute-start.29) | collective-permute-done | bytes 393248 | tf_op jit(solution)/shard_map/ppermute | solution.py:227
  113.1 2.5 %shard_map.83 = f32[1,1,15,256,256]{4,3,2,1,0:T(8,128)} custom-call(s32[1,1,15]{2,1,0:T(1,128)} %rows_in.11, s32[1,1,15]{2,1,0:T(1,128)} %cols_in.11, s32[1,1,15]{2,1,0:T(1,128)} %live_in.7, f32[15,256,256]{2,1,0:T(8,128)S(1)} %get-tuple-element.59.v_ref, bf16[4,384,256]{2,1,0:T(8,128)(2,1)S(1)} %get-tuple-element.57.rh, ...), custom_call_target="tpu_custom_call", output_to_operand_aliasing={{}: (7, {})} | custom-call | flops 2264924160 | bytes 20000000 | tf_op jit(solution)/shard_map/pallas_call | solution.py:362
  (58 shorter events, 15.8 us)
Async XLA Ops:
  0.6 12.3 %collective-permute-start.1 = (f32[384,256]{1,0:T(8,128)}, f32[384,256]{1,0:T(8,128)S(1)}, u32[]{:S(2)}, u32[]{:S(2)}) collective-permute-start(f32[384,256]{1,0:T(8,128)} %refs_8_.1), channel_id=1, source_target_pairs={{0,16},{8,24},{16,0},{24,8},{1,17},{9,25},{17,1},{25,9},{2,18},{10... | collective-permute-start | bytes 1179656 | tf_op jit(solution)/shard_map/ppermute | solution.py:245
  3.6 10.8 %collective-permute-start.3 = (f32[384,256]{1,0:T(8,128)}, f32[384,256]{1,0:T(8,128)S(1)}, u32[]{:S(2)}, u32[]{:S(2)}) collective-permute-start(f32[384,256]{1,0:T(8,128)} %refs_8_.1), channel_id=1, source_target_pairs={{0,2},{2,4},{4,6},{6,7},{7,5},{5,3},{3,1},{1,0},{8,10},{10,12},{12... | collective-permute-start | bytes 1179656 | tf_op jit(solution)/shard_map/ppermute | solution.py:224
  5.2 10.8 %collective-permute-start.5 = (f32[384,256]{1,0:T(8,128)}, f32[384,256]{1,0:T(8,128)S(1)}, u32[]{:S(2)}, u32[]{:S(2)}) collective-permute-start(f32[384,256]{1,0:T(8,128)} %refs_8_.1), channel_id=1, source_target_pairs={{2,0},{4,2},{6,4},{7,6},{5,7},{3,5},{1,3},{0,1},{10,8},{12,10},{14... | collective-permute-start | bytes 1179656 | tf_op jit(solution)/shard_map/ppermute | solution.py:225
  5.7 10.8 %collective-permute-start = (f32[384,256]{1,0:T(8,128)}, f32[384,256]{1,0:T(8,128)S(1)}, u32[]{:S(2)}, u32[]{:S(2)}) collective-permute-start(f32[384,256]{1,0:T(8,128)} %refs_8_.1), channel_id=1, source_target_pairs={{0,8},{8,0},{16,24},{24,16},{1,9},{9,1},{17,25},{25,17},{2,10},{10... | collective-permute-start | bytes 1179656 | tf_op jit(solution)/shard_map/ppermute | solution.py:246
  13.0 3.5 %collective-permute-start.2 = (f32[384,256]{1,0:T(8,128)S(1)}, f32[384,256]{1,0:T(8,128)S(1)}, u32[]{:S(2)}, u32[]{:S(2)}) collective-permute-start(f32[384,256]{1,0:T(8,128)S(1)} %collective-permute-done.1.refs_2_.refs_10_), channel_id=1, source_target_pairs={{0,8},{8,0},{16,24},{24,16},{1,9},{9,1},{17,25},{25,17},{2,10},{10... | collective-permute-start | bytes 1179656 | tf_op jit(solution)/shard_map/ppermute | solution.py:246
  14.4 12.9 %collective-permute-start.4 = (f32[384,256]{1,0:T(8,128)S(1)}, f32[384,256]{1,0:T(8,128)S(1)}, u32[]{:S(2)}, u32[]{:S(2)}) collective-permute-start(f32[384,256]{1,0:T(8,128)S(1)} %collective-permute-done.3.refs_1_), channel_id=1, source_target_pairs={{0,2},{2,4},{4,6},{6,7},{7,5},{5,3},{3,1},{1,0},{8,10},{10,12},{12... | collective-permute-start | bytes 1179656 | tf_op jit(solution)/shard_map/ppermute | solution.py:224
  16.0 11.3 %collective-permute-start.6 = (f32[384,256]{1,0:T(8,128)S(1)}, f32[384,256]{1,0:T(8,128)}, u32[]{:S(2)}, u32[]{:S(2)}) collective-permute-start(f32[384,256]{1,0:T(8,128)S(1)} %collective-permute-done.5.refs_7_), channel_id=1, source_target_pairs={{2,0},{4,2},{6,4},{7,6},{5,7},{3,5},{1,3},{0,1},{10,8},{12,10},{14... | collective-permute-start | bytes 1179656 | tf_op jit(solution)/shard_map/ppermute | solution.py:225
  25.7 28.9 %copy-start.3 = (f32[384,256]{1,0:T(8,128)S(1)}, f32[384,256]{1,0:T(8,128)}, u32[]{:S(2)}) copy-start(f32[384,256]{1,0:T(8,128)} %refs_8_.1) | copy-start | bytes 1179652
  25.7 11.1 %collective-permute-start.13 = (f32[384,256]{1,0:T(8,128)}, f32[384,256]{1,0:T(8,128)}, u32[]{:S(2)}, u32[]{:S(2)}) collective-permute-start(f32[384,256]{1,0:T(8,128)} %get-tuple-element.45), channel_id=1, source_target_pairs={{0,2},{2,4},{4,6},{6,7},{7,5},{5,3},{3,1},{1,0},{10,8},{12,10},{14... | collective-permute-start | bytes 1179656 | tf_op jit(solution)/shard_map/ppermute | solution.py:231
  27.3 16.8 %collective-permute-start.7 = (f32[384,256]{1,0:T(8,128)S(1)}, f32[384,256]{1,0:T(8,128)S(1)}, u32[]{:S(2)}, u32[]{:S(2)}) collective-permute-start(f32[384,256]{1,0:T(8,128)S(1)} %collective-permute-done.4.refs_2_), channel_id=1, source_target_pairs={{0,2},{2,4},{4,6},{6,7},{7,5},{5,3},{3,1},{1,0},{8,10},{10,12},{12... | collective-permute-start | bytes 1179656 | tf_op jit(solution)/shard_map/ppermute | solution.py:224
  28.9 15.3 %collective-permute-start.8 = (f32[384,256]{1,0:T(8,128)}, f32[384,256]{1,0:T(8,128)S(1)}, u32[]{:S(2)}, u32[]{:S(2)}) collective-permute-start(f32[384,256]{1,0:T(8,128)} %collective-permute-done.6.refs_6_), channel_id=1, source_target_pairs={{2,0},{4,2},{6,4},{7,6},{5,7},{3,5},{1,3},{0,1},{10,8},{12,10},{14... | collective-permute-start | bytes 1179656 | tf_op jit(solution)/shard_map/ppermute | solution.py:225
  29.3 25.3 %copy-start.1 = (f32[15,256,256]{2,1,0:T(8,128)S(1)}, f32[15,256,256]{2,1,0:T(8,128)}, u32[]{:S(2)}) copy-start(f32[15,256,256]{2,1,0:T(8,128)} %copy-done) | copy-start | bytes 11796484
  38.1 12.1 %collective-permute-start.17 = (f32[384,256]{1,0:T(8,128)S(1)}, f32[384,256]{1,0:T(8,128)S(1)}, u32[]{:S(2)}, u32[]{:S(2)}) collective-permute-start(f32[384,256]{1,0:T(8,128)S(1)} %get-tuple-element.67), channel_id=1, source_target_pairs={{2,0},{4,2},{6,4},{7,6},{5,7},{3,5},{1,3},{0,1},{10,8},{12,10},{14... | collective-permute-start | bytes 1179656 | tf_op jit(solution)/shard_map/ppermute | solution.py:236
  39.8 13.2 %collective-permute-start.14 = (f32[384,256]{1,0:T(8,128)S(1)}, f32[384,256]{1,0:T(8,128)S(1)}, u32[]{:S(2)}, u32[]{:S(2)}) collective-permute-start(f32[384,256]{1,0:T(8,128)S(1)} %get-tuple-element.66), channel_id=1, source_target_pairs={{0,2},{2,4},{4,6},{6,7},{7,5},{5,3},{3,1},{1,0},{8,10},{10,12},{12... | collective-permute-start | bytes 1179656 | tf_op jit(solution)/shard_map/ppermute | solution.py:235
  44.2 10.4 %collective-permute-start.9 = (f32[384,256]{1,0:T(8,128)S(1)}, f32[384,256]{1,0:T(8,128)S(1)}, u32[]{:S(2)}, u32[]{:S(2)}) collective-permute-start(f32[384,256]{1,0:T(8,128)S(1)} %broadcast_select_fusion.1), channel_id=1, source_target_pairs={{0,2},{2,4},{4,6},{6,7},{7,5},{5,3},{3,1},{1,0},{10,8},{12,10},{14... | collective-permute-start | bytes 1179656 | tf_op jit(solution)/shard_map/ppermute | solution.py:227
  51.3 9.5 %collective-permute-start.18 = (f32[384,256]{1,0:T(8,128)S(1)}, f32[384,256]{1,0:T(8,128)S(1)}, u32[]{:S(2)}, u32[]{:S(2)}) collective-permute-start(f32[384,256]{1,0:T(8,128)S(1)} %add.50), channel_id=1, source_target_pairs={{2,0},{4,2},{6,4},{7,6},{5,7},{3,5},{1,3},{0,1},{10,8},{12,10},{14... | collective-permute-start | bytes 1179656 | tf_op jit(solution)/shard_map/ppermute | solution.py:236
  54.0 8.6 %collective-permute-start.15 = (f32[384,256]{1,0:T(8,128)S(1)}, f32[384,256]{1,0:T(8,128)S(1)}, u32[]{:S(2)}, u32[]{:S(2)}) collective-permute-start(f32[384,256]{1,0:T(8,128)S(1)} %add.46), channel_id=1, source_target_pairs={{0,2},{2,4},{4,6},{6,7},{7,5},{5,3},{3,1},{1,0},{8,10},{10,12},{12... | collective-permute-start | bytes 1179656 | tf_op jit(solution)/shard_map/ppermute | solution.py:235
  59.6 3.5 %collective-permute-start.10 = (f32[384,256]{1,0:T(8,128)S(1)}, f32[384,256]{1,0:T(8,128)S(1)}, u32[]{:S(2)}, u32[]{:S(2)}) collective-permute-start(f32[384,256]{1,0:T(8,128)S(1)} %get-tuple-element.39), channel_id=1, source_target_pairs={{0,8},{8,0},{16,24},{24,16},{1,9},{9,1},{17,25},{25,17},{2,10},{10... | collective-permute-start | bytes 1179656 | tf_op jit(solution)/shard_map/ppermute | solution.py:249
  59.7 7.4 %collective-permute-start.12 = (f32[384,256]{1,0:T(8,128)S(1)}, f32[384,256]{1,0:T(8,128)S(1)}, u32[]{:S(2)}, u32[]{:S(2)}) collective-permute-start(f32[384,256]{1,0:T(8,128)S(1)} %get-tuple-element.41), channel_id=1, source_target_pairs={{0,8},{8,0},{16,24},{24,16},{1,9},{9,1},{17,25},{25,17},{2,10},{10... | collective-permute-start | bytes 1179656 | tf_op jit(solution)/shard_map/ppermute | solution.py:249
  60.9 10.5 %collective-permute-start.19 = (f32[384,256]{1,0:T(8,128)S(1)}, f32[384,256]{1,0:T(8,128)S(1)}, u32[]{:S(2)}, u32[]{:S(2)}) collective-permute-start(f32[384,256]{1,0:T(8,128)S(1)} %add.51), channel_id=1, source_target_pairs={{2,0},{4,2},{6,4},{7,6},{5,7},{3,5},{1,3},{0,1},{10,8},{12,10},{14... | collective-permute-start | bytes 1179656 | tf_op jit(solution)/shard_map/ppermute | solution.py:236
  62.7 10.1 %collective-permute-start.16 = (f32[384,256]{1,0:T(8,128)S(1)}, f32[384,256]{1,0:T(8,128)S(1)}, u32[]{:S(2)}, u32[]{:S(2)}) collective-permute-start(f32[384,256]{1,0:T(8,128)S(1)} %add.47), channel_id=1, source_target_pairs={{0,2},{2,4},{4,6},{6,7},{7,5},{5,3},{3,1},{1,0},{8,10},{10,12},{12... | collective-permute-start | bytes 1179656 | tf_op jit(solution)/shard_map/ppermute | solution.py:235
  63.1 10.0 %collective-permute-start.11 = (f32[384,256]{1,0:T(8,128)S(1)}, f32[384,256]{1,0:T(8,128)S(1)}, u32[]{:S(2)}, u32[]{:S(2)}) collective-permute-start(f32[384,256]{1,0:T(8,128)S(1)} %add.41), channel_id=1, source_target_pairs={{0,16},{8,24},{16,0},{24,8},{1,17},{9,25},{17,1},{25,9},{2,18},{10... | collective-permute-start | bytes 1179656 | tf_op jit(solution)/shard_map/ppermute | solution.py:252
  73.3 9.1 %collective-permute-start.21 = (f32[384,256]{1,0:T(8,128)S(1)}, f32[384,256]{1,0:T(8,128)S(1)}, u32[]{:S(2)}, u32[]{:S(2)}) collective-permute-start(f32[384,256]{1,0:T(8,128)S(1)} %add_add_fusion.refs_0_), channel_id=1, source_target_pairs={{0,16},{8,24},{16,0},{24,8},{1,17},{9,25},{17,1},{25,9},{2,18},{10... | collective-permute-start | bytes 1179656 | tf_op jit(solution)/shard_map/ppermute | solution.py:245
  74.8 8.6 %collective-permute-start.23 = (f32[384,256]{1,0:T(8,128)S(1)}, f32[384,256]{1,0:T(8,128)S(1)}, u32[]{:S(2)}, u32[]{:S(2)}) collective-permute-start(f32[384,256]{1,0:T(8,128)S(1)} %add_add_fusion.refs_0_), channel_id=1, source_target_pairs={{0,2},{2,4},{4,6},{6,7},{7,5},{5,3},{3,1},{1,0},{8,10},{10,12},{12... | collective-permute-start | bytes 1179656 | tf_op jit(solution)/shard_map/ppermute | solution.py:224
  76.3 8.4 %collective-permute-start.24 = (f32[384,256]{1,0:T(8,128)S(1)}, f32[384,256]{1,0:T(8,128)S(1)}, u32[]{:S(2)}, u32[]{:S(2)}) collective-permute-start(f32[384,256]{1,0:T(8,128)S(1)} %add_add_fusion.refs_0_), channel_id=1, source_target_pairs={{2,0},{4,2},{6,4},{7,6},{5,7},{3,5},{1,3},{0,1},{10,8},{12,10},{14... | collective-permute-start | bytes 1179656 | tf_op jit(solution)/shard_map/ppermute | solution.py:225
  76.9 8.6 %collective-permute-start.20 = (f32[384,256]{1,0:T(8,128)S(1)}, f32[384,256]{1,0:T(8,128)S(1)}, u32[]{:S(2)}, u32[]{:S(2)}) collective-permute-start(f32[384,256]{1,0:T(8,128)S(1)} %add_add_fusion.refs_0_), channel_id=1, source_target_pairs={{0,8},{8,0},{16,24},{24,16},{1,9},{9,1},{17,25},{25,17},{2,10},{10... | collective-permute-start | bytes 1179656 | tf_op jit(solution)/shard_map/ppermute | solution.py:246
  82.3 3.1 %collective-permute-start.22 = (f32[384,256]{1,0:T(8,128)S(1)}, f32[384,256]{1,0:T(8,128)S(1)}, u32[]{:S(2)}, u32[]{:S(2)}) collective-permute-start(f32[384,256]{1,0:T(8,128)S(1)} %collective-permute-done.21.refs_2_), channel_id=1, source_target_pairs={{0,8},{8,0},{16,24},{24,16},{1,9},{9,1},{17,25},{25,17},{2,10},{10... | collective-permute-start | bytes 1179656 | tf_op jit(solution)/shard_map/ppermute | solution.py:246
  83.4 10.4 %collective-permute-start.25 = (f32[384,256]{1,0:T(8,128)S(1)}, f32[384,256]{1,0:T(8,128)S(1)}, u32[]{:S(2)}, u32[]{:S(2)}) collective-permute-start(f32[384,256]{1,0:T(8,128)S(1)} %collective-permute-done.23.refs_1_), channel_id=1, source_target_pairs={{0,2},{2,4},{4,6},{6,7},{7,5},{5,3},{3,1},{1,0},{8,10},{10,12},{12... | collective-permute-start | bytes 1179656 | tf_op jit(solution)/shard_map/ppermute | solution.py:224
  84.6 9.8 %collective-permute-start.26 = (f32[384,256]{1,0:T(8,128)S(1)}, f32[384,256]{1,0:T(8,128)S(1)}, u32[]{:S(2)}, u32[]{:S(2)}) collective-permute-start(f32[384,256]{1,0:T(8,128)S(1)} %collective-permute-done.24.refs_2_), channel_id=1, source_target_pairs={{2,0},{4,2},{6,4},{7,6},{5,7},{3,5},{1,3},{0,1},{10,8},{12,10},{14... | collective-permute-start | bytes 1179656 | tf_op jit(solution)/shard_map/ppermute | solution.py:225
  94.4 8.9 %collective-permute-start.27 = (f32[384,256]{1,0:T(8,128)S(1)}, f32[384,256]{1,0:T(8,128)S(1)}, u32[]{:S(2)}, u32[]{:S(2)}) collective-permute-start(f32[384,256]{1,0:T(8,128)S(1)} %collective-permute-done.25.refs_3_), channel_id=1, source_target_pairs={{0,2},{2,4},{4,6},{6,7},{7,5},{5,3},{3,1},{1,0},{8,10},{10,12},{12... | collective-permute-start | bytes 1179656 | tf_op jit(solution)/shard_map/ppermute | solution.py:224
  96.1 9.2 %collective-permute-start.28 = (f32[384,256]{1,0:T(8,128)S(1)}, f32[384,256]{1,0:T(8,128)S(1)}, u32[]{:S(2)}, u32[]{:S(2)}) collective-permute-start(f32[384,256]{1,0:T(8,128)S(1)} %collective-permute-done.26.refs_4_), channel_id=1, source_target_pairs={{2,0},{4,2},{6,4},{7,6},{5,7},{3,5},{1,3},{0,1},{10,8},{12,10},{14... | collective-permute-start | bytes 1179656 | tf_op jit(solution)/shard_map/ppermute | solution.py:225
  105.3 7.8 %collective-permute-start.29 = (f32[384,256]{1,0:T(8,128)S(1)}, f32[384,256]{1,0:T(8,128)S(1)}, u32[]{:S(2)}, u32[]{:S(2)}) collective-permute-start(f32[384,256]{1,0:T(8,128)S(1)} %broadcast_select_fusion), channel_id=1, source_target_pairs={{0,2},{2,4},{4,6},{6,7},{7,5},{5,3},{3,1},{1,0},{10,8},{12,10},{14... | collective-permute-start | bytes 1179656 | tf_op jit(solution)/shard_map/ppermute | solution.py:227
  (5 other events, 27.1 us)

commit v2 on v1

--- a/solution.py
+++ b/solution.py
@@ -73,28 +73,34 @@
     return copies
 
 
-def w_kernel(nr, nc, rows_in, cols_in, t_in, *refs):
-    x_refs, out_refs, refs = refs[:nr], refs[nr : nr + nc], refs[nr + nc :]
-    t_ref, rows, cols, sems, t_sems, out_sems, xh, xl, acc = refs
-    small = fetch((rows_in, cols_in), (rows, cols), sems)
+def w_kernel(nr, nc, near, rows_in, cols_in, own_in, t_in, *refs):
+    x_refs, out_refs, refs = refs[: nr - 1], refs[nr - 1 : nr - 1 + nc], refs[nr - 1 + nc :]
+    t_ref, rows, cols, own, sems, t_sems, out_sems, xh, xl, acc = refs
+    small = fetch((own_in, rows_in, cols_in), (own, rows, cols), sems)
     groups = []
     for k in range(t_ref.shape[0] // GROUP):
         at = pl.ds(k * GROUP, GROUP)
         groups.append(pltpu.make_async_copy(t_in.at[0, 0, at], t_ref.at[at], t_sems.at[k]))
         groups[-1].start()
-    fill(x_refs, xh, xl)
+    for k, ref in enumerate(x_refs):
+        xh[k + 1], xl[k + 1] = split(ref[...])
     acc[...] = jnp.zeros_like(acc)
     for copy in small:
         copy.wait()
+    xh[0], xl[0] = split(own[...])
     for slot in range(t_ref.shape[0]):
         if slot % GROUP == 0:
             groups[slot // GROUP].wait()
         j = row_slot(cols[slot], nr, 1)
         i = ahead(rows[slot], nc)
         acc[i] += dot3((xh[j], xl[j]), split(t_ref[slot]), NT)
-    copies = [pltpu.make_async_copy(acc.at[k], out_refs[k], out_sems.at[k]) for k in range(nc)]
-    for copy in copies:
-        copy.start()
+    copies = []
+    for k in range(nc):
+        if k in near:
+            out_refs[k][...] = acc[k]
+        else:
+            copies.append(pltpu.make_async_copy(acc.at[k], out_refs[k], out_sems.at[k]))
+            copies[-1].start()
     for copy in copies:
         copy.wait()
 
@@ -291,17 +297,26 @@
     tile_rows, tile_cols, tile_active, omega_tiles, omega_diag = map(
         in_hbm, (tile_rows, tile_cols, tile_active, omega_tiles, omega_diag)
     )
-    x_row = row_gather(samples)
-    *w, held = call(
-        functools.partial(w_kernel, nr, nc),
-        3,
-        nr,
-        [in_place] * nc + [whole],
-        [pltpu.HBM((count, side), F32)] * nc + [tiles],
-        ids(2) + [sems(2), sems(slots // GROUP), sems(nc)] + panel(nr) + [pltpu.VMEM((nc, count, side), F32)],
-        10 + nc,
-    )(tile_rows, tile_cols, omega_tiles, *x_row)
-    x_col = ring_gather(samples, {far - 1: lambda found: w[0]})
+    near = ()
+    x_row, w = [], []
+
+    def mirror(found):
+        source = samples
+        x_row.extend(row_gather(source))
+        made_w = call(
+            functools.partial(w_kernel, nr, nc, near),
+            4,
+            nr - 1,
+            [whole if k in near else in_place for k in range(nc)] + [whole],
+            [block if k in near else pltpu.HBM((count, side), F32) for k in range(nc)] + [tiles],
+            ids(2) + [pltpu.VMEM((count, side), F32), sems(3), sems(slots // GROUP), sems(nc)] + panel(nr) + [pltpu.VMEM((nc, count, side), F32)],
+            10 + nc,
+        )(tile_rows, tile_cols, in_hbm(samples), omega_tiles, *x_row[1:])
+        w.extend(made_w)
+        return w[0]
+
+    x_col = ring_gather(samples, {far: mirror})
+    held = w.pop()
     w_own = ring_sum(w)
     y = call(
         functools.partial(y_kernel, nr, nc),

time: 116 us -> 115 us (level)
    ppermute x6, starting transfers between devices: 9.03 us -> 7.86 us  [ring_gather(): found[d] = go(one, 'col', right)]
    unnamed x14 -> x12, local copies, waits for them, and re-layouts: 2.93 us -> 1.94 us
  transfers between devices with their start and end apart: 30 -> 30, of which waited for: 17 -> 17; matrix products, arithmetic and copies ran while one was open for 3% -> 3% of each run, Pallas kernels for 24% -> 25%
where the time goes in v2:
time: 115 us; the launch traced here: 114 us
  waiting for transfers between devices  47.3 us (41%)
  Pallas kernels  30.7 us (27%)
  starting transfers between devices  29.7 us (26%)
  other arithmetic  3.81 us (3%)
  local copies, waits for them, and re-layouts  1.94 us (2%)
    ppermute x2, waiting for transfers between devices, row_gather(): found.append(go(found[-1], 'row', chip))  12.7 us
    ppermute x6, waiting for transfers between devices, ring_gather(): found[d] = go(one, 'col', right)  10.9 us
    ppermute x3, waiting for transfers between devices, ring_sum(): two = go(two, 'col', left)  9.82 us
    ppermute x6, starting transfers between devices, ring_gather(): found[d] = go(one, 'col', right)  7.86 us
    ppermute x1, waiting for transfers between devices, ring_sum(): first = go(parts[far], ('row', 'col'), both)  7.5 us
    pallas_call x1, Pallas kernels, mirror(): call(functools.partial(w_kernel, nr, nc, near), 4, nr - 1, [whole if k in...  6.46 us
    pallas_call x1, Pallas kernels, second(): call(functools.partial(second_kernel, nr, nc, scale, places), 3, 3 + len(...  6.16 us
    pallas_call x2, Pallas kernels, per_device(): call(functools.partial(late_kernel, nr, nc, scale, places), 3, 3 + len(pl...  5.94 us
  transfers between devices with their start and end apart: 30, of which 17 were waited for; matrix products, arithmetic and copies ran while one was open for 3% of the time, Pallas kernels for 25%

profile of v2, /device:TPU:0, one launch (start us, length us, event | category | flops | bytes accessed | tf_op | source)
XLA Modules:
  0.0 114.4 jit_solution(257931641741948411)
XLA Ops:
  0.6 3.0 %collective-permute-start.1 = (f32[384,256]{1,0:T(8,128)}, f32[384,256]{1,0:T(8,128)S(1)}, u32[]{:S(2)}, u32[]{:S(2)}) collective-permute-start(f32[384,256]{1,0:T(8,128)} %refs_8_.1), channel_id=1, source_target_pairs={{0,16},{8,24},{16,0},{24,8},{1,17},{9,25},{17,1},{25,9},{2,18},{10... | collective-permute-start | bytes 1179656 | tf_op jit(solution)/shard_map/ppermute | solution.py:251
  3.6 1.6 %collective-permute-start.3 = (f32[384,256]{1,0:T(8,128)}, f32[384,256]{1,0:T(8,128)S(1)}, u32[]{:S(2)}, u32[]{:S(2)}) collective-permute-start(f32[384,256]{1,0:T(8,128)} %refs_8_.1), channel_id=1, source_target_pairs={{0,2},{2,4},{4,6},{6,7},{7,5},{5,3},{3,1},{1,0},{8,10},{10,12},{12... | collective-permute-start | bytes 1179656 | tf_op jit(solution)/shard_map/ppermute | solution.py:230
  5.7 7.3 %collective-permute-done.1.refs_1_.refs_10_ = f32[384,256]{1,0:T(8,128)S(1)} collective-permute-done((f32[384,256]{1,0:T(8,128)}, f32[384,256]{1,0:T(8,128)S(1)}, u32[]{:S(2)}, u32[]{:S(2)}) %collective-permute-start.1) | collective-permute-done | bytes 393248 | tf_op jit(solution)/shard_map/ppermute | solution.py:251
  13.0 1.5 %collective-permute-done.3.refs_1_ = f32[384,256]{1,0:T(8,128)S(1)} collective-permute-done((f32[384,256]{1,0:T(8,128)}, f32[384,256]{1,0:T(8,128)S(1)}, u32[]{:S(2)}, u32[]{:S(2)}) %collective-permute-start.3) | collective-permute-done | bytes 393248 | tf_op jit(solution)/shard_map/ppermute | solution.py:230
  14.4 1.6 %collective-permute-start.4 = (f32[384,256]{1,0:T(8,128)S(1)}, f32[384,256]{1,0:T(8,128)S(1)}, u32[]{:S(2)}, u32[]{:S(2)}) collective-permute-start(f32[384,256]{1,0:T(8,128)S(1)} %collective-permute-done.3.refs_1_), channel_id=1, source_target_pairs={{0,2},{2,4},{4,6},{6,7},{7,5},{5,3},{3,1},{1,0},{8,10},{10,12},{12... | collective-permute-start | bytes 1179656 | tf_op jit(solution)/shard_map/ppermute | solution.py:230
  16.5 6.5 %shard_map.77 = (f32[384,256]{1,0:T(8,128)}, f32[384,256]{1,0:T(8,128)}, f32[384,256]{1,0:T(8,128)}, f32[384,256]{1,0:T(8,128)}, f32[384,256]{1,0:T(8,128)}, /*i...) custom-call(s32[1,1,15]{2,1,0:T(1,128)} %rows_in.11, ...), custom_call_target="tpu_custom_call" | custom-call | flops 2264924160 | bytes 20000000 | tf_op jit(solution)/shard_map/pallas_call | solution.py:306
  22.9 1.9 %copy-done = f32[15,256,256]{2,1,0:T(8,128)} copy-done((f32[15,256,256]{2,1,0:T(8,128)}, f32[15,256,256]{2,1,0:T(8,128)S(1)}, u32[]{:S(2)}) %copy-start) | copy-done | bytes 3932184
  24.9 1.6 %collective-permute-start.13 = (f32[384,256]{1,0:T(8,128)}, f32[384,256]{1,0:T(8,128)}, u32[]{:S(2)}, u32[]{:S(2)}) collective-permute-start(f32[384,256]{1,0:T(8,128)} %get-tuple-element.45), channel_id=1, source_target_pairs={{0,2},{2,4},{4,6},{6,7},{7,5},{5,3},{3,1},{1,0},{10,8},{12,10},{14... | collective-permute-start | bytes 1179656 | tf_op jit(solution)/shard_map/ppermute | solution.py:237
  26.4 1.6 %collective-permute-start.5 = (f32[384,256]{1,0:T(8,128)S(1)}, f32[384,256]{1,0:T(8,128)S(1)}, u32[]{:S(2)}, u32[]{:S(2)}) collective-permute-start(f32[384,256]{1,0:T(8,128)S(1)} %collective-permute-done.4.refs_2_), channel_id=1, source_target_pairs={{0,2},{2,4},{4,6},{6,7},{7,5},{5,3},{3,1},{1,0},{8,10},{10,12},{12... | collective-permute-start | bytes 1179656 | tf_op jit(solution)/shard_map/ppermute | solution.py:230
  28.5 7.5 %collective-permute-done.13 = f32[384,256]{1,0:T(8,128)} collective-permute-done((f32[384,256]{1,0:T(8,128)}, f32[384,256]{1,0:T(8,128)}, u32[]{:S(2)}, u32[]{:S(2)}) %collective-permute-start.13) | collective-permute-done | bytes 393248 | tf_op jit(solution)/shard_map/ppermute | solution.py:237
  37.3 1.6 %collective-permute-start.17 = (f32[384,256]{1,0:T(8,128)S(1)}, f32[384,256]{1,0:T(8,128)S(1)}, u32[]{:S(2)}, u32[]{:S(2)}) collective-permute-start(f32[384,256]{1,0:T(8,128)S(1)} %get-tuple-element.67), channel_id=1, source_target_pairs={{2,0},{4,2},{6,4},{7,6},{5,7},{3,5},{1,3},{0,1},{10,8},{12,10},{14... | collective-permute-start | bytes 1179656 | tf_op jit(solution)/shard_map/ppermute | solution.py:242
  39.4 3.9 %collective-permute-done.5.refs_3_ = f32[384,256]{1,0:T(8,128)S(1)} collective-permute-done((f32[384,256]{1,0:T(8,128)S(1)}, f32[384,256]{1,0:T(8,128)S(1)}, u32[]{:S(2)}, u32[]{:S(2)}) %collective-permute-start.5) | collective-permute-done | bytes 393248 | tf_op jit(solution)/shard_map/ppermute | solution.py:230
  44.5 4.8 %collective-permute-done.17 = f32[384,256]{1,0:T(8,128)S(1)} collective-permute-done((f32[384,256]{1,0:T(8,128)S(1)}, f32[384,256]{1,0:T(8,128)S(1)}, u32[]{:S(2)}, u32[]{:S(2)}) %collective-permute-start.17) | collective-permute-done | bytes 393248 | tf_op jit(solution)/shard_map/ppermute | solution.py:242
  50.4 1.6 %collective-permute-start.18 = (f32[384,256]{1,0:T(8,128)S(1)}, f32[384,256]{1,0:T(8,128)S(1)}, u32[]{:S(2)}, u32[]{:S(2)}) collective-permute-start(f32[384,256]{1,0:T(8,128)S(1)} %add.50), channel_id=1, source_target_pairs={{2,0},{4,2},{6,4},{7,6},{5,7},{3,5},{1,3},{0,1},{10,8},{12,10},{14... | collective-permute-start | bytes 1179656 | tf_op jit(solution)/shard_map/ppermute | solution.py:242
  53.7 5.0 %shard_map.78 = (f32[384,256]{1,0:T(8,128)S(1)}, f32[384,256]{1,0:T(8,128)S(1)}, f32[384,256]{1,0:T(8,128)S(1)}, f32[384,256]{1,0:T(8,128)S(1)}) custom-call(s32[1,1,15]{2,1,0:T(1,128)} %rows_in.11, s32[1,1,15]{2,1,0:T(1,128)} %cols_in.11, f32[256,256]{1,0:T(8,128)} %d_in.3, f32[15,256,256]{2,1,0:T(8,128)S(1)} %copy-done.1, f32[384,256]{1,0:T(8,128)S(1)} %copy-done.2, ...), custom_call_target="tpu_custom_call" | custom-call | flops 2264924160 | bytes 20000000 | tf_op jit(solution)/shard_map/pallas_call | solution.py:321
  60.0 1.7 %collective-permute-start.19 = (f32[384,256]{1,0:T(8,128)S(1)}, f32[384,256]{1,0:T(8,128)S(1)}, u32[]{:S(2)}, u32[]{:S(2)}) collective-permute-start(f32[384,256]{1,0:T(8,128)S(1)} %add.51), channel_id=1, source_target_pairs={{2,0},{4,2},{6,4},{7,6},{5,7},{3,5},{1,3},{0,1},{10,8},{12,10},{14... | collective-permute-start | bytes 1179656 | tf_op jit(solution)/shard_map/ppermute | solution.py:242
  62.3 1.7 %collective-permute-start.11 = (f32[384,256]{1,0:T(8,128)S(1)}, f32[384,256]{1,0:T(8,128)S(1)}, u32[]{:S(2)}, u32[]{:S(2)}) collective-permute-start(f32[384,256]{1,0:T(8,128)S(1)} %add.41), channel_id=1, source_target_pairs={{0,16},{8,24},{16,0},{24,8},{1,17},{9,25},{17,1},{25,9},{2,18},{10... | collective-permute-start | bytes 1179656 | tf_op jit(solution)/shard_map/ppermute | solution.py:258
  64.0 2.2 %shard_map.79 = (bf16[8,256,384]{2,1,0:T(8,128)(2,1)S(1)}, bf16[8,256,384]{2,1,0:T(8,128)(2,1)S(1)}, bf16[4,384,256]{2,1,0:T(8,128)(2,1)S(1)}, bf16[4,384,256]{2,1,0:T(8,128)(2,1)S(1)}) custom-call(f32[384,256]{1,0:T(8,128)S(1)} %copy-done.2, f32[384,256]{1,0:T(8,128)S(1)} %collective-permute-done.3.refs_1_, f32[384,256]{1,0:T(8,128)S(1)} %collective-permute-done.4.refs_2_, ...), custom_call_target="tpu_custom_call" | custom-call | flops 2264924160 | bytes 20000000 | tf_op jit(solution)/shard_map/pallas_call | solution.py:331
  66.2 4.3 %collective-permute-done.19 = f32[384,256]{1,0:T(8,128)S(1)} collective-permute-done((f32[384,256]{1,0:T(8,128)S(1)}, f32[384,256]{1,0:T(8,128)S(1)}, u32[]{:S(2)}, u32[]{:S(2)}) %collective-permute-start.19) | collective-permute-done | bytes 393248 | tf_op jit(solution)/shard_map/ppermute | solution.py:242
  70.5 1.4 %collective-permute-done.16 = f32[384,256]{1,0:T(8,128)S(1)} collective-permute-done((f32[384,256]{1,0:T(8,128)S(1)}, f32[384,256]{1,0:T(8,128)S(1)}, u32[]{:S(2)}, u32[]{:S(2)}) %collective-permute-start.16) | collective-permute-done | bytes 393248 | tf_op jit(solution)/shard_map/ppermute | solution.py:241
  72.4 1.6 %collective-permute-start.21 = (f32[384,256]{1,0:T(8,128)S(1)}, f32[384,256]{1,0:T(8,128)S(1)}, u32[]{:S(2)}, u32[]{:S(2)}) collective-permute-start(f32[384,256]{1,0:T(8,128)S(1)} %add_add_fusion.refs_0_), channel_id=1, source_target_pairs={{0,16},{8,24},{16,0},{24,8},{1,17},{9,25},{17,1},{25,9},{2,18},{10... | collective-permute-start | bytes 1179656 | tf_op jit(solution)/shard_map/ppermute | solution.py:251
  76.0 5.4 %collective-permute-done.21.refs_2_ = f32[384,256]{1,0:T(8,128)S(1)} collective-permute-done((f32[384,256]{1,0:T(8,128)S(1)}, f32[384,256]{1,0:T(8,128)S(1)}, u32[]{:S(2)}, u32[]{:S(2)}) %collective-permute-start.21) | collective-permute-done | bytes 393248 | tf_op jit(solution)/shard_map/ppermute | solution.py:251
  83.1 1.5 %collective-permute-start.26 = (f32[384,256]{1,0:T(8,128)S(1)}, f32[384,256]{1,0:T(8,128)S(1)}, u32[]{:S(2)}, u32[]{:S(2)}) collective-permute-start(f32[384,256]{1,0:T(8,128)S(1)} %collective-permute-done.24.refs_2_), channel_id=1, source_target_pairs={{2,0},{4,2},{6,4},{7,6},{5,7},{3,5},{1,3},{0,1},{10,8},{12,10},{14... | collective-permute-start | bytes 1179656 | tf_op jit(solution)/shard_map/ppermute | solution.py:231
  84.6 5.0 %shard_map.80 = (f32[15,256,256]{2,1,0:T(8,128)S(1)}, f32[256,256]{1,0:T(8,128)}) custom-call(s32[1,1,15]{2,1,0:T(1,128)} %rows_in.11, s32[1,1,15]{2,1,0:T(1,128)} %cols_in.11, s32[1,1,15]{2,1,0:T(1,128)} %live_in.7, f32[256,256]{1,0:T(8,128)} %d_in.3, f32[15,256,256]{2,1,0:T(8,128)S(1)} %copy-done.1, bf16[8,256,384]{2,1,0:T(8,128)(2,1)S(1)} %get-tuple-element.53.th, ...), custom_call_target="tpu_custom_call" | custom-call | flops 2264924160 | bytes 20000000 | tf_op jit(solution)/shard_map/pallas_call | solution.py:346
  89.6 3.4 %collective-permute-done.25.refs_3_ = f32[384,256]{1,0:T(8,128)S(1)} collective-permute-done((f32[384,256]{1,0:T(8,128)S(1)}, f32[384,256]{1,0:T(8,128)S(1)}, u32[]{:S(2)}, u32[]{:S(2)}) %collective-permute-start.25) | collective-permute-done | bytes 393248 | tf_op jit(solution)/shard_map/ppermute | solution.py:230
  93.2 1.5 %collective-permute-start.27 = (f32[384,256]{1,0:T(8,128)S(1)}, f32[384,256]{1,0:T(8,128)S(1)}, u32[]{:S(2)}, u32[]{:S(2)}) collective-permute-start(f32[384,256]{1,0:T(8,128)S(1)} %collective-permute-done.25.refs_3_), channel_id=1, source_target_pairs={{0,2},{2,4},{4,6},{6,7},{7,5},{5,3},{3,1},{1,0},{8,10},{10,12},{12... | collective-permute-start | bytes 1179656 | tf_op jit(solution)/shard_map/ppermute | solution.py:230
  95.2 6.2 %shard_map.81 = (f32[1,1,15,256,256]{4,3,2,1,0:T(8,128)}, f32[15,256,256]{2,1,0:T(8,128)S(1)}) custom-call(s32[1,1,15]{2,1,0:T(1,128)} %rows_in.11, s32[1,1,15]{2,1,0:T(1,128)} %cols_in.11, s32[1,1,15]{2,1,0:T(1,128)} %live_in.7, f32[15,256,256]{2,1,0:T(8,128)S(1)} %get-tuple-element.56.v_ref, bf16[4,384,256]{2,1,0:T(8,128)(2,1)S(1)} %get-tuple-element.57.rh, ...), custom_call_target="tpu_custom_call" | custom-call | flops 2264924160 | bytes 20000000 | tf_op jit(solution)/shard_map/pallas_call | solution.py:361
  102.5 1.4 %collective-permute-done.28.refs_1_ = f32[384,256]{1,0:T(8,128)S(1)} collective-permute-done((f32[384,256]{1,0:T(8,128)S(1)}, f32[384,256]{1,0:T(8,128)S(1)}, u32[]{:S(2)}, u32[]{:S(2)}) %collective-permute-start.28) | collective-permute-done | bytes 393248 | tf_op jit(solution)/shard_map/ppermute | solution.py:231
  103.9 1.5 %collective-permute-start.29 = (f32[384,256]{1,0:T(8,128)S(1)}, f32[384,256]{1,0:T(8,128)S(1)}, u32[]{:S(2)}, u32[]{:S(2)}) collective-permute-start(f32[384,256]{1,0:T(8,128)S(1)} %broadcast_select_fusion), channel_id=1, source_target_pairs={{0,2},{2,4},{4,6},{6,7},{7,5},{5,3},{3,1},{1,0},{10,8},{12,10},{14... | collective-permute-start | bytes 1179656 | tf_op jit(solution)/shard_map/ppermute | solution.py:233
  105.5 3.5 %shard_map.82.refs_1_ = f32[1,1,15,256,256]{4,3,2,1,0:T(8,128)} custom-call(s32[1,1,15]{2,1,0:T(1,128)} %rows_in.11, s32[1,1,15]{2,1,0:T(1,128)} %cols_in.11, s32[1,1,15]{2,1,0:T(1,128)} %live_in.7, f32[15,256,256]{2,1,0:T(8,128)S(1)} %get-tuple-element.59.v_ref, bf16[4,384,256]{2,1,0:T(8,128)(2,1)S(1)} %get-tuple-element.57.rh, ...), custom_call_target="tpu_custom_call", output_to_operand_aliasing={{}: (8, {})} | custom-call | flops 2264924160 | bytes 20000000 | tf_op jit(solution)/shard_map/pallas_call | solution.py:377
  109.0 2.8 %collective-permute-done.29.refs_0_ = f32[384,256]{1,0:T(8,128)S(1)} collective-permute-done((f32[384,256]{1,0:T(8,128)S(1)}, f32[384,256]{1,0:T(8,128)S(1)}, u32[]{:S(2)}, u32[]{:S(2)}) %collective-permute-start.29) | collective-permute-done | bytes 393248 | tf_op jit(solution)/shard_map/ppermute | solution.py:233
  111.8 2.5 %shard_map.83 = f32[1,1,15,256,256]{4,3,2,1,0:T(8,128)} custom-call(s32[1,1,15]{2,1,0:T(1,128)} %rows_in.11, s32[1,1,15]{2,1,0:T(1,128)} %cols_in.11, s32[1,1,15]{2,1,0:T(1,128)} %live_in.7, f32[15,256,256]{2,1,0:T(8,128)S(1)} %get-tuple-element.59.v_ref, bf16[4,384,256]{2,1,0:T(8,128)(2,1)S(1)} %get-tuple-element.57.rh, ...), custom_call_target="tpu_custom_call", output_to_operand_aliasing={{}: (7, {})} | custom-call | flops 2264924160 | bytes 20000000 | tf_op jit(solution)/shard_map/pallas_call | solution.py:377
  (56 shorter events, 14.9 us)
Async XLA Ops:
  0.6 12.3 %collective-permute-start.1 = (f32[384,256]{1,0:T(8,128)}, f32[384,256]{1,0:T(8,128)S(1)}, u32[]{:S(2)}, u32[]{:S(2)}) collective-permute-start(f32[384,256]{1,0:T(8,128)} %refs_8_.1), channel_id=1, source_target_pairs={{0,16},{8,24},{16,0},{24,8},{1,17},{9,25},{17,1},{25,9},{2,18},{10... | collective-permute-start | bytes 1179656 | tf_op jit(solution)/shard_map/ppermute | solution.py:251
  3.6 10.8 %collective-permute-start.3 = (f32[384,256]{1,0:T(8,128)}, f32[384,256]{1,0:T(8,128)S(1)}, u32[]{:S(2)}, u32[]{:S(2)}) collective-permute-start(f32[384,256]{1,0:T(8,128)} %refs_8_.1), channel_id=1, source_target_pairs={{0,2},{2,4},{4,6},{6,7},{7,5},{5,3},{3,1},{1,0},{8,10},{10,12},{12... | collective-permute-start | bytes 1179656 | tf_op jit(solution)/shard_map/ppermute | solution.py:230
  5.2 10.8 %collective-permute-start.6 = (f32[384,256]{1,0:T(8,128)}, f32[384,256]{1,0:T(8,128)S(1)}, u32[]{:S(2)}, u32[]{:S(2)}) collective-permute-start(f32[384,256]{1,0:T(8,128)} %refs_8_.1), channel_id=1, source_target_pairs={{2,0},{4,2},{6,4},{7,6},{5,7},{3,5},{1,3},{0,1},{10,8},{12,10},{14... | collective-permute-start | bytes 1179656 | tf_op jit(solution)/shard_map/ppermute | solution.py:231
  5.7 10.8 %collective-permute-start = (f32[384,256]{1,0:T(8,128)}, f32[384,256]{1,0:T(8,128)S(1)}, u32[]{:S(2)}, u32[]{:S(2)}) collective-permute-start(f32[384,256]{1,0:T(8,128)} %refs_8_.1), channel_id=1, source_target_pairs={{0,8},{8,0},{16,24},{24,16},{1,9},{9,1},{17,25},{25,17},{2,10},{10... | collective-permute-start | bytes 1179656 | tf_op jit(solution)/shard_map/ppermute | solution.py:252
  13.0 3.5 %collective-permute-start.2 = (f32[384,256]{1,0:T(8,128)S(1)}, f32[384,256]{1,0:T(8,128)S(1)}, u32[]{:S(2)}, u32[]{:S(2)}) collective-permute-start(f32[384,256]{1,0:T(8,128)S(1)} %collective-permute-done.1.refs_1_.refs_10_), channel_id=1, source_target_pairs={{0,8},{8,0},{16,24},{24,16},{1,9},{9,1},{17,25},{25,17},{2,10},{10... | collective-permute-start | bytes 1179656 | tf_op jit(solution)/shard_map/ppermute | solution.py:252
  14.4 12.0 %collective-permute-start.4 = (f32[384,256]{1,0:T(8,128)S(1)}, f32[384,256]{1,0:T(8,128)S(1)}, u32[]{:S(2)}, u32[]{:S(2)}) collective-permute-start(f32[384,256]{1,0:T(8,128)S(1)} %collective-permute-done.3.refs_1_), channel_id=1, source_target_pairs={{0,2},{2,4},{4,6},{6,7},{7,5},{5,3},{3,1},{1,0},{8,10},{10,12},{12... | collective-permute-start | bytes 1179656 | tf_op jit(solution)/shard_map/ppermute | solution.py:230
  16.0 12.0 %collective-permute-start.7 = (f32[384,256]{1,0:T(8,128)S(1)}, f32[384,256]{1,0:T(8,128)}, u32[]{:S(2)}, u32[]{:S(2)}) collective-permute-start(f32[384,256]{1,0:T(8,128)S(1)} %collective-permute-done.6.refs_7_), channel_id=1, source_target_pairs={{2,0},{4,2},{6,4},{7,6},{5,7},{3,5},{1,3},{0,1},{10,8},{12,10},{14... | collective-permute-start | bytes 1179656 | tf_op jit(solution)/shard_map/ppermute | solution.py:231
  24.9 28.9 %copy-start.2 = (f32[384,256]{1,0:T(8,128)S(1)}, f32[384,256]{1,0:T(8,128)}, u32[]{:S(2)}) copy-start(f32[384,256]{1,0:T(8,128)} %refs_8_.1) | copy-start | bytes 1179652
  24.9 11.1 %collective-permute-start.13 = (f32[384,256]{1,0:T(8,128)}, f32[384,256]{1,0:T(8,128)}, u32[]{:S(2)}, u32[]{:S(2)}) collective-permute-start(f32[384,256]{1,0:T(8,128)} %get-tuple-element.45), channel_id=1, source_target_pairs={{0,2},{2,4},{4,6},{6,7},{7,5},{5,3},{3,1},{1,0},{10,8},{12,10},{14... | collective-permute-start | bytes 1179656 | tf_op jit(solution)/shard_map/ppermute | solution.py:237
  26.4 16.8 %collective-permute-start.5 = (f32[384,256]{1,0:T(8,128)S(1)}, f32[384,256]{1,0:T(8,128)S(1)}, u32[]{:S(2)}, u32[]{:S(2)}) collective-permute-start(f32[384,256]{1,0:T(8,128)S(1)} %collective-permute-done.4.refs_2_), channel_id=1, source_target_pairs={{0,2},{2,4},{4,6},{6,7},{7,5},{5,3},{3,1},{1,0},{8,10},{10,12},{12... | collective-permute-start | bytes 1179656 | tf_op jit(solution)/shard_map/ppermute | solution.py:230
  28.0 15.3 %collective-permute-start.8 = (f32[384,256]{1,0:T(8,128)}, f32[384,256]{1,0:T(8,128)S(1)}, u32[]{:S(2)}, u32[]{:S(2)}) collective-permute-start(f32[384,256]{1,0:T(8,128)} %collective-permute-done.7.refs_6_), channel_id=1, source_target_pairs={{2,0},{4,2},{6,4},{7,6},{5,7},{3,5},{1,3},{0,1},{10,8},{12,10},{14... | collective-permute-start | bytes 1179656 | tf_op jit(solution)/shard_map/ppermute | solution.py:231
  28.5 25.3 %copy-start.1 = (f32[15,256,256]{2,1,0:T(8,128)S(1)}, f32[15,256,256]{2,1,0:T(8,128)}, u32[]{:S(2)}) copy-start(f32[15,256,256]{2,1,0:T(8,128)} %copy-done) | copy-start | bytes 11796484
  37.3 12.1 %collective-permute-start.17 = (f32[384,256]{1,0:T(8,128)S(1)}, f32[384,256]{1,0:T(8,128)S(1)}, u32[]{:S(2)}, u32[]{:S(2)}) collective-permute-start(f32[384,256]{1,0:T(8,128)S(1)} %get-tuple-element.67), channel_id=1, source_target_pairs={{2,0},{4,2},{6,4},{7,6},{5,7},{3,5},{1,3},{0,1},{10,8},{12,10},{14... | collective-permute-start | bytes 1179656 | tf_op jit(solution)/shard_map/ppermute | solution.py:242
  38.9 13.2 %collective-permute-start.14 = (f32[384,256]{1,0:T(8,128)S(1)}, f32[384,256]{1,0:T(8,128)S(1)}, u32[]{:S(2)}, u32[]{:S(2)}) collective-permute-start(f32[384,256]{1,0:T(8,128)S(1)} %get-tuple-element.66), channel_id=1, source_target_pairs={{0,2},{2,4},{4,6},{6,7},{7,5},{5,3},{3,1},{1,0},{8,10},{10,12},{12... | collective-permute-start | bytes 1179656 | tf_op jit(solution)/shard_map/ppermute | solution.py:241
  43.3 10.4 %collective-permute-start.9 = (f32[384,256]{1,0:T(8,128)S(1)}, f32[384,256]{1,0:T(8,128)S(1)}, u32[]{:S(2)}, u32[]{:S(2)}) collective-permute-start(f32[384,256]{1,0:T(8,128)S(1)} %broadcast_select_fusion.1), channel_id=1, source_target_pairs={{0,2},{2,4},{4,6},{6,7},{7,5},{5,3},{3,1},{1,0},{10,8},{12,10},{14... | collective-permute-start | bytes 1179656 | tf_op jit(solution)/shard_map/ppermute | solution.py:233
  50.4 9.5 %collective-permute-start.18 = (f32[384,256]{1,0:T(8,128)S(1)}, f32[384,256]{1,0:T(8,128)S(1)}, u32[]{:S(2)}, u32[]{:S(2)}) collective-permute-start(f32[384,256]{1,0:T(8,128)S(1)} %add.50), channel_id=1, source_target_pairs={{2,0},{4,2},{6,4},{7,6},{5,7},{3,5},{1,3},{0,1},{10,8},{12,10},{14... | collective-permute-start | bytes 1179656 | tf_op jit(solution)/shard_map/ppermute | solution.py:242
  53.1 8.6 %collective-permute-start.15 = (f32[384,256]{1,0:T(8,128)S(1)}, f32[384,256]{1,0:T(8,128)S(1)}, u32[]{:S(2)}, u32[]{:S(2)}) collective-permute-start(f32[384,256]{1,0:T(8,128)S(1)} %add.46), channel_id=1, source_target_pairs={{0,2},{2,4},{4,6},{6,7},{7,5},{5,3},{3,1},{1,0},{8,10},{10,12},{12... | collective-permute-start | bytes 1179656 | tf_op jit(solution)/shard_map/ppermute | solution.py:241
  58.7 3.5 %collective-permute-start.10 = (f32[384,256]{1,0:T(8,128)S(1)}, f32[384,256]{1,0:T(8,128)S(1)}, u32[]{:S(2)}, u32[]{:S(2)}) collective-permute-start(f32[384,256]{1,0:T(8,128)S(1)} %get-tuple-element.39), channel_id=1, source_target_pairs={{0,8},{8,0},{16,24},{24,16},{1,9},{9,1},{17,25},{25,17},{2,10},{10... | collective-permute-start | bytes 1179656 | tf_op jit(solution)/shard_map/ppermute | solution.py:255
  58.8 7.4 %collective-permute-start.12 = (f32[384,256]{1,0:T(8,128)S(1)}, f32[384,256]{1,0:T(8,128)S(1)}, u32[]{:S(2)}, u32[]{:S(2)}) collective-permute-start(f32[384,256]{1,0:T(8,128)S(1)} %get-tuple-element.41), channel_id=1, source_target_pairs={{0,8},{8,0},{16,24},{24,16},{1,9},{9,1},{17,25},{25,17},{2,10},{10... | collective-permute-start | bytes 1179656 | tf_op jit(solution)/shard_map/ppermute | solution.py:255
  60.0 10.5 %collective-permute-start.19 = (f32[384,256]{1,0:T(8,128)S(1)}, f32[384,256]{1,0:T(8,128)S(1)}, u32[]{:S(2)}, u32[]{:S(2)}) collective-permute-start(f32[384,256]{1,0:T(8,128)S(1)} %add.51), channel_id=1, source_target_pairs={{2,0},{4,2},{6,4},{7,6},{5,7},{3,5},{1,3},{0,1},{10,8},{12,10},{14... | collective-permute-start | bytes 1179656 | tf_op jit(solution)/shard_map/ppermute | solution.py:242
  61.8 10.1 %collective-permute-start.16 = (f32[384,256]{1,0:T(8,128)S(1)}, f32[384,256]{1,0:T(8,128)S(1)}, u32[]{:S(2)}, u32[]{:S(2)}) collective-permute-start(f32[384,256]{1,0:T(8,128)S(1)} %add.47), channel_id=1, source_target_pairs={{0,2},{2,4},{4,6},{6,7},{7,5},{5,3},{3,1},{1,0},{8,10},{10,12},{12... | collective-permute-start | bytes 1179656 | tf_op jit(solution)/shard_map/ppermute | solution.py:241
  62.3 10.0 %collective-permute-start.11 = (f32[384,256]{1,0:T(8,128)S(1)}, f32[384,256]{1,0:T(8,128)S(1)}, u32[]{:S(2)}, u32[]{:S(2)}) collective-permute-start(f32[384,256]{1,0:T(8,128)S(1)} %add.41), channel_id=1, source_target_pairs={{0,16},{8,24},{16,0},{24,8},{1,17},{9,25},{17,1},{25,9},{2,18},{10... | collective-permute-start | bytes 1179656 | tf_op jit(solution)/shard_map/ppermute | solution.py:258
  72.4 9.0 %collective-permute-start.21 = (f32[384,256]{1,0:T(8,128)S(1)}, f32[384,256]{1,0:T(8,128)S(1)}, u32[]{:S(2)}, u32[]{:S(2)}) collective-permute-start(f32[384,256]{1,0:T(8,128)S(1)} %add_add_fusion.refs_0_), channel_id=1, source_target_pairs={{0,16},{8,24},{16,0},{24,8},{1,17},{9,25},{17,1},{25,9},{2,18},{10... | collective-permute-start | bytes 1179656 | tf_op jit(solution)/shard_map/ppermute | solution.py:251
  74.0 8.6 %collective-permute-start.23 = (f32[384,256]{1,0:T(8,128)S(1)}, f32[384,256]{1,0:T(8,128)S(1)}, u32[]{:S(2)}, u32[]{:S(2)}) collective-permute-start(f32[384,256]{1,0:T(8,128)S(1)} %add_add_fusion.refs_0_), channel_id=1, source_target_pairs={{0,2},{2,4},{4,6},{6,7},{7,5},{5,3},{3,1},{1,0},{8,10},{10,12},{12... | collective-permute-start | bytes 1179656 | tf_op jit(solution)/shard_map/ppermute | solution.py:230
  75.0 8.0 %collective-permute-start.24 = (f32[384,256]{1,0:T(8,128)S(1)}, f32[384,256]{1,0:T(8,128)S(1)}, u32[]{:S(2)}, u32[]{:S(2)}) collective-permute-start(f32[384,256]{1,0:T(8,128)S(1)} %add_add_fusion.refs_0_), channel_id=1, source_target_pairs={{2,0},{4,2},{6,4},{7,6},{5,7},{3,5},{1,3},{0,1},{10,8},{12,10},{14... | collective-permute-start | bytes 1179656 | tf_op jit(solution)/shard_map/ppermute | solution.py:231
  76.0 8.6 %collective-permute-start.20 = (f32[384,256]{1,0:T(8,128)S(1)}, f32[384,256]{1,0:T(8,128)S(1)}, u32[]{:S(2)}, u32[]{:S(2)}) collective-permute-start(f32[384,256]{1,0:T(8,128)S(1)} %add_add_fusion.refs_0_), channel_id=1, source_target_pairs={{0,8},{8,0},{16,24},{24,16},{1,9},{9,1},{17,25},{25,17},{2,10},{10... | collective-permute-start | bytes 1179656 | tf_op jit(solution)/shard_map/ppermute | solution.py:252
  81.4 3.1 %collective-permute-start.22 = (f32[384,256]{1,0:T(8,128)S(1)}, f32[384,256]{1,0:T(8,128)S(1)}, u32[]{:S(2)}, u32[]{:S(2)}) collective-permute-start(f32[384,256]{1,0:T(8,128)S(1)} %collective-permute-done.21.refs_2_), channel_id=1, source_target_pairs={{0,8},{8,0},{16,24},{24,16},{1,9},{9,1},{17,25},{25,17},{2,10},{10... | collective-permute-start | bytes 1179656 | tf_op jit(solution)/shard_map/ppermute | solution.py:252
  82.5 10.4 %collective-permute-start.25 = (f32[384,256]{1,0:T(8,128)S(1)}, f32[384,256]{1,0:T(8,128)S(1)}, u32[]{:S(2)}, u32[]{:S(2)}) collective-permute-start(f32[384,256]{1,0:T(8,128)S(1)} %collective-permute-done.23.refs_1_), channel_id=1, source_target_pairs={{0,2},{2,4},{4,6},{6,7},{7,5},{5,3},{3,1},{1,0},{8,10},{10,12},{12... | collective-permute-start | bytes 1179656 | tf_op jit(solution)/shard_map/ppermute | solution.py:230
  83.1 10.1 %collective-permute-start.26 = (f32[384,256]{1,0:T(8,128)S(1)}, f32[384,256]{1,0:T(8,128)S(1)}, u32[]{:S(2)}, u32[]{:S(2)}) collective-permute-start(f32[384,256]{1,0:T(8,128)S(1)} %collective-permute-done.24.refs_2_), channel_id=1, source_target_pairs={{2,0},{4,2},{6,4},{7,6},{5,7},{3,5},{1,3},{0,1},{10,8},{12,10},{14... | collective-permute-start | bytes 1179656 | tf_op jit(solution)/shard_map/ppermute | solution.py:231
  93.2 9.3 %collective-permute-start.27 = (f32[384,256]{1,0:T(8,128)S(1)}, f32[384,256]{1,0:T(8,128)S(1)}, u32[]{:S(2)}, u32[]{:S(2)}) collective-permute-start(f32[384,256]{1,0:T(8,128)S(1)} %collective-permute-done.25.refs_3_), channel_id=1, source_target_pairs={{0,2},{2,4},{4,6},{6,7},{7,5},{5,3},{3,1},{1,0},{8,10},{10,12},{12... | collective-permute-start | bytes 1179656 | tf_op jit(solution)/shard_map/ppermute | solution.py:230
  94.7 9.1 %collective-permute-start.28 = (f32[384,256]{1,0:T(8,128)S(1)}, f32[384,256]{1,0:T(8,128)S(1)}, u32[]{:S(2)}, u32[]{:S(2)}) collective-permute-start(f32[384,256]{1,0:T(8,128)S(1)} %collective-permute-done.26.refs_4_), channel_id=1, source_target_pairs={{2,0},{4,2},{6,4},{7,6},{5,7},{3,5},{1,3},{0,1},{10,8},{12,10},{14... | collective-permute-start | bytes 1179656 | tf_op jit(solution)/shard_map/ppermute | solution.py:231
  103.9 7.8 %collective-permute-start.29 = (f32[384,256]{1,0:T(8,128)S(1)}, f32[384,256]{1,0:T(8,128)S(1)}, u32[]{:S(2)}, u32[]{:S(2)}) collective-permute-start(f32[384,256]{1,0:T(8,128)S(1)} %broadcast_select_fusion), channel_id=1, source_target_pairs={{0,2},{2,4},{4,6},{6,7},{7,5},{5,3},{3,1},{1,0},{10,8},{12,10},{14... | collective-permute-start | bytes 1179656 | tf_op jit(solution)/shard_map/ppermute | solution.py:233
  (4 other events, 26.2 us)

commit v3 on v2

--- a/solution.py
+++ b/solution.py
@@ -75,7 +75,7 @@
 
 def w_kernel(nr, nc, near, rows_in, cols_in, own_in, t_in, *refs):
     x_refs, out_refs, refs = refs[: nr - 1], refs[nr - 1 : nr - 1 + nc], refs[nr - 1 + nc :]
-    t_ref, rows, cols, own, sems, t_sems, out_sems, xh, xl, acc = refs
+    rows, cols, own, t_ref, sems, t_sems, out_sems, xh, xl, acc = refs
     small = fetch((own_in, rows_in, cols_in), (own, rows, cols), sems)
     groups = []
     for k in range(t_ref.shape[0] // GROUP):
@@ -128,9 +128,26 @@
     fill(r_refs, rh, rl)
 
 
-def first_kernel(nr, nc, scale, rows_in, cols_in, live_in, d_in, t_ref, th, tl, *refs):
+def first_kernel(nr, nc, scale, places, rows_in, cols_in, live_in, t_ref, rh, rl, *refs):
+    z_refs, refs = refs[: len(places)], refs[len(places) :]
+    out_ref, rows, cols, live, sems, zh, zl = refs
+    small = fetch((rows_in, cols_in, live_in), (rows, cols, live), sems)
+    fill_turned(z_refs, zh, zl)
+    for copy in small:
+        copy.wait()
+    for slot in range(t_ref.shape[0]):
+        place = behind(rows[slot], nc)
+        i = sum(jnp.where(place == p, k, 0) for k, p in enumerate(places))
+        mine = functools.reduce(jnp.logical_or, [place == p for p in places])
+        j = row_slot(cols[slot], nr, 1)
+        gradient = dot3((zh[i], zl[i]), (rh[j], rl[j]), NN)
+        step = jnp.where(jnp.logical_and(live[slot] > 0, mine), STEP_SIZE * scale, 0.0)
+        out_ref[slot] = t_ref[slot] - step * gradient
+
+
+def second_kernel(nr, nc, scale, places, rows_in, cols_in, live_in, d_in, v_ref, th, tl, *refs):
     z_refs, refs = refs[:nr], refs[nr:]
-    out_ref, dout_ref, rows, cols, live, d_ref, sems, zh, zl = refs
+    out_ref, made, dout_ref, rows, cols, live, d_ref, sems, zh, zl, out_sems = refs
     small = fetch((rows_in, cols_in, live_in, d_in), (rows, cols, live, d_ref), sems)
     fill(z_refs, zh, zl)
     for copy in small:
@@ -143,31 +160,16 @@
     gradient = gradient - jnp.where(on_diagonal, 1.0 / jnp.where(on_diagonal, tile, 1.0), 0.0)
     value = tile - STEP_SIZE * gradient
     dout_ref[...] = jnp.where(on_diagonal, value, shrink(value, STEP_SIZE * PENALTY))
-    for slot in range(t_ref.shape[0]):
+    copies, mine = [], []
+    for slot in range(v_ref.shape[0]):
         j = row_slot(cols[slot], nr, 1)
         i = behind(rows[slot], nc)
+        mine.append(functools.reduce(jnp.logical_or, [i == p for p in places]))
+        copies.append(pltpu.make_async_copy(made.at[slot], out_ref.at[0, 0, slot], out_sems.at[slot]))
         gradient = dot3((th[i], tl[i]), (zh[j], zl[j]), NN)
-        out_ref[slot] = t_ref[slot] - jnp.where(live[slot] > 0, STEP_SIZE * scale, 0.0) * gradient
-
-
-def second_kernel(nr, nc, scale, places, rows_in, cols_in, live_in, v_ref, rh, rl, *refs):
-    z_refs, refs = refs[: len(places)], refs[len(places) :]
-    out_ref, made, rows, cols, live, sems, zh, zl, out_sems = refs
-    small = fetch((rows_in, cols_in, live_in), (rows, cols, live), sems)
-    fill_turned(z_refs, zh, zl)
-    for copy in small:
-        copy.wait()
-    copies, mine = [], []
-    for slot in range(v_ref.shape[0]):
-        place = behind(rows[slot], nc)
-        i = sum(jnp.where(place == p, k, 0) for k, p in enumerate(places))
-        mine.append(functools.reduce(jnp.logical_or, [place == p for p in places]))
-        copies.append(pltpu.make_async_copy(made.at[slot], out_ref.at[0, 0, slot], out_sems.at[slot]))
-        j = row_slot(cols[slot], nr, 1)
-        gradient = dot3((zh[i], zl[i]), (rh[j], rl[j]), NN)
-        value = v_ref[slot]
-        new = shrink(value - (STEP_SIZE * scale) * gradient, STEP_SIZE * PENALTY)
-        made[slot] = jnp.where(jnp.logical_and(live[slot] > 0, mine[slot]), new, value)
+        value = v_ref[slot] - jnp.where(live[slot] > 0, STEP_SIZE * scale, 0.0) * gradient
+        whole = jnp.logical_and(live[slot] > 0, mine[slot])
+        made[slot] = jnp.where(whole, shrink(value, STEP_SIZE * PENALTY), value)
     for slot in range(v_ref.shape[0]):
         pl.when(mine[slot])(copies[slot].start)
     for slot in range(v_ref.shape[0]):
@@ -294,6 +296,7 @@
     straight = jax.ShapeDtypeStruct((nr, count, side), BF16)
 
     in_hbm = functools.partial(pltpu.with_memory_space_constraint, memory_space=pltpu.HBM)
+    omega_tiles_raw = omega_tiles
     tile_rows, tile_cols, tile_active, omega_tiles, omega_diag = map(
         in_hbm, (tile_rows, tile_cols, tile_active, omega_tiles, omega_diag)
     )
@@ -307,16 +310,16 @@
             functools.partial(w_kernel, nr, nc, near),
             4,
             nr - 1,
-            [whole if k in near else in_place for k in range(nc)] + [whole],
-            [block if k in near else pltpu.HBM((count, side), F32) for k in range(nc)] + [tiles],
-            ids(2) + [pltpu.VMEM((count, side), F32), sems(3), sems(slots // GROUP), sems(nc)] + panel(nr) + [pltpu.VMEM((nc, count, side), F32)],
+            [whole if k in near else in_place for k in range(nc)],
+            [block if k in near else pltpu.HBM((count, side), F32) for k in range(nc)],
+            ids(2) + [pltpu.VMEM((count, side), F32), pltpu.VMEM((slots, side, side), F32), sems(3), sems(slots // GROUP), sems(nc)] + panel(nr) + [pltpu.VMEM((nc, count, side), F32)],
             10 + nc,
         )(tile_rows, tile_cols, in_hbm(samples), omega_tiles, *x_row[1:])
         w.extend(made_w)
         return w[0]
 
     x_col = ring_gather(samples, {far: mirror})
-    held = w.pop()
+    held = omega_tiles_raw[0, 0]
     w_own = ring_sum(w)
     y = call(
         functools.partial(y_kernel, nr, nc),
@@ -338,42 +341,41 @@
         8,
     )(*x_col, *x_row)
     z, th, tl, rh, rl = lax.optimization_barrier((z, th, tl, rh, rl))
-    z_row = row_gather(z)
     made = []
+    near_places, late_places, far_places = [0, 1, nc - 1], [p for d in range(2, far) for p in (d, nc - d)], [far]
 
     def first(found):
+        made.append(
+            call(
+                functools.partial(first_kernel, nr, nc, scale, near_places),
+                3,
+                3 + len(near_places),
+                whole,
+                tiles,
+                ids(3) + [sems(3)] + panel_t(len(near_places)),
+                10 + nc,
+            )(tile_rows, tile_cols, tile_active, held, rh, rl, *[found[p] for p in near_places])
+        )
+        return made[0]
+
+    def second(found):
+        z_row = row_gather(z)
         made.extend(
             call(
-                functools.partial(first_kernel, nr, nc, scale),
+                functools.partial(second_kernel, nr, nc, scale, near_places),
                 4,
                 3 + nr,
-                [whole] * 2,
-                [tiles, tile],
-                ids(3) + [pltpu.VMEM((side, side), F32), sems(4)] + panel(nr),
+                [in_place, whole, whole],
+                [jax.ShapeDtypeStruct(omega_tiles.shape, F32), tiles, tile],
+                ids(3) + [pltpu.VMEM((side, side), F32), sems(4)] + panel(nr) + [sems(slots)],
                 10 + nc,
-            )(tile_rows, tile_cols, tile_active, omega_diag, held, th, tl, *z_row)
+            )(tile_rows, tile_cols, tile_active, omega_diag, made[0], th, tl, *z_row)
         )
-        return made[0]
-
-    def second(found):
-        places = sum(steps[:-2], [])
-        made.extend(
-            call(
-                functools.partial(second_kernel, nr, nc, scale, places),
-                3,
-                3 + len(places),
-                [in_place, whole],
-                [jax.ShapeDtypeStruct(omega_tiles.shape, F32), tiles],
-                ids(3) + [sems(3)] + panel_t(len(places)) + [sems(slots)],
-                10 + nc,
-            )(tile_rows, tile_cols, tile_active, made[0], rh, rl, *[found[p] for p in places])
-        )
-        return made[-1]
-
-    steps = [[0], *[[d, nc - d] for d in range(1, far)], [far]]
+        return made[2]
+
     z_col = ring_gather(z, {far - 1: first, far: second})
-    _, new_diag, new_tiles, partial = made
-    for places in steps[-2:]:
+    _, new_tiles, partial, new_diag = made
+    for places in (late_places, far_places):
         new_tiles = call(
             functools.partial(late_kernel, nr, nc, scale, places),
             3,

time: 115 us -> 112 us (0.974)
  waiting for transfers between devices: 47.3 us -> 43.9 us
  local copies, waits for them, and re-layouts: 1.94 us -> 0.02 us
  Pallas kernels: 30.7 us -> 32.4 us
    ppermute x2, waiting for transfers between devices: 12.7 us -> 7.3 us  [row_gather(): found.append(go(found[-1], 'row', chip))]
    ppermute x6, waiting for transfers between devices: 1.65 us -> 5.49 us  [ring_gather(): found[nc - d] = go(two, 'col', left)]
    ppermute x6, starting transfers between devices: 4.29 us -> 2.05 us  [ring_gather(): found[nc - d] = go(two, 'col', left)]
    pallas_call x2, Pallas kernels: 5.94 us -> 8.14 us  [per_device(): call(functools.partial(late_kernel, nr, nc, scale, places), 3, 3 + len(pl...]
    ppermute x6, starting transfers between devices: 7.86 us -> 9.86 us  [ring_gather(): found[d] = go(one, 'col', right)]
    unnamed x12 -> x10, local copies, waits for them, and re-layouts: 1.94 us -> 0.02 us
    ppermute x3, starting transfers between devices: 1.36 us -> 3.26 us  [ring_sum(): one = go(one, 'col', right)]
    ppermute x3, starting transfers between devices: 4.98 us -> 3.07 us  [ring_sum(): two = go(two, 'col', left)]
  transfers between devices with their start and end apart: 30 -> 30, of which waited for: 17 -> 15; matrix products, arithmetic and copies ran while one was open for 3% -> 3% of each run, Pallas kernels for 25% -> 27%
where the time goes in v3:
time: 112 us; the launch traced here: 111 us
  waiting for transfers between devices  43.9 us (39%)
  Pallas kernels  32.4 us (29%)
  starting transfers between devices  30.4 us (27%)
  other arithmetic  3.81 us (3%)
    ppermute x6, waiting for transfers between devices, ring_gather(): found[d] = go(one, 'col', right)  12.1 us
    ppermute x6, starting transfers between devices, ring_gather(): found[d] = go(one, 'col', right)  9.86 us
    ppermute x3, waiting for transfers between devices, ring_sum(): two = go(two, 'col', left)  9.61 us
    pallas_call x2, Pallas kernels, per_device(): call(functools.partial(late_kernel, nr, nc, scale, places), 3, 3 + len(pl...  8.14 us
    ppermute x2, waiting for transfers between devices, row_gather(): found.append(go(found[-1], 'row', chip))  7.3 us
    pallas_call x1, Pallas kernels, mirror(): call(functools.partial(w_kernel, nr, nc, near), 4, nr - 1, [whole if k in...  6.49 us
    ppermute x1, waiting for transfers between devices, ring_sum(): first = go(parts[far], ('row', 'col'), both)  6.41 us
    pallas_call x1, Pallas kernels, second(): call(functools.partial(second_kernel, nr, nc, scale, near_places), 4, 3 +...  6.39 us
  transfers between devices with their start and end apart: 30, of which 15 were waited for; matrix products, arithmetic and copies ran while one was open for 3% of the time, Pallas kernels for 27%

profile of v3, /device:TPU:0, one launch (start us, length us, event | category | flops | bytes accessed | tf_op | source)
XLA Modules:
  0.0 111.5 jit_solution(17593358999966132505)
XLA Ops:
  0.6 3.0 %collective-permute-start.7 = (f32[384,256]{1,0:T(8,128)}, f32[384,256]{1,0:T(8,128)S(1)}, u32[]{:S(2)}, u32[]{:S(2)}) collective-permute-start(f32[384,256]{1,0:T(8,128)} %refs_8_.1), channel_id=1, source_target_pairs={{0,16},{8,24},{16,0},{24,8},{1,17},{9,25},{17,1},{25,9},{2,18},{10... | collective-permute-start | bytes 1179656 | tf_op jit(solution)/shard_map/ppermute | solution.py:253
  3.6 1.6 %collective-permute-start = (f32[384,256]{1,0:T(8,128)}, f32[384,256]{1,0:T(8,128)S(1)}, u32[]{:S(2)}, u32[]{:S(2)}) collective-permute-start(f32[384,256]{1,0:T(8,128)} %refs_8_.1), channel_id=1, source_target_pairs={{0,2},{2,4},{4,6},{6,7},{7,5},{5,3},{3,1},{1,0},{8,10},{10,12},{12... | collective-permute-start | bytes 1179656 | tf_op jit(solution)/shard_map/ppermute | solution.py:232
  5.7 7.3 %collective-permute-done.7.refs_1_.refs_10_ = f32[384,256]{1,0:T(8,128)S(1)} collective-permute-done((f32[384,256]{1,0:T(8,128)}, f32[384,256]{1,0:T(8,128)S(1)}, u32[]{:S(2)}, u32[]{:S(2)}) %collective-permute-start.7) | collective-permute-done | bytes 393248 | tf_op jit(solution)/shard_map/ppermute | solution.py:253
  13.0 1.5 %collective-permute-done.refs_1_ = f32[384,256]{1,0:T(8,128)S(1)} collective-permute-done((f32[384,256]{1,0:T(8,128)}, f32[384,256]{1,0:T(8,128)S(1)}, u32[]{:S(2)}, u32[]{:S(2)}) %collective-permute-start) | collective-permute-done | bytes 393248 | tf_op jit(solution)/shard_map/ppermute | solution.py:232
  14.4 1.6 %collective-permute-start.1 = (f32[384,256]{1,0:T(8,128)S(1)}, f32[384,256]{1,0:T(8,128)S(1)}, u32[]{:S(2)}, u32[]{:S(2)}) collective-permute-start(f32[384,256]{1,0:T(8,128)S(1)} %collective-permute-done.refs_1_), channel_id=1, source_target_pairs={{0,2},{2,4},{4,6},{6,7},{7,5},{5,3},{3,1},{1,0},{8,10},{10,12},{12... | collective-permute-start | bytes 1179656 | tf_op jit(solution)/shard_map/ppermute | solution.py:232
  16.5 6.5 %shard_map.77 = (f32[384,256]{1,0:T(8,128)}, f32[384,256]{1,0:T(8,128)}, f32[384,256]{1,0:T(8,128)}, f32[384,256]{1,0:T(8,128)}, f32[384,256]{1,0:T(8,128)}, /*i...) custom-call(s32[1,1,15]{2,1,0:T(1,128)} %rows_in.11, s32[1,1,15]{2,1,0:T(1,128)} %cols_in.11, ...), custom_call_target="tpu_custom_call" | custom-call | flops 2264924160 | bytes 20000000 | tf_op jit(solution)/shard_map/pallas_call | solution.py:309
  23.0 1.6 %collective-permute-start.13 = (f32[384,256]{1,0:T(8,128)}, f32[384,256]{1,0:T(8,128)}, u32[]{:S(2)}, u32[]{:S(2)}) collective-permute-start(f32[384,256]{1,0:T(8,128)} %get-tuple-element.42), channel_id=1, source_target_pairs={{0,2},{2,4},{4,6},{6,7},{7,5},{5,3},{3,1},{1,0},{10,8},{12,10},{14... | collective-permute-start | bytes 1179656 | tf_op jit(solution)/shard_map/ppermute | solution.py:239
  24.6 1.7 %collective-permute-start.2 = (f32[384,256]{1,0:T(8,128)S(1)}, f32[384,256]{1,0:T(8,128)S(1)}, u32[]{:S(2)}, u32[]{:S(2)}) collective-permute-start(f32[384,256]{1,0:T(8,128)S(1)} %collective-permute-done.1.refs_2_), channel_id=1, source_target_pairs={{0,2},{2,4},{4,6},{6,7},{7,5},{5,3},{3,1},{1,0},{8,10},{10,12},{12... | collective-permute-start | bytes 1179656 | tf_op jit(solution)/shard_map/ppermute | solution.py:232
  26.3 1.4 %collective-permute-done.4.refs_6_ = f32[384,256]{1,0:T(8,128)} collective-permute-done((f32[384,256]{1,0:T(8,128)S(1)}, f32[384,256]{1,0:T(8,128)}, u32[]{:S(2)}, u32[]{:S(2)}) %collective-permute-start.4) | collective-permute-done | bytes 393248 | tf_op jit(solution)/shard_map/ppermute | solution.py:233
  27.7 6.4 %collective-permute-done.13 = f32[384,256]{1,0:T(8,128)} collective-permute-done((f32[384,256]{1,0:T(8,128)}, f32[384,256]{1,0:T(8,128)}, u32[]{:S(2)}, u32[]{:S(2)}) %collective-permute-start.13) | collective-permute-done | bytes 393248 | tf_op jit(solution)/shard_map/ppermute | solution.py:239
  34.1 1.3 %add_select_fusion.1 = (f32[384,256]{1,0:T(8,128)S(1)}, f32[384,256]{1,0:T(8,128)S(1)}) fusion(f32[384,256]{1,0:T(8,128)} %get-tuple-element.41, f32[384,256]{1,0:T(8,128)} %collective-permute-done.13, pred[]{:T(512)S(6)} %eq.5, f32[384,256]{1,0:T(8,128)} %get-tuple-element.45), kind=kLoop, calls=%fused_computation.1 | loop fusion | flops 393216 | bytes 1966081 | tf_op jit(solution)/shard_map/jit(_where)/select_n | solution.py:240
  35.4 1.8 %collective-permute-start.17 = (f32[384,256]{1,0:T(8,128)S(1)}, f32[384,256]{1,0:T(8,128)S(1)}, u32[]{:S(2)}, u32[]{:S(2)}) collective-permute-start(f32[384,256]{1,0:T(8,128)S(1)} %get-tuple-element.63), channel_id=1, source_target_pairs={{2,0},{4,2},{6,4},{7,6},{5,7},{3,5},{1,3},{0,1},{10,8},{12,10},{14... | collective-permute-start | bytes 1179656 | tf_op jit(solution)/shard_map/ppermute | solution.py:244
  37.5 4.4 %collective-permute-done.2.refs_3_ = f32[384,256]{1,0:T(8,128)S(1)} collective-permute-done((f32[384,256]{1,0:T(8,128)S(1)}, f32[384,256]{1,0:T(8,128)S(1)}, u32[]{:S(2)}, u32[]{:S(2)}) %collective-permute-start.2) | collective-permute-done | bytes 393248 | tf_op jit(solution)/shard_map/ppermute | solution.py:232
  42.0 2.0 %collective-permute-start.9 = (f32[384,256]{1,0:T(8,128)S(1)}, f32[384,256]{1,0:T(8,128)S(1)}, u32[]{:S(2)}, u32[]{:S(2)}) collective-permute-start(f32[384,256]{1,0:T(8,128)S(1)} %broadcast_select_fusion.1), channel_id=1, source_target_pairs={{0,2},{2,4},{4,6},{6,7},{7,5},{5,3},{3,1},{1,0},{10,8},{12,10},{14... | collective-permute-start | bytes 1179656 | tf_op jit(solution)/shard_map/ppermute | solution.py:235
  43.9 4.5 %collective-permute-done.17 = f32[384,256]{1,0:T(8,128)S(1)} collective-permute-done((f32[384,256]{1,0:T(8,128)S(1)}, f32[384,256]{1,0:T(8,128)S(1)}, u32[]{:S(2)}, u32[]{:S(2)}) %collective-permute-start.17) | collective-permute-done | bytes 393248 | tf_op jit(solution)/shard_map/ppermute | solution.py:244
  52.7 5.0 %shard_map.78 = (f32[384,256]{1,0:T(8,128)S(1)}, f32[384,256]{1,0:T(8,128)S(1)}, f32[384,256]{1,0:T(8,128)S(1)}, f32[384,256]{1,0:T(8,128)S(1)}) custom-call(s32[1,1,15]{2,1,0:T(1,128)} %rows_in.11, s32[1,1,15]{2,1,0:T(1,128)} %cols_in.11, f32[256,256]{1,0:T(8,128)} %d_in.3, f32[15,256,256]{2,1,0:T(8,128)S(1)} %bitcast.1, f32[384,256]{1,0:T(8,128)S(1)} %copy-done.1, ...), custom_call_target="tpu_custom_call" | custom-call | flops 2264924160 | bytes 20000000 | tf_op jit(solution)/shard_map/pallas_call | solution.py:324
  58.2 1.5 %collective-permute-done.18 = f32[384,256]{1,0:T(8,128)S(1)} collective-permute-done((f32[384,256]{1,0:T(8,128)S(1)}, f32[384,256]{1,0:T(8,128)S(1)}, u32[]{:S(2)}, u32[]{:S(2)}) %collective-permute-start.18) | collective-permute-done | bytes 393248 | tf_op jit(solution)/shard_map/ppermute | solution.py:244
  60.2 1.8 %collective-permute-start.16 = (f32[384,256]{1,0:T(8,128)S(1)}, f32[384,256]{1,0:T(8,128)S(1)}, u32[]{:S(2)}, u32[]{:S(2)}) collective-permute-start(f32[384,256]{1,0:T(8,128)S(1)} %add.47), channel_id=1, source_target_pairs={{0,2},{2,4},{4,6},{6,7},{7,5},{5,3},{3,1},{1,0},{8,10},{10,12},{12... | collective-permute-start | bytes 1179656 | tf_op jit(solution)/shard_map/ppermute | solution.py:243
  62.1 1.6 %collective-permute-start.11 = (f32[384,256]{1,0:T(8,128)S(1)}, f32[384,256]{1,0:T(8,128)S(1)}, u32[]{:S(2)}, u32[]{:S(2)}) collective-permute-start(f32[384,256]{1,0:T(8,128)S(1)} %add.41), channel_id=1, source_target_pairs={{0,16},{8,24},{16,0},{24,8},{1,17},{9,25},{17,1},{25,9},{2,18},{10... | collective-permute-start | bytes 1179656 | tf_op jit(solution)/shard_map/ppermute | solution.py:260
  63.6 2.2 %shard_map.79 = (bf16[8,256,384]{2,1,0:T(8,128)(2,1)S(1)}, bf16[8,256,384]{2,1,0:T(8,128)(2,1)S(1)}, bf16[4,384,256]{2,1,0:T(8,128)(2,1)S(1)}, bf16[4,384,256]{2,1,0:T(8,128)(2,1)S(1)}) custom-call(f32[384,256]{1,0:T(8,128)S(1)} %copy-done.1, f32[384,256]{1,0:T(8,128)S(1)} %collective-permute-done.refs_1_, f32[384,256]{1,0:T(8,128)S(1)} %collective-permute-done.1.refs_2_, ...), custom_call_target="tpu_custom_call" | custom-call | flops 2264924160 | bytes 20000000 | tf_op jit(solution)/shard_map/pallas_call | solution.py:334
  65.8 3.6 %collective-permute-done.19 = f32[384,256]{1,0:T(8,128)S(1)} collective-permute-done((f32[384,256]{1,0:T(8,128)S(1)}, f32[384,256]{1,0:T(8,128)S(1)}, u32[]{:S(2)}, u32[]{:S(2)}) %collective-permute-start.19) | collective-permute-done | bytes 393248 | tf_op jit(solution)/shard_map/ppermute | solution.py:244
  71.4 1.6 %collective-permute-start.20 = (f32[384,256]{1,0:T(8,128)S(1)}, f32[384,256]{1,0:T(8,128)S(1)}, u32[]{:S(2)}, u32[]{:S(2)}) collective-permute-start(f32[384,256]{1,0:T(8,128)S(1)} %add_add_fusion.refs_0_), channel_id=1, source_target_pairs={{0,2},{2,4},{4,6},{6,7},{7,5},{5,3},{3,1},{1,0},{8,10},{10,12},{12... | collective-permute-start | bytes 1179656 | tf_op jit(solution)/shard_map/ppermute | solution.py:232
  73.5 1.7 %collective-permute-start.23 = (f32[384,256]{1,0:T(8,128)S(1)}, f32[384,256]{1,0:T(8,128)S(1)}, u32[]{:S(2)}, u32[]{:S(2)}) collective-permute-start(f32[384,256]{1,0:T(8,128)S(1)} %add_add_fusion.refs_0_), channel_id=1, source_target_pairs={{0,16},{8,24},{16,0},{24,8},{1,17},{9,25},{17,1},{25,9},{2,18},{10... | collective-permute-start | bytes 1179656 | tf_op jit(solution)/shard_map/ppermute | solution.py:253
  75.2 5.3 %collective-permute-done.20.refs_1_ = f32[384,256]{1,0:T(8,128)S(1)} collective-permute-done((f32[384,256]{1,0:T(8,128)S(1)}, f32[384,256]{1,0:T(8,128)S(1)}, u32[]{:S(2)}, u32[]{:S(2)}) %collective-permute-start.20) | collective-permute-done | bytes 393248 | tf_op jit(solution)/shard_map/ppermute | solution.py:232
  80.5 1.8 %collective-permute-start.25 = (f32[384,256]{1,0:T(8,128)S(1)}, f32[384,256]{1,0:T(8,128)S(1)}, u32[]{:S(2)}, u32[]{:S(2)}) collective-permute-start(f32[384,256]{1,0:T(8,128)S(1)} %collective-permute-done.20.refs_1_), channel_id=1, source_target_pairs={{0,2},{2,4},{4,6},{6,7},{7,5},{5,3},{3,1},{1,0},{8,10},{10,12},{12... | collective-permute-start | bytes 1179656 | tf_op jit(solution)/shard_map/ppermute | solution.py:232
  83.1 4.2 %shard_map.80.v_ref = f32[15,256,256]{2,1,0:T(8,128)S(1)} custom-call(s32[1,1,15]{2,1,0:T(1,128)} %rows_in.11, s32[1,1,15]{2,1,0:T(1,128)} %cols_in.11, s32[1,1,15]{2,1,0:T(1,128)} %live_in.7, f32[15,256,256]{2,1,0:T(8,128)S(1)} %bitcast.2, bf16[4,384,256]{2,1,0:T(8,128)(2,1)S(1)} %get-tuple-element.50.rh, bf16[4,384,256]{2,1,0:T(8,128)(2,1)S(1)} %get-tuple-element.51.rl, ...), custom_call_target="tpu_custom_call" | custom-call | flops 2264924160 | bytes 20000000 | tf_op jit(solution)/shard_map/pallas_call | solution.py:349
  88.3 1.8 %collective-permute-done.26.refs_1_ = f32[384,256]{1,0:T(8,128)S(1)} collective-permute-done((f32[384,256]{1,0:T(8,128)S(1)}, f32[384,256]{1,0:T(8,128)S(1)}, u32[]{:S(2)}, u32[]{:S(2)}) %collective-permute-start.26) | collective-permute-done | bytes 393248 | tf_op jit(solution)/shard_map/ppermute | solution.py:233
  90.1 1.6 %collective-permute-start.27 = (f32[384,256]{1,0:T(8,128)S(1)}, f32[384,256]{1,0:T(8,128)S(1)}, u32[]{:S(2)}, u32[]{:S(2)}) collective-permute-start(f32[384,256]{1,0:T(8,128)S(1)} %collective-permute-done.25.refs_0_), channel_id=1, source_target_pairs={{0,2},{2,4},{4,6},{6,7},{7,5},{5,3},{3,1},{1,0},{8,10},{10,12},{12... | collective-permute-start | bytes 1179656 | tf_op jit(solution)/shard_map/ppermute | solution.py:232
  92.1 6.4 %shard_map.81 = (f32[1,1,15,256,256]{4,3,2,1,0:T(8,128)}, f32[15,256,256]{2,1,0:T(8,128)S(1)}, f32[256,256]{1,0:T(8,128)}) custom-call(s32[1,1,15]{2,1,0:T(1,128)} %rows_in.11, s32[1,1,15]{2,1,0:T(1,128)} %cols_in.11, s32[1,1,15]{2,1,0:T(1,128)} %live_in.7, f32[256,256]{1,0:T(8,128)} %d_in.3, f32[15,256,256]{2,1,0:T(8,128)S(1)} %shard_map.80.v_ref, ...), custom_call_target="tpu_custom_call" | custom-call | flops 2264924160 | bytes 20000000 | tf_op jit(solution)/shard_map/pallas_call | solution.py:364
  98.5 2.3 %collective-permute-done.28.refs_3_ = f32[384,256]{1,0:T(8,128)S(1)} collective-permute-done((f32[384,256]{1,0:T(8,128)S(1)}, f32[384,256]{1,0:T(8,128)S(1)}, u32[]{:S(2)}, u32[]{:S(2)}) %collective-permute-start.28) | collective-permute-done | bytes 393248 | tf_op jit(solution)/shard_map/ppermute | solution.py:233
  102.1 5.5 %shard_map.82.refs_1_ = f32[1,1,15,256,256]{4,3,2,1,0:T(8,128)} custom-call(s32[1,1,15]{2,1,0:T(1,128)} %rows_in.11, s32[1,1,15]{2,1,0:T(1,128)} %cols_in.11, s32[1,1,15]{2,1,0:T(1,128)} %live_in.7, f32[15,256,256]{2,1,0:T(8,128)S(1)} %get-tuple-element.55.v_ref, bf16[4,384,256]{2,1,0:T(8,128)(2,1)S(1)} %get-tuple-element.50.rh, ...), custom_call_target="tpu_custom_call", output_to_operand_aliasing={{}: (10, {})} | custom-call | flops 2264924160 | bytes 20000000 | tf_op jit(solution)/shard_map/pallas_call | solution.py:379
  108.7 2.6 %shard_map.83 = f32[1,1,15,256,256]{4,3,2,1,0:T(8,128)} custom-call(s32[1,1,15]{2,1,0:T(1,128)} %rows_in.11, s32[1,1,15]{2,1,0:T(1,128)} %cols_in.11, s32[1,1,15]{2,1,0:T(1,128)} %live_in.7, f32[15,256,256]{2,1,0:T(8,128)S(1)} %get-tuple-element.55.v_ref, bf16[4,384,256]{2,1,0:T(8,128)(2,1)S(1)} %get-tuple-element.50.rh, ...), custom_call_target="tpu_custom_call", output_to_operand_aliasing={{}: (7, {})} | custom-call | flops 2264924160 | bytes 20000000 | tf_op jit(solution)/shard_map/pallas_call | solution.py:379
  (54 shorter events, 13.5 us)
Async XLA Ops:
  0.6 12.3 %collective-permute-start.7 = (f32[384,256]{1,0:T(8,128)}, f32[384,256]{1,0:T(8,128)S(1)}, u32[]{:S(2)}, u32[]{:S(2)}) collective-permute-start(f32[384,256]{1,0:T(8,128)} %refs_8_.1), channel_id=1, source_target_pairs={{0,16},{8,24},{16,0},{24,8},{1,17},{9,25},{17,1},{25,9},{2,18},{10... | collective-permute-start | bytes 1179656 | tf_op jit(solution)/shard_map/ppermute | solution.py:253
  3.6 10.8 %collective-permute-start = (f32[384,256]{1,0:T(8,128)}, f32[384,256]{1,0:T(8,128)S(1)}, u32[]{:S(2)}, u32[]{:S(2)}) collective-permute-start(f32[384,256]{1,0:T(8,128)} %refs_8_.1), channel_id=1, source_target_pairs={{0,2},{2,4},{4,6},{6,7},{7,5},{5,3},{3,1},{1,0},{8,10},{10,12},{12... | collective-permute-start | bytes 1179656 | tf_op jit(solution)/shard_map/ppermute | solution.py:232
  5.2 10.8 %collective-permute-start.3 = (f32[384,256]{1,0:T(8,128)}, f32[384,256]{1,0:T(8,128)S(1)}, u32[]{:S(2)}, u32[]{:S(2)}) collective-permute-start(f32[384,256]{1,0:T(8,128)} %refs_8_.1), channel_id=1, source_target_pairs={{2,0},{4,2},{6,4},{7,6},{5,7},{3,5},{1,3},{0,1},{10,8},{12,10},{14... | collective-permute-start | bytes 1179656 | tf_op jit(solution)/shard_map/ppermute | solution.py:233
  5.7 10.8 %collective-permute-start.6 = (f32[384,256]{1,0:T(8,128)}, f32[384,256]{1,0:T(8,128)S(1)}, u32[]{:S(2)}, u32[]{:S(2)}) collective-permute-start(f32[384,256]{1,0:T(8,128)} %refs_8_.1), channel_id=1, source_target_pairs={{0,8},{8,0},{16,24},{24,16},{1,9},{9,1},{17,25},{25,17},{2,10},{10... | collective-permute-start | bytes 1179656 | tf_op jit(solution)/shard_map/ppermute | solution.py:254
  13.0 3.5 %collective-permute-start.8 = (f32[384,256]{1,0:T(8,128)S(1)}, f32[384,256]{1,0:T(8,128)S(1)}, u32[]{:S(2)}, u32[]{:S(2)}) collective-permute-start(f32[384,256]{1,0:T(8,128)S(1)} %collective-permute-done.7.refs_1_.refs_10_), channel_id=1, source_target_pairs={{0,8},{8,0},{16,24},{24,16},{1,9},{9,1},{17,25},{25,17},{2,10},{10... | collective-permute-start | bytes 1179656 | tf_op jit(solution)/shard_map/ppermute | solution.py:254
  14.4 10.2 %collective-permute-start.1 = (f32[384,256]{1,0:T(8,128)S(1)}, f32[384,256]{1,0:T(8,128)S(1)}, u32[]{:S(2)}, u32[]{:S(2)}) collective-permute-start(f32[384,256]{1,0:T(8,128)S(1)} %collective-permute-done.refs_1_), channel_id=1, source_target_pairs={{0,2},{2,4},{4,6},{6,7},{7,5},{5,3},{3,1},{1,0},{8,10},{10,12},{12... | collective-permute-start | bytes 1179656 | tf_op jit(solution)/shard_map/ppermute | solution.py:232
  16.0 11.7 %collective-permute-start.4 = (f32[384,256]{1,0:T(8,128)S(1)}, f32[384,256]{1,0:T(8,128)}, u32[]{:S(2)}, u32[]{:S(2)}) collective-permute-start(f32[384,256]{1,0:T(8,128)S(1)} %collective-permute-done.3.refs_7_), channel_id=1, source_target_pairs={{2,0},{4,2},{6,4},{7,6},{5,7},{3,5},{1,3},{0,1},{10,8},{12,10},{14... | collective-permute-start | bytes 1179656 | tf_op jit(solution)/shard_map/ppermute | solution.py:233
  23.0 29.7 %copy-start.1 = (f32[384,256]{1,0:T(8,128)S(1)}, f32[384,256]{1,0:T(8,128)}, u32[]{:S(2)}) copy-start(f32[384,256]{1,0:T(8,128)} %refs_8_.1) | copy-start | bytes 1179652
  23.0 11.2 %collective-permute-start.13 = (f32[384,256]{1,0:T(8,128)}, f32[384,256]{1,0:T(8,128)}, u32[]{:S(2)}, u32[]{:S(2)}) collective-permute-start(f32[384,256]{1,0:T(8,128)} %get-tuple-element.42), channel_id=1, source_target_pairs={{0,2},{2,4},{4,6},{6,7},{7,5},{5,3},{3,1},{1,0},{10,8},{12,10},{14... | collective-permute-start | bytes 1179656 | tf_op jit(solution)/shard_map/ppermute | solution.py:239
  24.6 17.3 %collective-permute-start.2 = (f32[384,256]{1,0:T(8,128)S(1)}, f32[384,256]{1,0:T(8,128)S(1)}, u32[]{:S(2)}, u32[]{:S(2)}) collective-permute-start(f32[384,256]{1,0:T(8,128)S(1)} %collective-permute-done.1.refs_2_), channel_id=1, source_target_pairs={{0,2},{2,4},{4,6},{6,7},{7,5},{5,3},{3,1},{1,0},{8,10},{10,12},{12... | collective-permute-start | bytes 1179656 | tf_op jit(solution)/shard_map/ppermute | solution.py:232
  27.7 14.2 %collective-permute-start.5 = (f32[384,256]{1,0:T(8,128)}, f32[384,256]{1,0:T(8,128)S(1)}, u32[]{:S(2)}, u32[]{:S(2)}) collective-permute-start(f32[384,256]{1,0:T(8,128)} %collective-permute-done.4.refs_6_), channel_id=1, source_target_pairs={{2,0},{4,2},{6,4},{7,6},{5,7},{3,5},{1,3},{0,1},{10,8},{12,10},{14... | collective-permute-start | bytes 1179656 | tf_op jit(solution)/shard_map/ppermute | solution.py:233
  27.7 24.9 %copy-start = (f32[1,1,15,256,256]{4,3,2,1,0:T(8,128)S(1)}, f32[1,1,15,256,256]{4,3,2,1,0:T(8,128)}, u32[]{:S(2)}) copy-start(f32[1,1,15,256,256]{4,3,2,1,0:T(8,128)} %t_in.1) | copy-start | bytes 11796484
  35.4 13.0 %collective-permute-start.17 = (f32[384,256]{1,0:T(8,128)S(1)}, f32[384,256]{1,0:T(8,128)S(1)}, u32[]{:S(2)}, u32[]{:S(2)}) collective-permute-start(f32[384,256]{1,0:T(8,128)S(1)} %get-tuple-element.63), channel_id=1, source_target_pairs={{2,0},{4,2},{6,4},{7,6},{5,7},{3,5},{1,3},{0,1},{10,8},{12,10},{14... | collective-permute-start | bytes 1179656 | tf_op jit(solution)/shard_map/ppermute | solution.py:244
  37.2 13.2 %collective-permute-start.14 = (f32[384,256]{1,0:T(8,128)S(1)}, f32[384,256]{1,0:T(8,128)S(1)}, u32[]{:S(2)}, u32[]{:S(2)}) collective-permute-start(f32[384,256]{1,0:T(8,128)S(1)} %get-tuple-element.62), channel_id=1, source_target_pairs={{0,2},{2,4},{4,6},{6,7},{7,5},{5,3},{3,1},{1,0},{8,10},{10,12},{12... | collective-permute-start | bytes 1179656 | tf_op jit(solution)/shard_map/ppermute | solution.py:243
  42.0 10.7 %collective-permute-start.9 = (f32[384,256]{1,0:T(8,128)S(1)}, f32[384,256]{1,0:T(8,128)S(1)}, u32[]{:S(2)}, u32[]{:S(2)}) collective-permute-start(f32[384,256]{1,0:T(8,128)S(1)} %broadcast_select_fusion.1), channel_id=1, source_target_pairs={{0,2},{2,4},{4,6},{6,7},{7,5},{5,3},{3,1},{1,0},{10,8},{12,10},{14... | collective-permute-start | bytes 1179656 | tf_op jit(solution)/shard_map/ppermute | solution.py:235
  49.5 10.3 %collective-permute-start.18 = (f32[384,256]{1,0:T(8,128)S(1)}, f32[384,256]{1,0:T(8,128)S(1)}, u32[]{:S(2)}, u32[]{:S(2)}) collective-permute-start(f32[384,256]{1,0:T(8,128)S(1)} %add.50), channel_id=1, source_target_pairs={{2,0},{4,2},{6,4},{7,6},{5,7},{3,5},{1,3},{0,1},{10,8},{12,10},{14... | collective-permute-start | bytes 1179656 | tf_op jit(solution)/shard_map/ppermute | solution.py:244
  51.5 8.7 %collective-permute-start.15 = (f32[384,256]{1,0:T(8,128)S(1)}, f32[384,256]{1,0:T(8,128)S(1)}, u32[]{:S(2)}, u32[]{:S(2)}) collective-permute-start(f32[384,256]{1,0:T(8,128)S(1)} %add.46), channel_id=1, source_target_pairs={{0,2},{2,4},{4,6},{6,7},{7,5},{5,3},{3,1},{1,0},{8,10},{10,12},{12... | collective-permute-start | bytes 1179656 | tf_op jit(solution)/shard_map/ppermute | solution.py:243
  57.7 4.3 %collective-permute-start.10 = (f32[384,256]{1,0:T(8,128)S(1)}, f32[384,256]{1,0:T(8,128)S(1)}, u32[]{:S(2)}, u32[]{:S(2)}) collective-permute-start(f32[384,256]{1,0:T(8,128)S(1)} %get-tuple-element.36), channel_id=1, source_target_pairs={{0,8},{8,0},{16,24},{24,16},{1,9},{9,1},{17,25},{25,17},{2,10},{10... | collective-permute-start | bytes 1179656 | tf_op jit(solution)/shard_map/ppermute | solution.py:257
  57.8 8.1 %collective-permute-start.12 = (f32[384,256]{1,0:T(8,128)S(1)}, f32[384,256]{1,0:T(8,128)S(1)}, u32[]{:S(2)}, u32[]{:S(2)}) collective-permute-start(f32[384,256]{1,0:T(8,128)S(1)} %get-tuple-element.38), channel_id=1, source_target_pairs={{0,8},{8,0},{16,24},{24,16},{1,9},{9,1},{17,25},{25,17},{2,10},{10... | collective-permute-start | bytes 1179656 | tf_op jit(solution)/shard_map/ppermute | solution.py:257
  59.8 9.7 %collective-permute-start.19 = (f32[384,256]{1,0:T(8,128)S(1)}, f32[384,256]{1,0:T(8,128)S(1)}, u32[]{:S(2)}, u32[]{:S(2)}) collective-permute-start(f32[384,256]{1,0:T(8,128)S(1)} %add.51), channel_id=1, source_target_pairs={{2,0},{4,2},{6,4},{7,6},{5,7},{3,5},{1,3},{0,1},{10,8},{12,10},{14... | collective-permute-start | bytes 1179656 | tf_op jit(solution)/shard_map/ppermute | solution.py:244
  60.2 10.0 %collective-permute-start.16 = (f32[384,256]{1,0:T(8,128)S(1)}, f32[384,256]{1,0:T(8,128)S(1)}, u32[]{:S(2)}, u32[]{:S(2)}) collective-permute-start(f32[384,256]{1,0:T(8,128)S(1)} %add.47), channel_id=1, source_target_pairs={{0,2},{2,4},{4,6},{6,7},{7,5},{5,3},{3,1},{1,0},{8,10},{10,12},{12... | collective-permute-start | bytes 1179656 | tf_op jit(solution)/shard_map/ppermute | solution.py:243
  62.1 9.2 %collective-permute-start.11 = (f32[384,256]{1,0:T(8,128)S(1)}, f32[384,256]{1,0:T(8,128)S(1)}, u32[]{:S(2)}, u32[]{:S(2)}) collective-permute-start(f32[384,256]{1,0:T(8,128)S(1)} %add.41), channel_id=1, source_target_pairs={{0,16},{8,24},{16,0},{24,8},{1,17},{9,25},{17,1},{25,9},{2,18},{10... | collective-permute-start | bytes 1179656 | tf_op jit(solution)/shard_map/ppermute | solution.py:260
  71.4 9.1 %collective-permute-start.20 = (f32[384,256]{1,0:T(8,128)S(1)}, f32[384,256]{1,0:T(8,128)S(1)}, u32[]{:S(2)}, u32[]{:S(2)}) collective-permute-start(f32[384,256]{1,0:T(8,128)S(1)} %add_add_fusion.refs_0_), channel_id=1, source_target_pairs={{0,2},{2,4},{4,6},{6,7},{7,5},{5,3},{3,1},{1,0},{8,10},{10,12},{12... | collective-permute-start | bytes 1179656 | tf_op jit(solution)/shard_map/ppermute | solution.py:232
  73.0 9.3 %collective-permute-start.21 = (f32[384,256]{1,0:T(8,128)S(1)}, f32[384,256]{1,0:T(8,128)S(1)}, u32[]{:S(2)}, u32[]{:S(2)}) collective-permute-start(f32[384,256]{1,0:T(8,128)S(1)} %add_add_fusion.refs_0_), channel_id=1, source_target_pairs={{2,0},{4,2},{6,4},{7,6},{5,7},{3,5},{1,3},{0,1},{10,8},{12,10},{14... | collective-permute-start | bytes 1179656 | tf_op jit(solution)/shard_map/ppermute | solution.py:233
  73.5 9.1 %collective-permute-start.23 = (f32[384,256]{1,0:T(8,128)S(1)}, f32[384,256]{1,0:T(8,128)S(1)}, u32[]{:S(2)}, u32[]{:S(2)}) collective-permute-start(f32[384,256]{1,0:T(8,128)S(1)} %add_add_fusion.refs_0_), channel_id=1, source_target_pairs={{0,16},{8,24},{16,0},{24,8},{1,17},{9,25},{17,1},{25,9},{2,18},{10... | collective-permute-start | bytes 1179656 | tf_op jit(solution)/shard_map/ppermute | solution.py:253
  80.5 7.8 %collective-permute-start.25 = (f32[384,256]{1,0:T(8,128)S(1)}, f32[384,256]{1,0:T(8,128)S(1)}, u32[]{:S(2)}, u32[]{:S(2)}) collective-permute-start(f32[384,256]{1,0:T(8,128)S(1)} %collective-permute-done.20.refs_1_), channel_id=1, source_target_pairs={{0,2},{2,4},{4,6},{6,7},{7,5},{5,3},{3,1},{1,0},{8,10},{10,12},{12... | collective-permute-start | bytes 1179656 | tf_op jit(solution)/shard_map/ppermute | solution.py:232
  82.3 7.8 %collective-permute-start.26 = (f32[384,256]{1,0:T(8,128)S(1)}, f32[384,256]{1,0:T(8,128)S(1)}, u32[]{:S(2)}, u32[]{:S(2)}) collective-permute-start(f32[384,256]{1,0:T(8,128)S(1)} %collective-permute-done.21.refs_2_), channel_id=1, source_target_pairs={{2,0},{4,2},{6,4},{7,6},{5,7},{3,5},{1,3},{0,1},{10,8},{12,10},{14... | collective-permute-start | bytes 1179656 | tf_op jit(solution)/shard_map/ppermute | solution.py:233
  82.5 9.6 %collective-permute-start.22 = (f32[384,256]{1,0:T(8,128)S(1)}, f32[384,256]{1,0:T(8,128)S(1)}, u32[]{:S(2)}, u32[]{:S(2)}) collective-permute-start(f32[384,256]{1,0:T(8,128)S(1)} %add_add_fusion.refs_0_), channel_id=1, source_target_pairs={{0,8},{8,0},{16,24},{24,16},{1,9},{9,1},{17,25},{25,17},{2,10},{10... | collective-permute-start | bytes 1179656 | tf_op jit(solution)/shard_map/ppermute | solution.py:254
  82.5 9.6 %collective-permute-start.24 = (f32[384,256]{1,0:T(8,128)S(1)}, f32[384,256]{1,0:T(8,128)S(1)}, u32[]{:S(2)}, u32[]{:S(2)}) collective-permute-start(f32[384,256]{1,0:T(8,128)S(1)} %collective-permute-done.23.refs_2_), channel_id=1, source_target_pairs={{0,8},{8,0},{16,24},{24,16},{1,9},{9,1},{17,25},{25,17},{2,10},{10... | collective-permute-start | bytes 1179656 | tf_op jit(solution)/shard_map/ppermute | solution.py:254
  90.1 8.4 %collective-permute-start.27 = (f32[384,256]{1,0:T(8,128)S(1)}, f32[384,256]{1,0:T(8,128)S(1)}, u32[]{:S(2)}, u32[]{:S(2)}) collective-permute-start(f32[384,256]{1,0:T(8,128)S(1)} %collective-permute-done.25.refs_0_), channel_id=1, source_target_pairs={{0,2},{2,4},{4,6},{6,7},{7,5},{5,3},{3,1},{1,0},{8,10},{10,12},{12... | collective-permute-start | bytes 1179656 | tf_op jit(solution)/shard_map/ppermute | solution.py:232
  91.7 9.2 %collective-permute-start.28 = (f32[384,256]{1,0:T(8,128)S(1)}, f32[384,256]{1,0:T(8,128)S(1)}, u32[]{:S(2)}, u32[]{:S(2)}) collective-permute-start(f32[384,256]{1,0:T(8,128)S(1)} %collective-permute-done.26.refs_1_), channel_id=1, source_target_pairs={{2,0},{4,2},{6,4},{7,6},{5,7},{3,5},{1,3},{0,1},{10,8},{12,10},{14... | collective-permute-start | bytes 1179656 | tf_op jit(solution)/shard_map/ppermute | solution.py:233
  100.9 7.8 %collective-permute-start.29 = (f32[384,256]{1,0:T(8,128)S(1)}, f32[384,256]{1,0:T(8,128)S(1)}, u32[]{:S(2)}, u32[]{:S(2)}) collective-permute-start(f32[384,256]{1,0:T(8,128)S(1)} %broadcast_select_fusion), channel_id=1, source_target_pairs={{0,2},{2,4},{4,6},{6,7},{7,5},{5,3},{3,1},{1,0},{10,8},{12,10},{14... | collective-permute-start | bytes 1179656 | tf_op jit(solution)/shard_map/ppermute | solution.py:235
  (3 other events, 23.8 us)

commit v4 on v3

--- a/solution.py
+++ b/solution.py
@@ -176,11 +176,13 @@
         pl.when(mine[slot])(copies[slot].wait)
 
 
-def late_kernel(nr, nc, scale, places, rows_in, cols_in, live_in, v_ref, rh, rl, *refs):
-    z_refs, refs = refs[: len(places)], refs[len(places) :]
+def late_kernel(nr, nc, scale, places, parts, rows_in, cols_in, live_in, v_ref, rh, rl, *refs):
+    z_refs, refs = refs[: parts * len(places)], refs[parts * len(places) :]
     _, out_ref, rows, cols, live, sems, zh, zl, made, out_sems = refs
     small = fetch((rows_in, cols_in, live_in), (rows, cols, live), sems)
-    fill_turned(z_refs, zh, zl)
+    for k in range(len(places)):
+        block = jnp.concatenate([ref[...] for ref in z_refs[parts * k : parts * (k + 1)]], axis=0)
+        zh[k], zl[k] = split(block.T)
     for copy in small:
         copy.wait()
     mine, copies = [], []
@@ -222,13 +224,16 @@
     far = nc // 2
     go = lax.ppermute
 
-    def ring_gather(own, beside):
+    def ring_gather(own, beside, cut=False):
         found = [own] + [None] * (nc - 1)
         for d in range(1, far + 1):
             one, two = found[d - 1], found[(nc - d + 1) % nc]
             if d in beside:
                 one, two, _ = lax.optimization_barrier((one, two, beside[d](found)))
-            if d < far:
+            if d == far and cut:
+                half = own.shape[0] // 2
+                found[far] = (go(one[:half], "col", right), go(two[half:], "col", left))
+            elif d < far:
                 found[d] = go(one, "col", right)
                 found[nc - d] = go(two, "col", left)
             else:
@@ -373,13 +378,14 @@
         )
         return made[2]
 
-    z_col = ring_gather(z, {far - 1: first, far: second})
+    z_col = ring_gather(z, {far - 1: first, far: second}, True)
     _, new_tiles, partial, new_diag = made
     for places in (late_places, far_places):
+        came = [a for p in places for a in (z_col[p] if isinstance(z_col[p], tuple) else (z_col[p],))]
         new_tiles = call(
-            functools.partial(late_kernel, nr, nc, scale, places),
+            functools.partial(late_kernel, nr, nc, scale, places, len(came) // len(places)),
             3,
-            3 + len(places),
+            3 + len(came),
             in_place,
             jax.ShapeDtypeStruct(omega_tiles.shape, F32),
             ids(3)
@@ -387,8 +393,8 @@
             + panel_t(len(places))
             + [pltpu.VMEM((slots, side, side), F32), sems(slots)],
             10 + nc,
-            {6 + len(places): 0},
-        )(tile_rows, tile_cols, tile_active, partial, rh, rl, *[z_col[p] for p in places], new_tiles)
+            {6 + len(came): 0},
+        )(tile_rows, tile_cols, tile_active, partial, rh, rl, *came, new_tiles)
     return new_tiles, new_diag
 
 

time: 112 us -> 111 us (level)
  waiting for transfers between devices: 43.9 us -> 41.8 us
    ppermute x0 -> x2, starting transfers between devices: none -> 2.13 us  [ring_gather(): found[far] = (go(one[:half], 'col', right), go(two[half:], 'col', left))]
    ppermute x2 -> x1, starting transfers between devices: 3.15 us -> 1.96 us  [ring_gather(): found[far] = go(jnp.where(even_core, one, two), ('row', 'col'), both)]
  transfers between devices with their start and end apart: 30 -> 31, of which waited for: 15 -> 14; matrix products, arithmetic and copies ran while one was open for 3% -> 3% of each run, Pallas kernels for 27% -> 27%
where the time goes in v4:
time: 111 us; the launch traced here: 110 us
  waiting for transfers between devices  41.8 us (38%)
  Pallas kernels  32.4 us (29%)
  starting transfers between devices  31.3 us (28%)
  other arithmetic  3.76 us (3%)
    ppermute x6, waiting for transfers between devices, ring_gather(): found[d] = go(one, 'col', right)  12.1 us
    ppermute x6, starting transfers between devices, ring_gather(): found[d] = go(one, 'col', right)  9.86 us
    ppermute x3, waiting for transfers between devices, ring_sum(): two = go(two, 'col', left)  9.6 us
    pallas_call x2, Pallas kernels, per_device(): call(functools.partial(late_kernel, nr, nc, scale, places, len(came) // l...  8.15 us
    ppermute x2, waiting for transfers between devices, row_gather(): found.append(go(found[-1], 'row', chip))  7.3 us
    pallas_call x1, Pallas kernels, mirror(): call(functools.partial(w_kernel, nr, nc, near), 4, nr - 1, [whole if k in...  6.5 us
    ppermute x1, waiting for transfers between devices, ring_sum(): first = go(parts[far], ('row', 'col'), both)  6.43 us
    pallas_call x1, Pallas kernels, second(): call(functools.partial(second_kernel, nr, nc, scale, near_places), 4, 3 +...  6.39 us
  transfers between devices with their start and end apart: 31, of which 14 were waited for; matrix products, arithmetic and copies ran while one was open for 3% of the time, Pallas kernels for 27%

profile of v4, /device:TPU:0, one launch (start us, length us, event | category | flops | bytes accessed | tf_op | source)
XLA Modules:
  0.0 110.4 jit_solution(3890644696973890759)
XLA Ops:
  0.6 3.0 %collective-permute-start.7 = (f32[384,256]{1,0:T(8,128)}, f32[384,256]{1,0:T(8,128)S(1)}, u32[]{:S(2)}, u32[]{:S(2)}) collective-permute-start(f32[384,256]{1,0:T(8,128)} %refs_8_.1), channel_id=1, source_target_pairs={{0,16},{8,24},{16,0},{24,8},{1,17},{9,25},{17,1},{25,9},{2,18},{10... | collective-permute-start | bytes 1179656 | tf_op jit(solution)/shard_map/ppermute | solution.py:258
  3.6 1.6 %collective-permute-start = (f32[384,256]{1,0:T(8,128)}, f32[384,256]{1,0:T(8,128)S(1)}, u32[]{:S(2)}, u32[]{:S(2)}) collective-permute-start(f32[384,256]{1,0:T(8,128)} %refs_8_.1), channel_id=1, source_target_pairs={{0,2},{2,4},{4,6},{6,7},{7,5},{5,3},{3,1},{1,0},{8,10},{10,12},{12... | collective-permute-start | bytes 1179656 | tf_op jit(solution)/shard_map/ppermute | solution.py:237
  5.7 7.3 %collective-permute-done.7.refs_1_.refs_10_ = f32[384,256]{1,0:T(8,128)S(1)} collective-permute-done((f32[384,256]{1,0:T(8,128)}, f32[384,256]{1,0:T(8,128)S(1)}, u32[]{:S(2)}, u32[]{:S(2)}) %collective-permute-start.7) | collective-permute-done | bytes 393248 | tf_op jit(solution)/shard_map/ppermute | solution.py:258
  13.0 1.5 %collective-permute-done.refs_1_ = f32[384,256]{1,0:T(8,128)S(1)} collective-permute-done((f32[384,256]{1,0:T(8,128)}, f32[384,256]{1,0:T(8,128)S(1)}, u32[]{:S(2)}, u32[]{:S(2)}) %collective-permute-start) | collective-permute-done | bytes 393248 | tf_op jit(solution)/shard_map/ppermute | solution.py:237
  14.4 1.6 %collective-permute-start.1 = (f32[384,256]{1,0:T(8,128)S(1)}, f32[384,256]{1,0:T(8,128)S(1)}, u32[]{:S(2)}, u32[]{:S(2)}) collective-permute-start(f32[384,256]{1,0:T(8,128)S(1)} %collective-permute-done.refs_1_), channel_id=1, source_target_pairs={{0,2},{2,4},{4,6},{6,7},{7,5},{5,3},{3,1},{1,0},{8,10},{10,12},{12... | collective-permute-start | bytes 1179656 | tf_op jit(solution)/shard_map/ppermute | solution.py:237
  16.5 6.5 %shard_map.77 = (f32[384,256]{1,0:T(8,128)}, f32[384,256]{1,0:T(8,128)}, f32[384,256]{1,0:T(8,128)}, f32[384,256]{1,0:T(8,128)}, f32[384,256]{1,0:T(8,128)}, /*i...) custom-call(s32[1,1,15]{2,1,0:T(1,128)} %rows_in.11, s32[1,1,15]{2,1,0:T(1,128)} %cols_in.11, ...), custom_call_target="tpu_custom_call" | custom-call | flops 2264924160 | bytes 20000000 | tf_op jit(solution)/shard_map/pallas_call | solution.py:314
  23.0 1.6 %collective-permute-start.13 = (f32[384,256]{1,0:T(8,128)}, f32[384,256]{1,0:T(8,128)}, u32[]{:S(2)}, u32[]{:S(2)}) collective-permute-start(f32[384,256]{1,0:T(8,128)} %get-tuple-element.42), channel_id=1, source_target_pairs={{0,2},{2,4},{4,6},{6,7},{7,5},{5,3},{3,1},{1,0},{10,8},{12,10},{14... | collective-permute-start | bytes 1179656 | tf_op jit(solution)/shard_map/ppermute | solution.py:244
  24.6 1.7 %collective-permute-start.2 = (f32[384,256]{1,0:T(8,128)S(1)}, f32[384,256]{1,0:T(8,128)S(1)}, u32[]{:S(2)}, u32[]{:S(2)}) collective-permute-start(f32[384,256]{1,0:T(8,128)S(1)} %collective-permute-done.1.refs_2_), channel_id=1, source_target_pairs={{0,2},{2,4},{4,6},{6,7},{7,5},{5,3},{3,1},{1,0},{8,10},{10,12},{12... | collective-permute-start | bytes 1179656 | tf_op jit(solution)/shard_map/ppermute | solution.py:237
  26.3 1.4 %collective-permute-done.4.refs_6_ = f32[384,256]{1,0:T(8,128)} collective-permute-done((f32[384,256]{1,0:T(8,128)S(1)}, f32[384,256]{1,0:T(8,128)}, u32[]{:S(2)}, u32[]{:S(2)}) %collective-permute-start.4) | collective-permute-done | bytes 393248 | tf_op jit(solution)/shard_map/ppermute | solution.py:238
  27.7 6.4 %collective-permute-done.13 = f32[384,256]{1,0:T(8,128)} collective-permute-done((f32[384,256]{1,0:T(8,128)}, f32[384,256]{1,0:T(8,128)}, u32[]{:S(2)}, u32[]{:S(2)}) %collective-permute-start.13) | collective-permute-done | bytes 393248 | tf_op jit(solution)/shard_map/ppermute | solution.py:244
  35.5 1.8 %collective-permute-start.17 = (f32[384,256]{1,0:T(8,128)S(1)}, f32[384,256]{1,0:T(8,128)S(1)}, u32[]{:S(2)}, u32[]{:S(2)}) collective-permute-start(f32[384,256]{1,0:T(8,128)S(1)} %get-tuple-element.63), channel_id=1, source_target_pairs={{2,0},{4,2},{6,4},{7,6},{5,7},{3,5},{1,3},{0,1},{10,8},{12,10},{14... | collective-permute-start | bytes 1179656 | tf_op jit(solution)/shard_map/ppermute | solution.py:249
  37.5 4.4 %collective-permute-done.2.refs_3_ = f32[384,256]{1,0:T(8,128)S(1)} collective-permute-done((f32[384,256]{1,0:T(8,128)S(1)}, f32[384,256]{1,0:T(8,128)S(1)}, u32[]{:S(2)}, u32[]{:S(2)}) %collective-permute-start.2) | collective-permute-done | bytes 393248 | tf_op jit(solution)/shard_map/ppermute | solution.py:237
  42.0 2.0 %collective-permute-start.9 = (f32[384,256]{1,0:T(8,128)S(1)}, f32[384,256]{1,0:T(8,128)S(1)}, u32[]{:S(2)}, u32[]{:S(2)}) collective-permute-start(f32[384,256]{1,0:T(8,128)S(1)} %broadcast_select_fusion), channel_id=1, source_target_pairs={{0,2},{2,4},{4,6},{6,7},{7,5},{5,3},{3,1},{1,0},{10,8},{12,10},{14... | collective-permute-start | bytes 1179656 | tf_op jit(solution)/shard_map/ppermute | solution.py:240
  43.9 4.5 %collective-permute-done.17 = f32[384,256]{1,0:T(8,128)S(1)} collective-permute-done((f32[384,256]{1,0:T(8,128)S(1)}, f32[384,256]{1,0:T(8,128)S(1)}, u32[]{:S(2)}, u32[]{:S(2)}) %collective-permute-start.17) | collective-permute-done | bytes 393248 | tf_op jit(solution)/shard_map/ppermute | solution.py:249
  52.7 5.0 %shard_map.78 = (f32[384,256]{1,0:T(8,128)S(1)}, f32[384,256]{1,0:T(8,128)S(1)}, f32[384,256]{1,0:T(8,128)S(1)}, f32[384,256]{1,0:T(8,128)S(1)}) custom-call(s32[1,1,15]{2,1,0:T(1,128)} %rows_in.11, s32[1,1,15]{2,1,0:T(1,128)} %cols_in.11, f32[256,256]{1,0:T(8,128)} %d_in.3, f32[15,256,256]{2,1,0:T(8,128)S(1)} %bitcast.1, f32[384,256]{1,0:T(8,128)S(1)} %copy-done.1, ...), custom_call_target="tpu_custom_call" | custom-call | flops 2264924160 | bytes 20000000 | tf_op jit(solution)/shard_map/pallas_call | solution.py:329
  58.2 1.5 %collective-permute-done.18 = f32[384,256]{1,0:T(8,128)S(1)} collective-permute-done((f32[384,256]{1,0:T(8,128)S(1)}, f32[384,256]{1,0:T(8,128)S(1)}, u32[]{:S(2)}, u32[]{:S(2)}) %collective-permute-start.18) | collective-permute-done | bytes 393248 | tf_op jit(solution)/shard_map/ppermute | solution.py:249
  60.2 1.8 %collective-permute-start.16 = (f32[384,256]{1,0:T(8,128)S(1)}, f32[384,256]{1,0:T(8,128)S(1)}, u32[]{:S(2)}, u32[]{:S(2)}) collective-permute-start(f32[384,256]{1,0:T(8,128)S(1)} %add.47), channel_id=1, source_target_pairs={{0,2},{2,4},{4,6},{6,7},{7,5},{5,3},{3,1},{1,0},{8,10},{10,12},{12... | collective-permute-start | bytes 1179656 | tf_op jit(solution)/shard_map/ppermute | solution.py:248
  62.1 1.6 %collective-permute-start.11 = (f32[384,256]{1,0:T(8,128)S(1)}, f32[384,256]{1,0:T(8,128)S(1)}, u32[]{:S(2)}, u32[]{:S(2)}) collective-permute-start(f32[384,256]{1,0:T(8,128)S(1)} %add.41), channel_id=1, source_target_pairs={{0,16},{8,24},{16,0},{24,8},{1,17},{9,25},{17,1},{25,9},{2,18},{10... | collective-permute-start | bytes 1179656 | tf_op jit(solution)/shard_map/ppermute | solution.py:265
  63.6 2.2 %shard_map.79 = (bf16[8,256,384]{2,1,0:T(8,128)(2,1)S(1)}, bf16[8,256,384]{2,1,0:T(8,128)(2,1)S(1)}, bf16[4,384,256]{2,1,0:T(8,128)(2,1)S(1)}, bf16[4,384,256]{2,1,0:T(8,128)(2,1)S(1)}) custom-call(f32[384,256]{1,0:T(8,128)S(1)} %copy-done.1, f32[384,256]{1,0:T(8,128)S(1)} %collective-permute-done.refs_1_, f32[384,256]{1,0:T(8,128)S(1)} %collective-permute-done.1.refs_2_, ...), custom_call_target="tpu_custom_call" | custom-call | flops 2264924160 | bytes 20000000 | tf_op jit(solution)/shard_map/pallas_call | solution.py:339
  65.8 3.6 %collective-permute-done.19 = f32[384,256]{1,0:T(8,128)S(1)} collective-permute-done((f32[384,256]{1,0:T(8,128)S(1)}, f32[384,256]{1,0:T(8,128)S(1)}, u32[]{:S(2)}, u32[]{:S(2)}) %collective-permute-start.19) | collective-permute-done | bytes 393248 | tf_op jit(solution)/shard_map/ppermute | solution.py:249
  71.4 1.6 %collective-permute-start.20 = (f32[384,256]{1,0:T(8,128)S(1)}, f32[384,256]{1,0:T(8,128)S(1)}, u32[]{:S(2)}, u32[]{:S(2)}) collective-permute-start(f32[384,256]{1,0:T(8,128)S(1)} %add_add_fusion.refs_0_), channel_id=1, source_target_pairs={{0,2},{2,4},{4,6},{6,7},{7,5},{5,3},{3,1},{1,0},{8,10},{10,12},{12... | collective-permute-start | bytes 1179656 | tf_op jit(solution)/shard_map/ppermute | solution.py:237
  73.5 1.7 %collective-permute-start.23 = (f32[384,256]{1,0:T(8,128)S(1)}, f32[384,256]{1,0:T(8,128)S(1)}, u32[]{:S(2)}, u32[]{:S(2)}) collective-permute-start(f32[384,256]{1,0:T(8,128)S(1)} %add_add_fusion.refs_0_), channel_id=1, source_target_pairs={{0,16},{8,24},{16,0},{24,8},{1,17},{9,25},{17,1},{25,9},{2,18},{10... | collective-permute-start | bytes 1179656 | tf_op jit(solution)/shard_map/ppermute | solution.py:258
  75.2 5.3 %collective-permute-done.20.refs_1_ = f32[384,256]{1,0:T(8,128)S(1)} collective-permute-done((f32[384,256]{1,0:T(8,128)S(1)}, f32[384,256]{1,0:T(8,128)S(1)}, u32[]{:S(2)}, u32[]{:S(2)}) %collective-permute-start.20) | collective-permute-done | bytes 393248 | tf_op jit(solution)/shard_map/ppermute | solution.py:237
  80.5 1.8 %collective-permute-start.25 = (f32[384,256]{1,0:T(8,128)S(1)}, f32[384,256]{1,0:T(8,128)S(1)}, u32[]{:S(2)}, u32[]{:S(2)}) collective-permute-start(f32[384,256]{1,0:T(8,128)S(1)} %collective-permute-done.20.refs_1_), channel_id=1, source_target_pairs={{0,2},{2,4},{4,6},{6,7},{7,5},{5,3},{3,1},{1,0},{8,10},{10,12},{12... | collective-permute-start | bytes 1179656 | tf_op jit(solution)/shard_map/ppermute | solution.py:237
  83.0 4.2 %shard_map.80.v_ref = f32[15,256,256]{2,1,0:T(8,128)S(1)} custom-call(s32[1,1,15]{2,1,0:T(1,128)} %rows_in.11, s32[1,1,15]{2,1,0:T(1,128)} %cols_in.11, s32[1,1,15]{2,1,0:T(1,128)} %live_in.7, f32[15,256,256]{2,1,0:T(8,128)S(1)} %bitcast.2, bf16[4,384,256]{2,1,0:T(8,128)(2,1)S(1)} %get-tuple-element.50.rh, bf16[4,384,256]{2,1,0:T(8,128)(2,1)S(1)} %get-tuple-element.51.rl, ...), custom_call_target="tpu_custom_call" | custom-call | flops 2264924160 | bytes 20000000 | tf_op jit(solution)/shard_map/pallas_call | solution.py:354
  88.3 1.8 %collective-permute-done.26.refs_1_ = f32[384,256]{1,0:T(8,128)S(1)} collective-permute-done((f32[384,256]{1,0:T(8,128)S(1)}, f32[384,256]{1,0:T(8,128)S(1)}, u32[]{:S(2)}, u32[]{:S(2)}) %collective-permute-start.26) | collective-permute-done | bytes 393248 | tf_op jit(solution)/shard_map/ppermute | solution.py:238
  90.1 1.6 %collective-permute-start.27 = (f32[384,256]{1,0:T(8,128)S(1)}, f32[384,256]{1,0:T(8,128)S(1)}, u32[]{:S(2)}, u32[]{:S(2)}) collective-permute-start(f32[384,256]{1,0:T(8,128)S(1)} %collective-permute-done.25.refs_0_), channel_id=1, source_target_pairs={{0,2},{2,4},{4,6},{6,7},{7,5},{5,3},{3,1},{1,0},{8,10},{10,12},{12... | collective-permute-start | bytes 1179656 | tf_op jit(solution)/shard_map/ppermute | solution.py:237
  92.1 6.4 %shard_map.81 = (f32[1,1,15,256,256]{4,3,2,1,0:T(8,128)}, f32[15,256,256]{2,1,0:T(8,128)S(1)}, f32[256,256]{1,0:T(8,128)}) custom-call(s32[1,1,15]{2,1,0:T(1,128)} %rows_in.11, s32[1,1,15]{2,1,0:T(1,128)} %cols_in.11, s32[1,1,15]{2,1,0:T(1,128)} %live_in.7, f32[256,256]{1,0:T(8,128)} %d_in.3, f32[15,256,256]{2,1,0:T(8,128)S(1)} %shard_map.80.v_ref, ...), custom_call_target="tpu_custom_call" | custom-call | flops 2264924160 | bytes 20000000 | tf_op jit(solution)/shard_map/pallas_call | solution.py:369
  98.5 1.4 %collective-permute-done.28.refs_3_ = f32[384,256]{1,0:T(8,128)S(1)} collective-permute-done((f32[384,256]{1,0:T(8,128)S(1)}, f32[384,256]{1,0:T(8,128)S(1)}, u32[]{:S(2)}, u32[]{:S(2)}) %collective-permute-start.28) | collective-permute-done | bytes 393248 | tf_op jit(solution)/shard_map/ppermute | solution.py:238
  99.9 1.6 %collective-permute-start.29 = (f32[192,256]{1,0:T(8,128)S(1)}, f32[192,256]{1,0:T(8,128)S(1)}, u32[]{:S(2)}, u32[]{:S(2)}) collective-permute-start(f32[192,256]{1,0:T(8,128)S(1)} %slice.6), channel_id=1, source_target_pairs={{0,2},{2,4},{4,6},{6,7},{7,5},{5,3},{3,1},{1,0},{8,10},{10,12},{12... | collective-permute-start | bytes 589832 | tf_op jit(solution)/shard_map/ppermute | solution.py:235
  102.1 5.5 %shard_map.82.refs_2_ = f32[1,1,15,256,256]{4,3,2,1,0:T(8,128)} custom-call(s32[1,1,15]{2,1,0:T(1,128)} %rows_in.11, s32[1,1,15]{2,1,0:T(1,128)} %cols_in.11, s32[1,1,15]{2,1,0:T(1,128)} %live_in.7, f32[15,256,256]{2,1,0:T(8,128)S(1)} %get-tuple-element.55.v_ref, bf16[4,384,256]{2,1,0:T(8,128)(2,1)S(1)} %get-tuple-element.50.rh, ...), custom_call_target="tpu_custom_call", output_to_operand_aliasing={{}: (10, {})} | custom-call | flops 2264924160 | bytes 20000000 | tf_op jit(solution)/shard_map/pallas_call | solution.py:385
  107.6 2.6 %shard_map.83 = f32[1,1,15,256,256]{4,3,2,1,0:T(8,128)} custom-call(s32[1,1,15]{2,1,0:T(1,128)} %rows_in.11, s32[1,1,15]{2,1,0:T(1,128)} %cols_in.11, s32[1,1,15]{2,1,0:T(1,128)} %live_in.7, f32[15,256,256]{2,1,0:T(8,128)S(1)} %get-tuple-element.55.v_ref, bf16[4,384,256]{2,1,0:T(8,128)(2,1)S(1)} %get-tuple-element.50.rh, ...), custom_call_target="tpu_custom_call", output_to_operand_aliasing={{}: (8, {})} | custom-call | flops 2264924160 | bytes 20000000 | tf_op jit(solution)/shard_map/pallas_call | solution.py:385
  (57 shorter events, 13.0 us)
Async XLA Ops:
  0.6 12.3 %collective-permute-start.7 = (f32[384,256]{1,0:T(8,128)}, f32[384,256]{1,0:T(8,128)S(1)}, u32[]{:S(2)}, u32[]{:S(2)}) collective-permute-start(f32[384,256]{1,0:T(8,128)} %refs_8_.1), channel_id=1, source_target_pairs={{0,16},{8,24},{16,0},{24,8},{1,17},{9,25},{17,1},{25,9},{2,18},{10... | collective-permute-start | bytes 1179656 | tf_op jit(solution)/shard_map/ppermute | solution.py:258
  3.6 10.8 %collective-permute-start = (f32[384,256]{1,0:T(8,128)}, f32[384,256]{1,0:T(8,128)S(1)}, u32[]{:S(2)}, u32[]{:S(2)}) collective-permute-start(f32[384,256]{1,0:T(8,128)} %refs_8_.1), channel_id=1, source_target_pairs={{0,2},{2,4},{4,6},{6,7},{7,5},{5,3},{3,1},{1,0},{8,10},{10,12},{12... | collective-permute-start | bytes 1179656 | tf_op jit(solution)/shard_map/ppermute | solution.py:237
  5.2 10.8 %collective-permute-start.3 = (f32[384,256]{1,0:T(8,128)}, f32[384,256]{1,0:T(8,128)S(1)}, u32[]{:S(2)}, u32[]{:S(2)}) collective-permute-start(f32[384,256]{1,0:T(8,128)} %refs_8_.1), channel_id=1, source_target_pairs={{2,0},{4,2},{6,4},{7,6},{5,7},{3,5},{1,3},{0,1},{10,8},{12,10},{14... | collective-permute-start | bytes 1179656 | tf_op jit(solution)/shard_map/ppermute | solution.py:238
  5.7 10.8 %collective-permute-start.6 = (f32[384,256]{1,0:T(8,128)}, f32[384,256]{1,0:T(8,128)S(1)}, u32[]{:S(2)}, u32[]{:S(2)}) collective-permute-start(f32[384,256]{1,0:T(8,128)} %refs_8_.1), channel_id=1, source_target_pairs={{0,8},{8,0},{16,24},{24,16},{1,9},{9,1},{17,25},{25,17},{2,10},{10... | collective-permute-start | bytes 1179656 | tf_op jit(solution)/shard_map/ppermute | solution.py:259
  13.0 3.5 %collective-permute-start.8 = (f32[384,256]{1,0:T(8,128)S(1)}, f32[384,256]{1,0:T(8,128)S(1)}, u32[]{:S(2)}, u32[]{:S(2)}) collective-permute-start(f32[384,256]{1,0:T(8,128)S(1)} %collective-permute-done.7.refs_1_.refs_10_), channel_id=1, source_target_pairs={{0,8},{8,0},{16,24},{24,16},{1,9},{9,1},{17,25},{25,17},{2,10},{10... | collective-permute-start | bytes 1179656 | tf_op jit(solution)/shard_map/ppermute | solution.py:259
  14.4 10.2 %collective-permute-start.1 = (f32[384,256]{1,0:T(8,128)S(1)}, f32[384,256]{1,0:T(8,128)S(1)}, u32[]{:S(2)}, u32[]{:S(2)}) collective-permute-start(f32[384,256]{1,0:T(8,128)S(1)} %collective-permute-done.refs_1_), channel_id=1, source_target_pairs={{0,2},{2,4},{4,6},{6,7},{7,5},{5,3},{3,1},{1,0},{8,10},{10,12},{12... | collective-permute-start | bytes 1179656 | tf_op jit(solution)/shard_map/ppermute | solution.py:237
  16.0 11.7 %collective-permute-start.4 = (f32[384,256]{1,0:T(8,128)S(1)}, f32[384,256]{1,0:T(8,128)}, u32[]{:S(2)}, u32[]{:S(2)}) collective-permute-start(f32[384,256]{1,0:T(8,128)S(1)} %collective-permute-done.3.refs_7_), channel_id=1, source_target_pairs={{2,0},{4,2},{6,4},{7,6},{5,7},{3,5},{1,3},{0,1},{10,8},{12,10},{14... | collective-permute-start | bytes 1179656 | tf_op jit(solution)/shard_map/ppermute | solution.py:238
  23.0 29.7 %copy-start.1 = (f32[384,256]{1,0:T(8,128)S(1)}, f32[384,256]{1,0:T(8,128)}, u32[]{:S(2)}) copy-start(f32[384,256]{1,0:T(8,128)} %refs_8_.1) | copy-start | bytes 1179652
  23.0 11.2 %collective-permute-start.13 = (f32[384,256]{1,0:T(8,128)}, f32[384,256]{1,0:T(8,128)}, u32[]{:S(2)}, u32[]{:S(2)}) collective-permute-start(f32[384,256]{1,0:T(8,128)} %get-tuple-element.42), channel_id=1, source_target_pairs={{0,2},{2,4},{4,6},{6,7},{7,5},{5,3},{3,1},{1,0},{10,8},{12,10},{14... | collective-permute-start | bytes 1179656 | tf_op jit(solution)/shard_map/ppermute | solution.py:244
  24.6 17.3 %collective-permute-start.2 = (f32[384,256]{1,0:T(8,128)S(1)}, f32[384,256]{1,0:T(8,128)S(1)}, u32[]{:S(2)}, u32[]{:S(2)}) collective-permute-start(f32[384,256]{1,0:T(8,128)S(1)} %collective-permute-done.1.refs_2_), channel_id=1, source_target_pairs={{0,2},{2,4},{4,6},{6,7},{7,5},{5,3},{3,1},{1,0},{8,10},{10,12},{12... | collective-permute-start | bytes 1179656 | tf_op jit(solution)/shard_map/ppermute | solution.py:237
  27.7 14.2 %collective-permute-start.5 = (f32[384,256]{1,0:T(8,128)}, f32[384,256]{1,0:T(8,128)S(1)}, u32[]{:S(2)}, u32[]{:S(2)}) collective-permute-start(f32[384,256]{1,0:T(8,128)} %collective-permute-done.4.refs_6_), channel_id=1, source_target_pairs={{2,0},{4,2},{6,4},{7,6},{5,7},{3,5},{1,3},{0,1},{10,8},{12,10},{14... | collective-permute-start | bytes 1179656 | tf_op jit(solution)/shard_map/ppermute | solution.py:238
  35.5 12.9 %collective-permute-start.17 = (f32[384,256]{1,0:T(8,128)S(1)}, f32[384,256]{1,0:T(8,128)S(1)}, u32[]{:S(2)}, u32[]{:S(2)}) collective-permute-start(f32[384,256]{1,0:T(8,128)S(1)} %get-tuple-element.63), channel_id=1, source_target_pairs={{2,0},{4,2},{6,4},{7,6},{5,7},{3,5},{1,3},{0,1},{10,8},{12,10},{14... | collective-permute-start | bytes 1179656 | tf_op jit(solution)/shard_map/ppermute | solution.py:249
  37.2 13.2 %collective-permute-start.14 = (f32[384,256]{1,0:T(8,128)S(1)}, f32[384,256]{1,0:T(8,128)S(1)}, u32[]{:S(2)}, u32[]{:S(2)}) collective-permute-start(f32[384,256]{1,0:T(8,128)S(1)} %get-tuple-element.62), channel_id=1, source_target_pairs={{0,2},{2,4},{4,6},{6,7},{7,5},{5,3},{3,1},{1,0},{8,10},{10,12},{12... | collective-permute-start | bytes 1179656 | tf_op jit(solution)/shard_map/ppermute | solution.py:248
  42.0 10.6 %collective-permute-start.9 = (f32[384,256]{1,0:T(8,128)S(1)}, f32[384,256]{1,0:T(8,128)S(1)}, u32[]{:S(2)}, u32[]{:S(2)}) collective-permute-start(f32[384,256]{1,0:T(8,128)S(1)} %broadcast_select_fusion), channel_id=1, source_target_pairs={{0,2},{2,4},{4,6},{6,7},{7,5},{5,3},{3,1},{1,0},{10,8},{12,10},{14... | collective-permute-start | bytes 1179656 | tf_op jit(solution)/shard_map/ppermute | solution.py:240
  49.4 10.3 %collective-permute-start.18 = (f32[384,256]{1,0:T(8,128)S(1)}, f32[384,256]{1,0:T(8,128)S(1)}, u32[]{:S(2)}, u32[]{:S(2)}) collective-permute-start(f32[384,256]{1,0:T(8,128)S(1)} %add.50), channel_id=1, source_target_pairs={{2,0},{4,2},{6,4},{7,6},{5,7},{3,5},{1,3},{0,1},{10,8},{12,10},{14... | collective-permute-start | bytes 1179656 | tf_op jit(solution)/shard_map/ppermute | solution.py:249
  51.4 8.7 %collective-permute-start.15 = (f32[384,256]{1,0:T(8,128)S(1)}, f32[384,256]{1,0:T(8,128)S(1)}, u32[]{:S(2)}, u32[]{:S(2)}) collective-permute-start(f32[384,256]{1,0:T(8,128)S(1)} %add.46), channel_id=1, source_target_pairs={{0,2},{2,4},{4,6},{6,7},{7,5},{5,3},{3,1},{1,0},{8,10},{10,12},{12... | collective-permute-start | bytes 1179656 | tf_op jit(solution)/shard_map/ppermute | solution.py:248
  57.7 4.3 %collective-permute-start.10 = (f32[384,256]{1,0:T(8,128)S(1)}, f32[384,256]{1,0:T(8,128)S(1)}, u32[]{:S(2)}, u32[]{:S(2)}) collective-permute-start(f32[384,256]{1,0:T(8,128)S(1)} %get-tuple-element.36), channel_id=1, source_target_pairs={{0,8},{8,0},{16,24},{24,16},{1,9},{9,1},{17,25},{25,17},{2,10},{10... | collective-permute-start | bytes 1179656 | tf_op jit(solution)/shard_map/ppermute | solution.py:262
  57.7 8.1 %collective-permute-start.12 = (f32[384,256]{1,0:T(8,128)S(1)}, f32[384,256]{1,0:T(8,128)S(1)}, u32[]{:S(2)}, u32[]{:S(2)}) collective-permute-start(f32[384,256]{1,0:T(8,128)S(1)} %get-tuple-element.38), channel_id=1, source_target_pairs={{0,8},{8,0},{16,24},{24,16},{1,9},{9,1},{17,25},{25,17},{2,10},{10... | collective-permute-start | bytes 1179656 | tf_op jit(solution)/shard_map/ppermute | solution.py:262
  59.8 9.6 %collective-permute-start.19 = (f32[384,256]{1,0:T(8,128)S(1)}, f32[384,256]{1,0:T(8,128)S(1)}, u32[]{:S(2)}, u32[]{:S(2)}) collective-permute-start(f32[384,256]{1,0:T(8,128)S(1)} %add.51), channel_id=1, source_target_pairs={{2,0},{4,2},{6,4},{7,6},{5,7},{3,5},{1,3},{0,1},{10,8},{12,10},{14... | collective-permute-start | bytes 1179656 | tf_op jit(solution)/shard_map/ppermute | solution.py:249
  60.2 10.0 %collective-permute-start.16 = (f32[384,256]{1,0:T(8,128)S(1)}, f32[384,256]{1,0:T(8,128)S(1)}, u32[]{:S(2)}, u32[]{:S(2)}) collective-permute-start(f32[384,256]{1,0:T(8,128)S(1)} %add.47), channel_id=1, source_target_pairs={{0,2},{2,4},{4,6},{6,7},{7,5},{5,3},{3,1},{1,0},{8,10},{10,12},{12... | collective-permute-start | bytes 1179656 | tf_op jit(solution)/shard_map/ppermute | solution.py:248
  62.1 9.2 %collective-permute-start.11 = (f32[384,256]{1,0:T(8,128)S(1)}, f32[384,256]{1,0:T(8,128)S(1)}, u32[]{:S(2)}, u32[]{:S(2)}) collective-permute-start(f32[384,256]{1,0:T(8,128)S(1)} %add.41), channel_id=1, source_target_pairs={{0,16},{8,24},{16,0},{24,8},{1,17},{9,25},{17,1},{25,9},{2,18},{10... | collective-permute-start | bytes 1179656 | tf_op jit(solution)/shard_map/ppermute | solution.py:265
  71.4 9.1 %collective-permute-start.20 = (f32[384,256]{1,0:T(8,128)S(1)}, f32[384,256]{1,0:T(8,128)S(1)}, u32[]{:S(2)}, u32[]{:S(2)}) collective-permute-start(f32[384,256]{1,0:T(8,128)S(1)} %add_add_fusion.refs_0_), channel_id=1, source_target_pairs={{0,2},{2,4},{4,6},{6,7},{7,5},{5,3},{3,1},{1,0},{8,10},{10,12},{12... | collective-permute-start | bytes 1179656 | tf_op jit(solution)/shard_map/ppermute | solution.py:237
  73.0 9.3 %collective-permute-start.21 = (f32[384,256]{1,0:T(8,128)S(1)}, f32[384,256]{1,0:T(8,128)S(1)}, u32[]{:S(2)}, u32[]{:S(2)}) collective-permute-start(f32[384,256]{1,0:T(8,128)S(1)} %add_add_fusion.refs_0_), channel_id=1, source_target_pairs={{2,0},{4,2},{6,4},{7,6},{5,7},{3,5},{1,3},{0,1},{10,8},{12,10},{14... | collective-permute-start | bytes 1179656 | tf_op jit(solution)/shard_map/ppermute | solution.py:238
  73.5 9.1 %collective-permute-start.23 = (f32[384,256]{1,0:T(8,128)S(1)}, f32[384,256]{1,0:T(8,128)S(1)}, u32[]{:S(2)}, u32[]{:S(2)}) collective-permute-start(f32[384,256]{1,0:T(8,128)S(1)} %add_add_fusion.refs_0_), channel_id=1, source_target_pairs={{0,16},{8,24},{16,0},{24,8},{1,17},{9,25},{17,1},{25,9},{2,18},{10... | collective-permute-start | bytes 1179656 | tf_op jit(solution)/shard_map/ppermute | solution.py:258
  80.5 7.8 %collective-permute-start.25 = (f32[384,256]{1,0:T(8,128)S(1)}, f32[384,256]{1,0:T(8,128)S(1)}, u32[]{:S(2)}, u32[]{:S(2)}) collective-permute-start(f32[384,256]{1,0:T(8,128)S(1)} %collective-permute-done.20.refs_1_), channel_id=1, source_target_pairs={{0,2},{2,4},{4,6},{6,7},{7,5},{5,3},{3,1},{1,0},{8,10},{10,12},{12... | collective-permute-start | bytes 1179656 | tf_op jit(solution)/shard_map/ppermute | solution.py:237
  82.3 7.8 %collective-permute-start.26 = (f32[384,256]{1,0:T(8,128)S(1)}, f32[384,256]{1,0:T(8,128)S(1)}, u32[]{:S(2)}, u32[]{:S(2)}) collective-permute-start(f32[384,256]{1,0:T(8,128)S(1)} %collective-permute-done.21.refs_2_), channel_id=1, source_target_pairs={{2,0},{4,2},{6,4},{7,6},{5,7},{3,5},{1,3},{0,1},{10,8},{12,10},{14... | collective-permute-start | bytes 1179656 | tf_op jit(solution)/shard_map/ppermute | solution.py:238
  82.5 9.6 %collective-permute-start.22 = (f32[384,256]{1,0:T(8,128)S(1)}, f32[384,256]{1,0:T(8,128)S(1)}, u32[]{:S(2)}, u32[]{:S(2)}) collective-permute-start(f32[384,256]{1,0:T(8,128)S(1)} %add_add_fusion.refs_0_), channel_id=1, source_target_pairs={{0,8},{8,0},{16,24},{24,16},{1,9},{9,1},{17,25},{25,17},{2,10},{10... | collective-permute-start | bytes 1179656 | tf_op jit(solution)/shard_map/ppermute | solution.py:259
  82.5 9.6 %collective-permute-start.24 = (f32[384,256]{1,0:T(8,128)S(1)}, f32[384,256]{1,0:T(8,128)S(1)}, u32[]{:S(2)}, u32[]{:S(2)}) collective-permute-start(f32[384,256]{1,0:T(8,128)S(1)} %collective-permute-done.23.refs_2_), channel_id=1, source_target_pairs={{0,8},{8,0},{16,24},{24,16},{1,9},{9,1},{17,25},{25,17},{2,10},{10... | collective-permute-start | bytes 1179656 | tf_op jit(solution)/shard_map/ppermute | solution.py:259
  90.1 8.4 %collective-permute-start.27 = (f32[384,256]{1,0:T(8,128)S(1)}, f32[384,256]{1,0:T(8,128)S(1)}, u32[]{:S(2)}, u32[]{:S(2)}) collective-permute-start(f32[384,256]{1,0:T(8,128)S(1)} %collective-permute-done.25.refs_0_), channel_id=1, source_target_pairs={{0,2},{2,4},{4,6},{6,7},{7,5},{5,3},{3,1},{1,0},{8,10},{10,12},{12... | collective-permute-start | bytes 1179656 | tf_op jit(solution)/shard_map/ppermute | solution.py:237
  91.7 8.2 %collective-permute-start.28 = (f32[384,256]{1,0:T(8,128)S(1)}, f32[384,256]{1,0:T(8,128)S(1)}, u32[]{:S(2)}, u32[]{:S(2)}) collective-permute-start(f32[384,256]{1,0:T(8,128)S(1)} %collective-permute-done.26.refs_1_), channel_id=1, source_target_pairs={{2,0},{4,2},{6,4},{7,6},{5,7},{3,5},{1,3},{0,1},{10,8},{12,10},{14... | collective-permute-start | bytes 1179656 | tf_op jit(solution)/shard_map/ppermute | solution.py:238
  99.9 7.7 %collective-permute-start.29 = (f32[192,256]{1,0:T(8,128)S(1)}, f32[192,256]{1,0:T(8,128)S(1)}, u32[]{:S(2)}, u32[]{:S(2)}) collective-permute-start(f32[192,256]{1,0:T(8,128)S(1)} %slice.6), channel_id=1, source_target_pairs={{0,2},{2,4},{4,6},{6,7},{7,5},{5,3},{3,1},{1,0},{8,10},{10,12},{12... | collective-permute-start | bytes 589832 | tf_op jit(solution)/shard_map/ppermute | solution.py:235
  101.6 6.1 %collective-permute-start.30 = (f32[192,256]{1,0:T(8,128)S(1)}, f32[192,256]{1,0:T(8,128)S(1)}, u32[]{:S(2)}, u32[]{:S(2)}) collective-permute-start(f32[192,256]{1,0:T(8,128)S(1)} %slice.7), channel_id=1, source_target_pairs={{2,0},{4,2},{6,4},{7,6},{5,7},{3,5},{1,3},{0,1},{10,8},{12,10},{14... | collective-permute-start | bytes 589832 | tf_op jit(solution)/shard_map/ppermute | solution.py:235
  (4 other events, 48.7 us)
